TPU v7x, 32 devices: a whole 2x2x4 slice. The times are simulated.
32 devices in a mesh: rep: 4 (over x, core), fsdp: 2 (over y), tensor: 4 (over z).
Axes of the slice: x: 2, y: 2, z: 4, core: 2. Of those that a mesh axis runs over, the one named last changes fastest.
Arguments:
- block_input: bfloat16 [5120, 2048], P(('rep', 'fsdp', 'tensor')), may hold values from -6 to 6
- cotangent: bfloat16 [5120, 2048], P(('rep', 'fsdp', 'tensor')), may hold values from -6 to 6
- piece_starts: int32 [8, 2], P(('rep', 'fsdp')), may hold values from 0 to 384, as said below
- expert_ids: int32 [5120, 4], P(('rep', 'fsdp')), may hold values from 0 to 7, all different within a row; in each aligned block of 640 rows (0 to 639, 640 to 1279, ...) at most 400 rows name the same one
- norm_gains: bfloat16 [2, 2048], P(None, 'fsdp'), may hold values from 0.5 to 1.5
- qkv_weight: bfloat16 [3, 2048, 2048], P(None, 'fsdp', 'tensor'), may hold values from -0.125 to 0.125
- qkv_bias: bfloat16 [3, 16, 128], P(None, 'tensor', 'fsdp'), may hold values from -3 to 3
- out_weight: bfloat16 [2048, 2048], P('tensor', 'fsdp'), may hold values from -0.5 to 0.5
- router_weight: bfloat16 [2048, 8], P('fsdp'), may hold values from -0.0625 to 0.0625
- shared_gate: bfloat16 [2048], P('fsdp'), may hold values from -0.125 to 0.125
- expert_gate_up: bfloat16 [8, 2048, 2, 1408], P(None, 'fsdp', None, 'tensor'), may hold values from -0.125 to 0.125
- expert_down: bfloat16 [8, 1408, 2048], P(None, 'tensor', 'fsdp'), may hold values from -0.625 to 0.625
- shared_gate_up: bfloat16 [2048, 2, 5632], P('fsdp', None, 'tensor'), may hold values from -0.125 to 0.125
- shared_down: bfloat16 [5632, 2048], P('tensor', 'fsdp'), may hold values from -0.15625 to 0.15625
Outputs:
- output: bfloat16 [5120, 2048], P(('rep', 'fsdp', 'tensor'))
- input_grad: float32 [5120, 2048], P(('rep', 'fsdp', 'tensor'))
- norm_gains_grad: float32 [2, 2048], P(None, 'fsdp')
- qkv_weight_grad: float32 [3, 2048, 2048], P(None, 'fsdp', 'tensor')
- qkv_bias_grad: float32 [3, 16, 128], P(None, 'tensor', 'fsdp')
- out_weight_grad: float32 [2048, 2048], P('tensor', 'fsdp')
- router_weight_grad: float32 [2048, 8], P('fsdp')
- shared_gate_grad: float32 [2048], P('fsdp')
- expert_gate_up_grad: float32 [8, 2048, 2, 1408], P(None, 'fsdp', None, 'tensor')
- expert_down_grad: float32 [8, 1408, 2048], P(None, 'tensor', 'fsdp')
- shared_gate_up_grad: float32 [2048, 2, 5632], P('fsdp', None, 'tensor')
- shared_down_grad: float32 [5632, 2048], P('tensor', 'fsdp')
Inputs may be any that keep to these rules, and one draw needn't show every extreme that they name: `expert_ids`: in each sequence's rows (aligned blocks of 640 rows) no expert is named by more than 400 rows, a bound that some block reaches. `piece_starts`: each row holds 2 rising starts, each at least 256 after the one before.
All inputs are finite; a program needn't handle non-finite values.
Results may differ from a plain program's by a relative error of at most 0.025.
Values may be sent and summed in bfloat16 or wider, within the bound.
A program may use at most 384 MiB of HBM per device.

v0:
```python
import jax
import jax.numpy as jnp
from jax import lax
from jax.sharding import PartitionSpec as P

D = 2048
HEAD_DIM = 128
TOP = 4
EXPERTS = 8
LENGTH = 640
PIECE = 256
CAP = 400


HIGHEST = lax.Precision.HIGHEST
EPSILON = 1e-06


def rope_angles(length, head_dim):
    half_dim = head_dim // 2
    frequency = 1000000.0 ** (-jnp.arange(half_dim, dtype=jnp.float32) * (2.0 / head_dim))
    angles = jnp.arange(length, dtype=jnp.float32)[:, None] * frequency[None, :]
    return (jnp.cos(angles), jnp.sin(angles))


def rotate(head_rows, cos_table, sin_table):
    half_dim = head_rows.shape[-1] // 2
    leading = head_rows[..., :half_dim]
    trailing = head_rows[..., half_dim:]
    cos_rows = cos_table[:, None, :]
    sin_rows = sin_table[:, None, :]
    return jnp.concatenate(
        [leading * cos_rows - trailing * sin_rows, trailing * cos_rows + leading * sin_rows],
        axis=-1,
    )


def rotate_back(grad_rows, cos_table, sin_table):
    half_dim = grad_rows.shape[-1] // 2
    leading = grad_rows[..., :half_dim]
    trailing = grad_rows[..., half_dim:]
    cos_rows = cos_table[:, None, :]
    sin_rows = sin_table[:, None, :]
    return jnp.concatenate(
        [leading * cos_rows + trailing * sin_rows, trailing * cos_rows - leading * sin_rows],
        axis=-1,
    )


def visible_mask(starts_row, length, piece_len):
    position = jnp.arange(length, dtype=jnp.int32)
    inside = (position[None, :] >= starts_row[:, None]) & (
        position[None, :] < starts_row[:, None] + piece_len
    )
    label_ids = jnp.arange(1, starts_row.shape[0] + 1, dtype=jnp.int32)[:, None]
    labels = jnp.sum(jnp.where(inside, label_ids, 0), axis=0)
    causal = position[None, :] <= position[:, None]
    same_piece = (labels[:, None] == labels[None, :]) & (labels[:, None] > 0)
    return causal | same_piece


def slot_entries(routes, experts, capacity):
    flat_ids = routes.reshape(-1)
    onehot = (flat_ids[:, None] == jnp.arange(experts, dtype=jnp.int32)[None, :]).astype(jnp.int32)
    before = jnp.cumsum(onehot, axis=0) - onehot
    place_in = jnp.sum(before * onehot, axis=1)
    target = flat_ids * capacity + place_in
    entries = jnp.full((experts * capacity,), -1, jnp.int32)
    entries = entries.at[target].set(jnp.arange(flat_ids.shape[0], dtype=jnp.int32))
    return (target.reshape(routes.shape), entries)


def swiglu_back(act_grad, gate_pre, up_pre):
    sig_gate = jax.nn.sigmoid(gate_pre)
    gate_grad = act_grad * up_pre * sig_gate * (1.0 + gate_pre * (1.0 - sig_gate))
    up_grad = act_grad * gate_pre * sig_gate
    return jnp.concatenate([gate_grad, up_grad], axis=-1).astype(jnp.bfloat16)


def owner_order(grad, axis_dim, owners, replicas):
    shape = grad.shape
    piece_len = shape[axis_dim] // (owners * replicas)
    split = grad.reshape(shape[:axis_dim] + (owners, replicas, piece_len) + shape[axis_dim + 1 :])
    return jnp.swapaxes(split, axis_dim, axis_dim + 1).reshape(shape)


def shards(
    block_input,
    cotangent,
    piece_starts,
    expert_ids,
    norm_gains,
    qkv_weight,
    qkv_bias,
    out_weight,
    router_weight,
    shared_gate,
    expert_gate_up,
    expert_down,
    shared_gate_up,
    shared_down,
):

    def fetch_dense():
        return (
            lax.all_gather(norm_gains, "fsdp", axis=1, tiled=True),
            lax.all_gather(qkv_weight, "fsdp", axis=1, tiled=True),
            lax.all_gather(qkv_bias, "fsdp", axis=2, tiled=True),
            lax.all_gather(out_weight, "fsdp", axis=1, tiled=True),
            lax.all_gather(router_weight, "fsdp", axis=0, tiled=True),
            lax.all_gather(shared_gate, "fsdp", axis=0, tiled=True),
        )

    def fetch_experts():
        return (
            lax.all_gather(expert_gate_up, "fsdp", axis=1, tiled=True),
            lax.all_gather(expert_down, "fsdp", axis=2, tiled=True),
            lax.all_gather(shared_gate_up, "fsdp", axis=0, tiled=True),
            lax.all_gather(shared_down, "fsdp", axis=1, tiled=True),
        )

    gains_all, qkv_all, bias_all, out_all, router_all, gate_all = fetch_dense()
    gate_up_all, down_all, shared_up_all, shared_down_all = fetch_experts()
    local_width = qkv_all.shape[2]
    local_heads = local_width // HEAD_DIM
    ffe_local = gate_up_all.shape[3]
    fs_local = shared_up_all.shape[2]
    cos_table, sin_table = rope_angles(LENGTH, HEAD_DIM)
    scale = HEAD_DIM ** (-0.5)
    inputs_f = block_input.astype(jnp.float32)
    inverse_one = lax.rsqrt(jnp.mean(inputs_f * inputs_f, axis=-1, keepdims=True) + EPSILON)
    normed_local = (inputs_f * inverse_one * gains_all[0]).astype(jnp.bfloat16)
    normed = lax.all_gather(normed_local, "tensor", axis=0, tiled=True)
    project = jnp.einsum("ld,cde->cle", normed, qkv_all, preferred_element_type=jnp.float32)
    project = project + bias_all.reshape(3, 1, local_width)
    query_rows = rotate(
        project[0].reshape(LENGTH, local_heads, HEAD_DIM), cos_table, sin_table
    ).astype(jnp.bfloat16)
    key_rows = rotate(
        project[1].reshape(LENGTH, local_heads, HEAD_DIM), cos_table, sin_table
    ).astype(jnp.bfloat16)
    value_rows = project[2].reshape(LENGTH, local_heads, HEAD_DIM).astype(jnp.bfloat16)
    visible = visible_mask(piece_starts[0], LENGTH, PIECE)

    def attend_scores():
        raw_scores = (
            jnp.einsum("qhd,khd->hqk", query_rows, key_rows, preferred_element_type=jnp.float32)
            * scale
        )
        return jnp.where(visible[None], raw_scores, -1e30)

    scores = attend_scores()
    top_score = jnp.max(scores, axis=-1, keepdims=True)
    weights_exp = jnp.exp(scores - top_score)
    row_total = jnp.sum(weights_exp, axis=-1, keepdims=True)
    probs = weights_exp / row_total
    log_total = top_score + jnp.log(row_total)
    attended = (
        jnp.einsum(
            "hqk,khd->qhd",
            probs.astype(jnp.bfloat16),
            value_rows,
            preferred_element_type=jnp.float32,
        )
        .reshape(LENGTH, local_width)
        .astype(jnp.bfloat16)
    )
    heads_part = jnp.dot(attended, out_all, preferred_element_type=jnp.float32)
    branch_local = lax.psum_scatter(
        heads_part.astype(jnp.bfloat16), "tensor", scatter_dimension=0, tiled=True
    ).astype(jnp.float32)
    hidden = inputs_f + branch_local
    inverse_two = lax.rsqrt(jnp.mean(hidden * hidden, axis=-1, keepdims=True) + EPSILON)
    normed_two_local = (hidden * inverse_two * gains_all[1]).astype(jnp.bfloat16)
    normed_two, grad_rows = (
        lax.all_gather(normed_two_local, "tensor", axis=0, tiled=True),
        lax.all_gather(cotangent, "tensor", axis=0, tiled=True),
    )
    logits = jnp.dot(normed_two, router_all, preferred_element_type=jnp.float32)
    router_probs = jax.nn.softmax(logits, axis=-1)
    gate_sel = jnp.take_along_axis(router_probs, expert_ids, axis=1)
    target, entries = slot_entries(expert_ids, EXPERTS, CAP)
    live = entries >= 0
    safe_entry = jnp.maximum(entries, 0)
    token_of = safe_entry // TOP
    slot_rows = jnp.where(live[:, None], normed_two[token_of], jnp.zeros((), jnp.bfloat16)).reshape(
        EXPERTS, CAP, D
    )
    gate_up_flat = gate_up_all.reshape(EXPERTS, D, 2 * ffe_local)
    expert_pre = jnp.einsum(
        "ecd,edf->ecf", slot_rows, gate_up_flat, preferred_element_type=jnp.float32
    )
    gate_pre = expert_pre[..., :ffe_local]
    up_pre = expert_pre[..., ffe_local:]
    expert_act = (jax.nn.silu(gate_pre) * up_pre).astype(jnp.bfloat16)
    expert_out = jnp.einsum(
        "ecf,efd->ecd", expert_act, down_all, preferred_element_type=jnp.float32
    ).reshape(EXPERTS * CAP, D)
    picked = expert_out[target]
    routed = jnp.sum(gate_sel[:, :, None] * picked, axis=1)
    shared_up_flat = shared_up_all.reshape(D, 2 * fs_local)
    shared_pre = jnp.dot(normed_two, shared_up_flat, preferred_element_type=jnp.float32)
    shared_act = (jax.nn.silu(shared_pre[:, :fs_local]) * shared_pre[:, fs_local:]).astype(
        jnp.bfloat16
    )
    shared_out = jnp.dot(shared_act, shared_down_all, preferred_element_type=jnp.float32)
    shared_scale = jax.nn.sigmoid(jnp.dot(normed_two, gate_all, preferred_element_type=jnp.float32))
    mixer_part = routed + shared_scale[:, None] * shared_out
    mixer_local = lax.psum_scatter(
        mixer_part.astype(jnp.bfloat16), "tensor", scatter_dimension=0, tiled=True
    ).astype(jnp.float32)
    result = (hidden + mixer_local).astype(jnp.bfloat16)
    gains_all, qkv_all, bias_all, out_all, router_all, gate_all = fetch_dense()
    gate_up_all, down_all, shared_up_all, shared_down_all = fetch_experts()
    gate_up_flat = gate_up_all.reshape(EXPERTS, D, 2 * ffe_local)
    shared_up_flat = shared_up_all.reshape(D, 2 * fs_local)
    slot_scale = jnp.where(live, gate_sel.reshape(-1)[safe_entry], 0.0)
    slot_grad = (
        (slot_scale[:, None] * grad_rows[token_of]).astype(jnp.bfloat16).reshape(EXPERTS, CAP, D)
    )
    gate_grad = jnp.sum(picked * grad_rows[:, None, :], axis=-1)
    act_grad = jnp.einsum("ecd,efd->ecf", slot_grad, down_all, preferred_element_type=jnp.float32)
    down_grad = jnp.einsum(
        "ecf,ecd->efd", expert_act, slot_grad, preferred_element_type=jnp.float32
    )
    pre_grad = swiglu_back(act_grad, gate_pre, up_pre)
    gate_up_grad = jnp.einsum(
        "ecd,ecf->edf", slot_rows, pre_grad, preferred_element_type=jnp.float32
    )
    row_grad = jnp.einsum(
        "ecf,edf->ecd", pre_grad, gate_up_flat, preferred_element_type=jnp.float32
    ).reshape(EXPERTS * CAP, D)
    normed_grad = jnp.sum(row_grad[target], axis=1)
    chosen_grid = expert_ids[:, :, None] == jnp.arange(EXPERTS, dtype=jnp.int32)[None, None, :]
    prob_grad = jnp.sum(jnp.where(chosen_grid, gate_grad[:, :, None], 0.0), axis=1)
    logit_grad = router_probs * (
        prob_grad - jnp.sum(router_probs * prob_grad, axis=-1, keepdims=True)
    )
    router_grad = jnp.einsum(
        "ld,le->de", normed_two, logit_grad, precision=HIGHEST, preferred_element_type=jnp.float32
    )
    normed_grad = normed_grad + jnp.einsum(
        "le,de->ld", logit_grad, router_all, precision=HIGHEST, preferred_element_type=jnp.float32
    )
    scale_grad = jnp.sum(shared_out * grad_rows, axis=-1)
    scale_logit_grad = scale_grad * shared_scale * (1.0 - shared_scale)
    gate_vec_grad = jnp.einsum(
        "ld,l->d",
        normed_two,
        scale_logit_grad,
        precision=HIGHEST,
        preferred_element_type=jnp.float32,
    )
    normed_grad = normed_grad + scale_logit_grad[:, None] * gate_all
    shared_out_grad = (shared_scale[:, None] * grad_rows).astype(jnp.bfloat16)
    shared_act_grad = jnp.einsum(
        "ld,fd->lf", shared_out_grad, shared_down_all, preferred_element_type=jnp.float32
    )
    shared_down_grad = jnp.einsum(
        "lf,ld->fd", shared_act, shared_out_grad, preferred_element_type=jnp.float32
    )
    shared_pre_grad = swiglu_back(
        shared_act_grad, shared_pre[:, :fs_local], shared_pre[:, fs_local:]
    )
    shared_up_grad = jnp.einsum(
        "ld,lf->df", normed_two, shared_pre_grad, preferred_element_type=jnp.float32
    )
    normed_grad = normed_grad + jnp.einsum(
        "lf,df->ld", shared_pre_grad, shared_up_flat, preferred_element_type=jnp.float32
    )
    normed_two_grad = lax.psum_scatter(
        normed_grad.astype(jnp.bfloat16), "tensor", scatter_dimension=0, tiled=True
    ).astype(jnp.float32)
    cot_local = cotangent.astype(jnp.float32)
    scaled_two = normed_two_grad * gains_all[1]
    hidden_grad = cot_local + inverse_two * (
        scaled_two
        - hidden * inverse_two * inverse_two * jnp.mean(scaled_two * hidden, axis=-1, keepdims=True)
    )
    gain_two_grad = jnp.sum(normed_two_grad * hidden * inverse_two, axis=0)
    branch_grad = lax.all_gather(hidden_grad.astype(jnp.bfloat16), "tensor", axis=0, tiled=True)
    out_grad = jnp.einsum("lf,ld->fd", attended, branch_grad, preferred_element_type=jnp.float32)
    attended_grad = jnp.einsum(
        "ld,fd->lf", branch_grad, out_all, preferred_element_type=jnp.float32
    )
    attended_grad = attended_grad.astype(jnp.bfloat16).reshape(LENGTH, local_heads, HEAD_DIM)
    probs = jnp.exp(attend_scores() - log_total)
    value_grad = jnp.einsum(
        "hqk,qhd->khd",
        probs.astype(jnp.bfloat16),
        attended_grad,
        preferred_element_type=jnp.float32,
    )
    pgrad_rows = jnp.einsum(
        "qhd,khd->hqk", attended_grad, value_rows, preferred_element_type=jnp.float32
    )
    score_grad = (
        probs * (pgrad_rows - jnp.sum(probs * pgrad_rows, axis=-1, keepdims=True))
    ).astype(jnp.bfloat16)
    query_grad = (
        jnp.einsum("hqk,khd->qhd", score_grad, key_rows, preferred_element_type=jnp.float32) * scale
    )
    key_grad = (
        jnp.einsum("hqk,qhd->khd", score_grad, query_rows, preferred_element_type=jnp.float32)
        * scale
    )
    project_grad = jnp.stack(
        [
            rotate_back(query_grad, cos_table, sin_table).reshape(LENGTH, local_width),
            rotate_back(key_grad, cos_table, sin_table).reshape(LENGTH, local_width),
            value_grad.reshape(LENGTH, local_width),
        ]
    ).astype(jnp.bfloat16)
    bias_grad = jnp.sum(project_grad, axis=1, dtype=jnp.float32).reshape(3, local_heads, HEAD_DIM)
    qkv_grad = jnp.einsum("ld,cle->cde", normed, project_grad, preferred_element_type=jnp.float32)
    normed_one_grad = jnp.einsum(
        "cle,cde->ld", project_grad, qkv_all, preferred_element_type=jnp.float32
    )
    input_row_grad = lax.psum_scatter(
        normed_one_grad.astype(jnp.bfloat16), "tensor", scatter_dimension=0, tiled=True
    ).astype(jnp.float32)
    scaled_one = input_row_grad * gains_all[0]
    input_grad = hidden_grad + inverse_one * (
        scaled_one
        - inputs_f
        * inverse_one
        * inverse_one
        * jnp.mean(scaled_one * inputs_f, axis=-1, keepdims=True)
    )
    gain_one_grad = jnp.sum(input_row_grad * inputs_f * inverse_one, axis=0)
    gains_sum, router_sum, gate_vec_sum = lax.psum(
        (jnp.stack([gain_one_grad, gain_two_grad]), router_grad, gate_vec_grad),
        ("rep", "fsdp", "tensor"),
    )
    owners = lax.axis_size("fsdp")
    replicas = lax.axis_size("rep")
    shard_len = D // owners
    shard_start = lax.axis_index("fsdp") * shard_len
    gains_out = lax.dynamic_slice_in_dim(gains_sum, shard_start, shard_len, 1)
    router_out = lax.dynamic_slice_in_dim(router_sum, shard_start, shard_len, 0)
    gate_vec_out = lax.dynamic_slice_in_dim(gate_vec_sum, shard_start, shard_len, 0)
    large_grads = (
        qkv_grad,
        bias_grad,
        out_grad,
        gate_up_grad.reshape(EXPERTS, D, 2, ffe_local),
        down_grad,
        shared_up_grad.reshape(D, 2, fs_local),
        shared_down_grad,
    )
    reordered = (
        owner_order(large_grads[0], 1, owners, replicas),
        owner_order(large_grads[1], 2, owners, replicas),
        owner_order(large_grads[2], 1, owners, replicas),
        owner_order(large_grads[3], 1, owners, replicas),
        owner_order(large_grads[4], 2, owners, replicas),
        owner_order(large_grads[5], 0, owners, replicas),
        owner_order(large_grads[6], 1, owners, replicas),
    )
    pieces = (
        lax.psum_scatter(
            reordered[0].astype(jnp.bfloat16), ("rep", "fsdp"), scatter_dimension=1, tiled=True
        ).astype(jnp.float32),
        lax.psum_scatter(
            reordered[1].astype(jnp.bfloat16), ("rep", "fsdp"), scatter_dimension=2, tiled=True
        ).astype(jnp.float32),
        lax.psum_scatter(
            reordered[2].astype(jnp.bfloat16), ("rep", "fsdp"), scatter_dimension=1, tiled=True
        ).astype(jnp.float32),
        lax.psum_scatter(
            reordered[3].astype(jnp.bfloat16), ("rep", "fsdp"), scatter_dimension=1, tiled=True
        ).astype(jnp.float32),
        lax.psum_scatter(
            reordered[4].astype(jnp.bfloat16), ("rep", "fsdp"), scatter_dimension=2, tiled=True
        ).astype(jnp.float32),
        lax.psum_scatter(
            reordered[5].astype(jnp.bfloat16), ("rep", "fsdp"), scatter_dimension=0, tiled=True
        ).astype(jnp.float32),
        lax.psum_scatter(
            reordered[6].astype(jnp.bfloat16), ("rep", "fsdp"), scatter_dimension=1, tiled=True
        ).astype(jnp.float32),
    )
    finals = (
        lax.all_gather(pieces[0].astype(jnp.bfloat16), "rep", axis=1, tiled=True).astype(
            jnp.float32
        ),
        lax.all_gather(pieces[1].astype(jnp.bfloat16), "rep", axis=2, tiled=True).astype(
            jnp.float32
        ),
        lax.all_gather(pieces[2].astype(jnp.bfloat16), "rep", axis=1, tiled=True).astype(
            jnp.float32
        ),
        lax.all_gather(pieces[3].astype(jnp.bfloat16), "rep", axis=1, tiled=True).astype(
            jnp.float32
        ),
        lax.all_gather(pieces[4].astype(jnp.bfloat16), "rep", axis=2, tiled=True).astype(
            jnp.float32
        ),
        lax.all_gather(pieces[5].astype(jnp.bfloat16), "rep", axis=0, tiled=True).astype(
            jnp.float32
        ),
        lax.all_gather(pieces[6].astype(jnp.bfloat16), "rep", axis=1, tiled=True).astype(
            jnp.float32
        ),
    )
    return (
        result,
        input_grad,
        gains_out,
        finals[0],
        finals[1],
        finals[2],
        router_out,
        gate_vec_out,
        finals[3],
        finals[4],
        finals[5],
        finals[6],
    )


def solution(mesh):
    in_specs = (
        P(("rep", "fsdp", "tensor"), None),
        P(("rep", "fsdp", "tensor"), None),
        P(("rep", "fsdp"), None),
        P(("rep", "fsdp"), None),
        P(None, "fsdp"),
        P(None, "fsdp", "tensor"),
        P(None, "tensor", "fsdp"),
        P("tensor", "fsdp"),
        P("fsdp", None),
        P("fsdp"),
        P(None, "fsdp", None, "tensor"),
        P(None, "tensor", "fsdp"),
        P("fsdp", None, "tensor"),
        P("tensor", "fsdp"),
    )
    out_specs = (
        P(("rep", "fsdp", "tensor"), None),
        P(("rep", "fsdp", "tensor"), None),
        P(None, "fsdp"),
        P(None, "fsdp", "tensor"),
        P(None, "tensor", "fsdp"),
        P("tensor", "fsdp"),
        P("fsdp", None),
        P("fsdp"),
        P(None, "fsdp", None, "tensor"),
        P(None, "tensor", "fsdp"),
        P("fsdp", None, "tensor"),
        P("tensor", "fsdp"),
    )
    return jax.shard_map(shards, mesh=mesh, in_specs=in_specs, out_specs=out_specs, check_vma=False)
```

profile of v0, /device:TPU:0, one launch (start us, length us, event | category | flops | bytes accessed | tf_op | source)
XLA Modules:
  0.0 2443.3 jit_solution(7979649340278530106)
XLA Ops:
  30.0 43.4 %all-gather.17.cloned.1.call-done = bf16[640,2048]{1,0:T(8,128)(2,1)} async-done(((bf16[160,2048]{1,0:T(8,128)(2,1)}), bf16[640,2048]{1,0:T(8,128)(2,1)}) %all-gather.17.cloned.1.call-update) | async-done | bytes 2621456 | tf_op jit(solution)/shard_map/all_gather | solution.py:133
  73.4 81.3 %all-gather.19.cloned.1.call-done = bf16[3,2048,512]{1,2,0:T(8,128)(2,1)} async-done(((bf16[3,1024,512]{1,2,0:T(8,128)(2,1)}), bf16[3,2048,512]{1,2,0:T(8,128)(2,1)}) %all-gather.19.cloned.1.call-update) | async-done | bytes 6291472 | tf_op jit(solution)/shard_map/all_gather | solution.py:107
  195.3 51.0 %reduce-scatter.13.cloned.1.call-done = bf16[160,2048]{1,0:T(8,128)(2,1)} async-done(((bf16[640,2048]{1,0:T(8,128)(2,1)}), bf16[160,2048]{1,0:T(8,128)(2,1)}) %reduce-scatter.13.cloned.1.call-update) | async-done | bytes 655376 | tf_op jit(solution)/shard_map/reduce_scatter | solution.py:169
  278.3 24.0 all-gather.33.cloned.1.call-done
  307.3 13.4 gather_fusion.3
  320.7 122.9 %all-gather.29.cloned.1.call-done = bf16[2048,2,1408]{2,1,0:T(2,128)(2,1)} async-done(((bf16[1024,2,1408]{2,1,0:T(2,128)(2,1)}), bf16[2048,2,1408]{2,1,0:T(2,128)(2,1)}) %all-gather.29.cloned.1.call-update) | async-done | bytes 11534352 | tf_op jit(solution)/shard_map/all_gather | solution.py:118
  454.8 45.7 %all-gather.23.cloned.1.call-done = bf16[640,2048]{1,0:T(8,128)(2,1)} async-done(((bf16[160,2048]{1,0:T(8,128)(2,1)}), bf16[640,2048]{1,0:T(8,128)(2,1)}) %all-gather.23.cloned.1.call-update) | async-done | bytes 2621456 | tf_op jit(solution)/shard_map/all_gather | solution.py:176
  503.7 15.3 gather_fusion.5
  520.6 16.9 gather_fusion.2
  537.8 13.4 gather_fusion
  552.7 13.4 fusion.81
  575.4 12.4 multiply_convert_fusion.6
  590.4 13.7 fusion.21
  604.0 243.3 %all-gather.25.cloned.1.call-done = bf16[8,2048,2,352]{1,3,2,0:T(8,128)(2,1)} async-done(((bf16[8,1024,2,352]{1,3,2,0:T(8,128)(2,1)}), bf16[8,2048,2,352]{1,3,2,0:T(8,128)(2,1)}) %all-gather.25.cloned.1.call-update) | async-done | bytes 23068688 | tf_op jit(solution)/shard_map/all_gather | solution.py:116
  847.3 26.7 %fusion.1 = f32[8,400,704]{2,1,0:T(8,128)} fusion(bf16[8,2048,704]{1,2,0:T(8,128)(2,1)} %bitcast.178, bf16[8,400,2048]{2,1,0:T(8,128)(2,1)} %bitcast.145, pred[8,400]{1,0:T(8,128)(4,1)S(1)} %broadcast_in_dim.76), kind=kOutput, calls=%fused_computation.13 | convolution fusion | flops 9234022400 | bytes 45190272 | tf_op jit(solution)/shard_map/ecd,edf->ecf/dot_general | solution.py:190
  874.0 115.8 %all-gather.27.cloned.1.call-done = bf16[8,352,2048]{2,1,0:T(8,128)(2,1)} async-done(((bf16[8,352,1024]{2,1,0:T(8,128)(2,1)}), bf16[8,352,2048]{2,1,0:T(8,128)(2,1)}) %all-gather.27.cloned.1.call-update) | async-done | bytes 11534352 | tf_op jit(solution)/shard_map/all_gather | solution.py:117
  989.8 20.0 multiply_convert_fusion.3
  1009.9 23.4 fusion.17
  1033.3 28.1 %gather_fusion.4 = f32[2560,2048]{1,0:T(8,128)} fusion(f32[3200,2048]{1,0:T(8,128)} %bitcast.135, s32[3072]{0:T(1024)S(1)} %copy-done.12), kind=kCustom, calls=%fused_computation.4 | custom fusion | bytes 41953280 | tf_op jit(solution)/shard_map/gather | solution.py:233
  1061.4 23.6 reshape.365
  1085.0 16.8 fusion.80
  1101.8 28.1 %gather_fusion.1 = f32[2560,2048]{1,0:T(8,128)} fusion(f32[3200,2048]{1,0:T(8,128)} %bitcast.134, s32[3072]{0:T(1024)S(1)} %copy-done.12), kind=kCustom, calls=%fused_computation.1 | custom fusion | bytes 41953280 | tf_op jit(solution)/shard_map/gather | solution.py:199
  1129.9 23.6 reshape.337
  1153.6 24.9 %multiply_reduce_fusion = (f32[640,4]{1,0:T(8,128)S(1)}, f32[640,2048]{1,0:T(8,128)}) fusion(f32[640,4,2048]{2,1,0:T(4,128)} %reshape.337, f32[640,2048]{1,0:T(8,128)} %convert_element_type.268, f32[640,4]{1,0:T(8,128)S(1)} %copy-done.22), kind=kLoop, calls=%fused_computation.9 | loop fusion | flops 19658240 | bytes 31477760 | tf_op jit(solution)/shard_map/reduce_sum | solution.py:221
  1189.1 18.8 reduce_sum.178
  1216.5 52.2 %reduce-scatter.17.cloned.1.call-done = bf16[160,2048]{1,0:T(8,128)(2,1)} async-done(((bf16[640,2048]{1,0:T(8,128)(2,1)}), bf16[160,2048]{1,0:T(8,128)(2,1)}) %reduce-scatter.17.cloned.1.call-update) | async-done | bytes 655376 | tf_op jit(solution)/shard_map/reduce_scatter | solution.py:271
  1316.6 14.2 convolution_convert_fusion.1
  1330.7 22.8 convert_element_type.304
  1430.5 12.2 fusion.8
  1442.6 19.7 convert_element_type.299
  1462.3 20.7 copy.353
  1483.1 19.4 convert_element_type.301
  1504.2 23.7 convolution_convert_fusion
  1527.9 38.1 %convert_element_type.294 = bf16[8,2,4,256,2,352]{3,2,1,5,4,0:T(4,128)(2,1)} reshape(bf16[8,2048,704]{1,2,0:T(8,128)(2,1)} %convolution_convert_fusion) | data formatting | bytes 46137344 | tf_op jit(solution)/shard_map/convert_element_type | solution.py:371
  1566.0 39.6 %copy.352 = bf16[8,4,2,256,2,352]{3,2,1,5,4,0:T(2,128)(2,1)} copy(bf16[8,4,2,256,2,352]{3,1,2,5,4,0:T(4,128)(2,1)} %bitcast.136) | data formatting | bytes 46137344 | tf_op jit(solution)/shard_map/convert_element_type | solution.py:371
  1605.6 38.3 %convert_element_type.296 = bf16[8,2048,2,352]{1,3,2,0:T(8,128)(2,1)} reshape(bf16[8,4,2,256,2,352]{3,2,1,5,4,0:T(2,128)(2,1)} %copy.352) | data formatting | bytes 46137344 | tf_op jit(solution)/shard_map/convert_element_type | solution.py:371
  1667.3 89.6 %reduce-scatter.27.cloned.1.call-done = bf16[8,352,256]{2,1,0:T(8,128)(2,1)} async-done(((bf16[8,352,2048]{2,1,0:T(8,128)(2,1)}), bf16[8,352,256]{2,1,0:T(8,128)(2,1)}) %reduce-scatter.27.cloned.1.call-update) | async-done | bytes 1441808 | tf_op jit(solution)/shard_map/reduce_scatter | solution.py:373
  1757.0 149.3 %reduce-scatter.25.cloned.1.call-done = bf16[8,256,2,352]{1,3,2,0:T(8,128)(2,1)} async-done(((bf16[8,2048,2,352]{1,3,2,0:T(8,128)(2,1)}), bf16[8,256,2,352]{1,3,2,0:T(8,128)(2,1)}) %reduce-scatter.25.cloned.1.call-update) | async-done | bytes 2883600 | tf_op jit(solution)/shard_map/reduce_scatter | solution.py:370
  1907.5 122.5 %all-reduce.5.cloned.1.call-done = f32[2048,8]{0,1:T(8,128)} async-done(((f32[2048,8]{0,1:T(8,128)}), f32[2048,8]{0,1:T(8,128)}) %all-reduce.5.cloned.1.call-update) | async-done | bytes 65552 | tf_op jit(solution)/shard_map/psum | solution.py:331
  2031.4 28.3 %all-gather.47.cloned.1.call-done = bf16[1408,1024]{1,0:T(8,128)(2,1)} async-done(((bf16[1408,256]{1,0:T(8,128)(2,1)}), bf16[1408,1024]{1,0:T(8,128)(2,1)}) %all-gather.47.cloned.1.call-update) | async-done | bytes 2883600 | tf_op jit(solution)/shard_map/all_gather | solution.py:402
  2064.7 40.5 %all-gather.45.cloned.1.call-done = bf16[1024,2,1408]{2,1,0:T(2,128)(2,1)} async-done(((bf16[256,2,1408]{2,1,0:T(2,128)(2,1)}), bf16[1024,2,1408]{2,1,0:T(2,128)(2,1)}) %all-gather.45.cloned.1.call-update) | async-done | bytes 5767184 | tf_op jit(solution)/shard_map/all_gather | solution.py:399
  2113.7 25.8 %reduce-scatter.31.cloned.1.call-done = bf16[16,12]{1,0:T(8,128)(2,1)} async-done(((bf16[128,12]{1,0:T(8,128)(2,1)}), bf16[16,12]{1,0:T(8,128)(2,1)}) %reduce-scatter.31.cloned.1.call-update) | async-done | bytes 400
  2160.5 52.4 %reduce-scatter.19.cloned.1.call-done = bf16[160,2048]{1,0:T(8,128)(2,1)} async-done(((bf16[640,2048]{1,0:T(8,128)(2,1)}), bf16[160,2048]{1,0:T(8,128)(2,1)}) %reduce-scatter.19.cloned.1.call-update) | async-done | bytes 655376 | tf_op jit(solution)/shard_map/reduce_scatter | solution.py:319
  2214.4 43.9 %all-reduce.1 = (f32[2,2048]{1,0:T(2,128)S(1)}, f32[2048]{0:T(1024)S(1)}) all-reduce(f32[2,2048]{1,0:T(2,128)S(1)} %pad_maximum_fusion.15, f32[2048]{0:T(1024)S(1)} %bitcast.172), channel_id=1, replica_groups=mesh['rep'=4,'fsdp'=2,'tensor'=4] {'rep','fsdp','tensor'}, use_global_device_ids=true, to_apply=%region_26.27 | all-reduce | flops 6144 | bytes 49152 | tf_op jit(solution)/shard_map/psum | solution.py:331
  2271.8 26.0 %all-gather.37.cloned.1.call-done = bf16[3,1024,512]{2,1,0:T(8,128)(2,1)} async-done(((bf16[3,256,512]{2,1,0:T(8,128)(2,1)}), bf16[3,1024,512]{2,1,0:T(8,128)(2,1)}) %all-gather.37.cloned.1.call-update) | async-done | bytes 3145744 | tf_op jit(solution)/shard_map/all_gather | solution.py:384
  2303.3 40.2 %all-gather.43.cloned.1.call-done = bf16[8,352,1024]{2,1,0:T(8,128)(2,1)} async-done(((bf16[8,352,256]{2,1,0:T(8,128)(2,1)}), bf16[8,352,1024]{2,1,0:T(8,128)(2,1)}) %all-gather.43.cloned.1.call-update) | async-done | bytes 5767184 | tf_op jit(solution)/shard_map/all_gather | solution.py:396
  2352.1 70.8 %all-gather.41.cloned.1.call-done = bf16[8,1024,2,352]{1,3,2,0:T(8,128)(2,1)} async-done(((bf16[8,256,2,352]{1,3,2,0:T(8,128)(2,1)}), bf16[8,1024,2,352]{1,3,2,0:T(8,128)(2,1)}) %all-gather.41.cloned.1.call-update) | async-done | bytes 11534352 | tf_op jit(solution)/shard_map/all_gather | solution.py:393
  2422.9 13.3 convert_element_type.297
  (390 shorter events, 362.9 us)
Async XLA Ops:
  7.2 66.3 %all-gather.17.cloned.1.call-start = ((), (), s32[]{:S(2)}) async-start(), calls=%async_computation.10 | async-start | bytes 3276800 | tf_op jit(solution)/shard_map/all_gather | solution.py:133
  12.7 235.1 %copy-start.47 = (f32[1,2048]{1,0:T(1,128)}, f32[1,2048]{1,0:T(1,128)S(1)}, u32[]{:S(2)}) copy-start(f32[1,2048]{1,0:T(1,128)S(1)} %get-tuple-element.138) | copy-start | bytes 24580
  16.8 138.0 %all-gather.19.cloned.1.call-start = ((), (), s32[]{:S(2)}) async-start(), calls=%async_computation.11 | async-start | bytes 9437184 | tf_op jit(solution)/shard_map/all_gather | solution.py:107
  21.5 168.0 %all-gather.21.cloned.1.call-start = ((), (), s32[]{:S(2)}) async-start(), calls=%async_computation.12 | async-start | bytes 3145728 | tf_op jit(solution)/shard_map/all_gather | solution.py:109
  22.2 224.2 %reduce-scatter.13.cloned.1.call-start = ((), (), s32[]{:S(2)}) async-start(), calls=%async_computation.13 | async-start | bytes 3276800 | tf_op jit(solution)/shard_map/reduce_scatter | solution.py:169
  28.8 146.9 %copy-start.23 = (f32[640,64]{1,0:T(8,128)}, f32[640,64]{1,0:T(8,128)S(1)}, u32[]{:S(2)}) copy-start(f32[640,64]{1,0:T(8,128)S(1)} %get-tuple-element.140) | copy-start | bytes 491524
  28.8 146.9 %copy-start.25 = (f32[640,64]{1,0:T(8,128)}, f32[640,64]{1,0:T(8,128)S(1)}, u32[]{:S(2)}) copy-start(f32[640,64]{1,0:T(8,128)S(1)} %get-tuple-element.141) | copy-start | bytes 491524
  194.1 108.2 %all-gather.33.cloned.1.call-start = ((), (), s32[]{:S(2)}) async-start(), calls=%async_computation.20 | async-start | bytes 3276800 | tf_op jit(solution)/shard_map/all_gather | solution.py:177
  194.7 248.8 %all-gather.29.cloned.1.call-start = ((), (), s32[]{:S(2)}) async-start(), calls=%async_computation.17 | async-start | bytes 17301504 | tf_op jit(solution)/shard_map/all_gather | solution.py:118
  195.3 305.2 %all-gather.23.cloned.1.call-start = ((), (), s32[]{:S(2)}) async-start(), calls=%async_computation.14 | async-start | bytes 3276800 | tf_op jit(solution)/shard_map/all_gather | solution.py:176
  250.0 325.4 %all-gather.31.cloned.1.call-start = ((), (), s32[]{:S(2)}) async-start(), calls=%async_computation.18 | async-start | bytes 8650752 | tf_op jit(solution)/shard_map/all_gather | solution.py:119
  250.8 596.6 %all-gather.25.cloned.1.call-start = ((), (), s32[]{:S(2)}) async-start(), calls=%async_computation.15 | async-start | bytes 34603008 | tf_op jit(solution)/shard_map/all_gather | solution.py:116
  251.5 738.3 %all-gather.27.cloned.1.call-start = ((), (), s32[]{:S(2)}) async-start(), calls=%async_computation.16 | async-start | bytes 17301504 | tf_op jit(solution)/shard_map/all_gather | solution.py:117
  252.1 1016.6 %reduce-scatter.17.cloned.1.call-start = ((), (), s32[]{:S(2)}) async-start(), calls=%async_computation.21 | async-start | bytes 3276800 | tf_op jit(solution)/shard_map/reduce_scatter | solution.py:271
  277.6 222.9 %copy-start.43 = (bf16[2048,8]{0,1:T(8,128)(2,1)}, bf16[2048,8]{0,1:T(8,128)(2,1)S(1)}, u32[]{:S(2)}) copy-start(bf16[2048,8]{0,1:T(8,128)(2,1)S(1)} %all_gather.78) | copy-start | bytes 98308
  537.7 309.7 %copy-start.79 = (pred[8,400]{1,0:T(8,128)(4,1)}, pred[8,400]{1,0:T(8,128)(4,1)S(1)}, u32[]{:S(2)}) copy-start(pred[8,400]{1,0:T(8,128)(4,1)S(1)} %broadcast_in_dim.76) | copy-start | bytes 9604
  537.8 452.0 %copy-start.73 = (f32[8,400]{1,0:T(8,128)}, f32[8,400]{1,0:T(8,128)S(1)}, u32[]{:S(2)}) copy-start(f32[8,400]{1,0:T(8,128)S(1)} %mul.616) | copy-start | bytes 38404
  1009.9 75.1 %copy-start.36 = (bf16[8,400,352]{2,1,0:T(8,128)(2,1)}, bf16[8,400,352]{2,1,0:T(8,128)(2,1)S(1)}, u32[]{:S(2)}) copy-start(bf16[8,400,352]{2,1,0:T(8,128)(2,1)S(1)} %get-tuple-element.110) | copy-start | bytes 6758404
  1216.4 52.3 %copy-start.48 = (f32[1,2048]{1,0:T(1,128)S(1)}, f32[1,2048]{1,0:T(1,128)}, u32[]{:S(2)}) copy-start(f32[1,2048]{1,0:T(1,128)} %copy-done.47) | copy-start | bytes 24580
  1216.4 52.3 %copy-start.70 = (f32[160]{0:T(256)S(1)}, f32[160]{0:T(256)}, u32[]{:S(2)}) copy-start(f32[160]{0:T(256)} %copy-done.69) | copy-start | bytes 1924
  1216.4 148.5 %all-gather.35.cloned.1.call-start = ((), (), s32[]{:S(2)}) async-start(), calls=%async_computation.22 | async-start | bytes 3276800 | tf_op jit(solution)/shard_map/all_gather | solution.py:281
  1274.6 373.1 %reduce-scatter.29.cloned.1.call-start = ((), (), s32[]{:S(2)}) async-start(), calls=%async_computation.34 | async-start | bytes 6488064 | tf_op jit(solution)/shard_map/reduce_scatter | solution.py:379
  1314.8 334.8 %all-reduce.7.cloned.1.call-start = ((), (), s32[]{:S(2)}) async-start(), calls=%async_computation.37 | async-start | bytes 23068672
  1364.2 292.1 %reduce-scatter.23.cloned.1.call-start = ((), (), s32[]{:S(2)}) async-start(), calls=%async_computation.26 | async-start | bytes 2359296 | tf_op jit(solution)/shard_map/reduce_scatter | solution.py:367
  1382.3 284.5 %reduce-scatter.21.cloned.1.call-start = ((), (), s32[]{:S(2)}) async-start(), calls=%async_computation.24 | async-start | bytes 7077888 | tf_op jit(solution)/shard_map/reduce_scatter | solution.py:361
  1428.8 328.1 %reduce-scatter.27.cloned.1.call-start = ((), (), s32[]{:S(2)}) async-start(), calls=%async_computation.31 | async-start | bytes 12976128 | tf_op jit(solution)/shard_map/reduce_scatter | solution.py:373
  1502.5 403.8 %reduce-scatter.25.cloned.1.call-start = ((), (), s32[]{:S(2)}) async-start(), calls=%async_computation.29 | async-start | bytes 25952256 | tf_op jit(solution)/shard_map/reduce_scatter | solution.py:370
  1644.0 386.0 %all-reduce.5.cloned.1.call-start = ((), (), s32[]{:S(2)}) async-start(), calls=%async_computation.28 | async-start | bytes 131072 | tf_op jit(solution)/shard_map/psum | solution.py:331
  1647.6 412.1 %all-gather.47.cloned.1.call-start = ((), (), s32[]{:S(2)}) async-start(), calls=%async_computation.35 | async-start | bytes 3604480 | tf_op jit(solution)/shard_map/all_gather | solution.py:402
  1648.2 457.0 %all-gather.45.cloned.1.call-start = ((), (), s32[]{:S(2)}) async-start(), calls=%async_computation.33 | async-start | bytes 7208960 | tf_op jit(solution)/shard_map/all_gather | solution.py:399
  1653.2 486.3 %reduce-scatter.31.cloned.1.call-start = ((), (), s32[]{:S(2)}) async-start(), calls=%async_computation.36 | async-start | bytes 36864
  1656.2 501.7 %all-gather.39.cloned.1.call-start = ((), (), s32[]{:S(2)}) async-start(), calls=%async_computation.27 | async-start | bytes 1310720 | tf_op jit(solution)/shard_map/all_gather | solution.py:390
  1656.9 555.9 %reduce-scatter.19.cloned.1.call-start = ((), (), s32[]{:S(2)}) async-start(), calls=%async_computation.23 | async-start | bytes 3276800 | tf_op jit(solution)/shard_map/reduce_scatter | solution.py:319
  1665.9 602.1 %reduce-scatter.15.cloned.1.call-start = ((), (), s32[]{:S(2)}) async-start(), calls=%async_computation.19 | async-start | bytes 3276800 | tf_op jit(solution)/shard_map/reduce_scatter | solution.py:209
  1666.7 239.6 %copy-start.63 = (f32[640]{0:T(1024)S(1)}, f32[640]{0:T(1024)}, u32[]{:S(2)}) copy-start(f32[640]{0:T(1024)} %copy-done.62) | copy-start | bytes 7684
  1666.7 631.1 %all-gather.37.cloned.1.call-start = ((), (), s32[]{:S(2)}) async-start(), calls=%async_computation.25 | async-start | bytes 3932160 | tf_op jit(solution)/shard_map/all_gather | solution.py:384
  1667.3 676.2 %all-gather.43.cloned.1.call-start = ((), (), s32[]{:S(2)}) async-start(), calls=%async_computation.32 | async-start | bytes 7208960 | tf_op jit(solution)/shard_map/all_gather | solution.py:396
  1756.9 666.0 %all-gather.41.cloned.1.call-start = ((), (), s32[]{:S(2)}) async-start(), calls=%async_computation.30 | async-start | bytes 14417920 | tf_op jit(solution)/shard_map/all_gather | solution.py:393
  2113.6 99.3 %copy-start.11 = (bf16[160,2048]{1,0:T(8,128)(2,1)S(1)}, bf16[160,2048]{1,0:T(8,128)(2,1)}, u32[]{:S(2)}) copy-start(bf16[160,2048]{1,0:T(8,128)(2,1)} %param.14) | copy-start | bytes 1966084
  2113.6 99.3 %copy-start.51 = (f32[1,2048]{1,0:T(1,128)S(1)}, f32[1,2048]{1,0:T(1,128)}, u32[]{:S(2)}) copy-start(f32[1,2048]{1,0:T(1,128)} %copy-done.50) | copy-start | bytes 24580
  2113.6 99.3 %copy-start.76 = (f32[160]{0:T(256)S(1)}, f32[160]{0:T(256)}, u32[]{:S(2)}) copy-start(f32[160]{0:T(256)} %copy-done.75) | copy-start | bytes 1924
  2113.6 100.8 %copy-start.67 = (f32[2048]{0:T(1024)S(1)}, f32[2048]{0:T(1024)}, u32[]{:S(2)}) copy-start(f32[2048]{0:T(1024)} %get-tuple-element.98) | copy-start | bytes 24580
  2113.7 154.4 %copy-start.13 = (bf16[160,2048]{1,0:T(8,128)(2,1)S(1)}, bf16[160,2048]{1,0:T(8,128)(2,1)}, u32[]{:S(2)}) copy-start(bf16[160,2048]{1,0:T(8,128)(2,1)} %reduce-scatter.13.cloned.1.call-done) | copy-start | bytes 1966084
  2113.7 154.4 %copy-start.18 = (bf16[160,2048]{1,0:T(8,128)(2,1)S(1)}, bf16[160,2048]{1,0:T(8,128)(2,1)}, u32[]{:S(2)}) copy-start(bf16[160,2048]{1,0:T(8,128)(2,1)} %reduce-scatter.17.cloned.1.call-done) | copy-start | bytes 1966084
  2113.7 154.4 %copy-start.19 = (bf16[160,2048]{1,0:T(8,128)(2,1)S(1)}, bf16[160,2048]{1,0:T(8,128)(2,1)}, u32[]{:S(2)}) copy-start(bf16[160,2048]{1,0:T(8,128)(2,1)} %param.15) | copy-start | bytes 1966084
  2113.7 154.3 %copy-start.49 = (f32[1,2048]{1,0:T(1,128)S(1)}, f32[1,2048]{1,0:T(1,128)}, u32[]{:S(2)}) copy-start(f32[1,2048]{1,0:T(1,128)} %copy-done.47) | copy-start | bytes 24580
  2113.7 154.3 %copy-start.71 = (f32[160]{0:T(256)S(1)}, f32[160]{0:T(256)}, u32[]{:S(2)}) copy-start(f32[160]{0:T(256)} %copy-done.69) | copy-start | bytes 1924
  2113.7 154.3 %copy-start.78 = (f32[160]{0:T(256)S(1)}, f32[160]{0:T(256)}, u32[]{:S(2)}) copy-start(f32[160]{0:T(256)} %copy-done.77) | copy-start | bytes 1924
  (73 other events, 617.6 us)
Sparse Core Ops, SparseCore 0:
  16.9 56.5 all-gather.16
  75.6 79.1 all-gather.18
  156.3 33.1 all-gather.20
  194.2 52.0 reduce-scatter.12
  247.8 54.4 all-gather.32
  303.7 139.7 all-gather.28
  445.7 54.7 all-gather.22
  502.1 73.2 all-gather.30
  576.9 270.3 all-gather.24
  848.7 141.0 all-gather.26
  1216.5 52.0 reduce-scatter.16
  1274.7 54.4 all-gather.34
  1332.7 57.7 reduce-scatter.28
  1394.2 160.8 all-reduce.6
  1558.8 41.3 reduce-scatter.22
  1604.4 61.7 reduce-scatter.20
  1670.1 86.7 reduce-scatter.26
  1760.4 145.8 reduce-scatter.24
  1912.5 117.4 all-reduce.4
  2031.4 28.1 all-gather.46
  2061.8 43.3 all-gather.44
  2108.2 31.2 reduce-scatter.30
  2141.1 16.7 all-gather.38
  2160.7 52.1 reduce-scatter.18
  2215.3 52.6 reduce-scatter.14
  2269.5 28.2 all-gather.36
  2299.3 44.1 all-gather.42
  2345.2 77.6 all-gather.40
where the time goes:
time: 2450 us; the launch traced here: 2440 us
  waiting for transfers between devices  1470 us (60%)
  local copies, waits for them, and re-layouts  503 us (21%)
  matrix products  261 us (11%)
  other arithmetic  125 us (5%)
  blocking collectives  68.3 us (3%)
    all_gather x1, waiting for transfers between devices, fetch_experts(): lax.all_gather(expert_gate_up, 'fsdp', axis=1, tiled=True)  243 us
    reduce_scatter x1, waiting for transfers between devices, shards(): lax.psum_scatter(reordered[3].astype(jnp.bfloat16), ('rep', 'fsdp'), scat...  149 us
    all_gather x1, waiting for transfers between devices, fetch_experts(): lax.all_gather(shared_gate_up, 'fsdp', axis=0, tiled=True)  123 us
    psum x1, waiting for transfers between devices, shards(): lax.psum((jnp.stack([gain_one_grad, gain_two_grad]), router_grad, gate_ve...  123 us
    convert_element_type x3, local copies, waits for them, and re-layouts, shards(): reordered[3].astype(jnp.bfloat16)  116 us
    all_gather x1, waiting for transfers between devices, fetch_experts(): lax.all_gather(expert_down, 'fsdp', axis=2, tiled=True)  116 us
    reduce_scatter x1, waiting for transfers between devices, shards(): lax.psum_scatter(reordered[4].astype(jnp.bfloat16), ('rep', 'fsdp'), scat...  89.6 us
    all_gather x1, waiting for transfers between devices, fetch_dense(): lax.all_gather(qkv_weight, 'fsdp', axis=1, tiled=True)  81.3 us
  transfers between devices with their start and end apart: 28, of which 23 were waited for; matrix products, arithmetic and copies ran while one was open for 25% of the time, Pallas kernels for 0%

commit v1 on v0

v1 whole, which is shorter than its diff:
```python
import functools

import jax
import jax.numpy as jnp
from jax import lax
from jax.experimental import pallas as pl
from jax.experimental.pallas import tpu as pltpu
from jax.sharding import PartitionSpec as P

HEAD_DIM = 128
EXPERTS = 8
LENGTH = 640
PIECE = 256
EPSILON = 1e-06
BF16 = jnp.bfloat16
F32 = jnp.float32
COLS = 256


def rope_tables(length, head_dim):
    half_dim = head_dim // 2
    frequency = 1000000.0 ** (-jnp.arange(half_dim, dtype=F32) * (2.0 / head_dim))
    angles = jnp.arange(length, dtype=F32)[:, None] * frequency[None, :]
    return (jnp.cos(angles), jnp.sin(angles))


def rotate(head_rows, cos_table, sin_table):
    half_dim = head_rows.shape[-1] // 2
    leading = head_rows[..., :half_dim]
    trailing = head_rows[..., half_dim:]
    cos_rows = cos_table[:, None, :]
    sin_rows = sin_table[:, None, :]
    return jnp.concatenate(
        [leading * cos_rows - trailing * sin_rows, trailing * cos_rows + leading * sin_rows],
        axis=-1,
    )


def visible_mask(starts_row, length, piece_len):
    position = jnp.arange(length, dtype=jnp.int32)
    inside = (position[None, :] >= starts_row[:, None]) & (
        position[None, :] < starts_row[:, None] + piece_len
    )
    label_ids = jnp.arange(1, starts_row.shape[0] + 1, dtype=jnp.int32)[:, None]
    labels = jnp.sum(jnp.where(inside, label_ids, 0), axis=0)
    causal = position[None, :] <= position[:, None]
    same_piece = (labels[:, None] == labels[None, :]) & (labels[:, None] > 0)
    return causal | same_piece


def after(value, *others):
    return lax.optimization_barrier((value,) + others)[0]


def swap_y(a):
    return lax.ppermute(a, "fsdp", [(0, 1), (1, 0)])


def swap_x(a):
    n = lax.axis_size("rep")
    return lax.ppermute(a, "rep", [(i, i ^ 2) for i in range(n)])


def swap_core(a):
    n = lax.axis_size("rep")
    return lax.ppermute(a, "rep", [(i, i ^ 1) for i in range(n)])


def gather_rows(block):
    n = lax.axis_size("tensor")
    z = lax.axis_index("tensor")
    rows = block.shape[0]
    right, left = [block], [block]
    for _ in range(n - 1):
        right.append(lax.ppermute(right[-1], "tensor", [(i, i + 1) for i in range(n - 1)]))
        left.append(lax.ppermute(left[-1], "tensor", [(i, i - 1) for i in range(1, n)]))
    out = jnp.zeros((n * rows,) + block.shape[1:], block.dtype)
    out = lax.dynamic_update_slice_in_dim(out, block, z * rows, 0)
    for k in range(1, n):
        piece = jnp.where(z >= k, right[k], left[n - k])
        out = lax.dynamic_update_slice_in_dim(out, piece, lax.rem(z - k + n, n) * rows, 0)
    return out


def scatter_rows(total):
    n = lax.axis_size("tensor")
    z = lax.axis_index("tensor")
    rows = total.shape[0] // n

    def block(b):
        return lax.dynamic_slice_in_dim(total, jnp.clip(b, 0, n - 1) * rows, rows, 0).astype(F32)

    right = left = None
    for s in range(n - 1):
        to_right, to_left = block(n - 1 - s + z), block(s - (n - 1) + z)
        if s > 0:
            to_right = to_right + right.astype(F32)
            to_left = to_left + left.astype(F32)
        right = lax.ppermute(
            to_right.astype(BF16), "tensor", [(i, i + 1) for i in range(n - 1) if i <= s]
        )
        left = lax.ppermute(
            to_left.astype(BF16), "tensor", [(i, i - 1) for i in range(1, n) if n - 1 - i <= s]
        )
    return block(z) + right.astype(F32) + left.astype(F32)


def others_of(own, f, axis):
    if lax.axis_size("fsdp") == 2:
        return swap_y(own)
    whole = lax.all_gather(own, "fsdp", axis=axis, tiled=True)
    size = own.shape[axis]
    turned = jnp.roll(whole, -f * size, axis=axis)
    return lax.slice_in_dim(turned, size, whole.shape[axis], axis=axis)


def reduce_fsdp(own, other, f, axis):
    if lax.axis_size("fsdp") == 2:
        return own.astype(F32) + swap_y(other).astype(F32)
    whole = jnp.roll(jnp.concatenate([own, other], axis=axis), f * own.shape[axis], axis=axis)
    return lax.psum_scatter(whole, "fsdp", scatter_dimension=axis, tiled=True).astype(F32)


def sum_small(own, other, f):
    if lax.axis_size("fsdp") == 2:
        total = own + swap_y(other)
    else:
        whole = jnp.roll(jnp.concatenate([own, other], axis=1), f * own.shape[1], axis=1)
        total = lax.psum_scatter(whole, "fsdp", scatter_dimension=1, tiled=True)
    return sum_tensor(sum_rep(total))


def sum_rep(total):
    total = total + swap_core(total)
    return total + swap_x(total)


def sum_tensor(total):
    n = lax.axis_size("tensor")
    step = 1
    while step < n:
        total = total + lax.ppermute(total, "tensor", [(i, i ^ step) for i in range(n)])
        step *= 2
    return total


def dot_nt(a, b):
    return lax.dot_general(a, b, (((1,), (1,)), ((), ())), preferred_element_type=F32)


def dot_nn(a, b):
    return lax.dot_general(a, b, (((1,), (0,)), ((), ())), preferred_element_type=F32)


def experts_kernel(
    rows, width, own_width, hidden,
    x0, x1, c0, c1, gate, w_own, w_oth,
    dw_own, dw_oth, mix0, mix1, ng0, ng1, gate_grad,
    xv, cv, wg, wu, wd, ga, pg, pu, st_mix, st_ng, st_dw, in_sem, mix_sem, ng_sem, dw_sem,
):
    seq = rows // 2
    loads = []

    def load(src, dst):
        copy = pltpu.make_async_copy(src, dst, in_sem.at[len(loads)])
        copy.start()
        loads.append(copy)

    for part, w in ((0, wg), (1, wu), (2, wd)):
        for k in range(2):
            r = pl.ds(k * hidden, hidden)
            load(w_own.at[k, part], w.at[r, pl.ds(0, own_width)])
            load(w_oth.at[k, part], w.at[r, pl.ds(own_width, width - own_width)])
        if part == 0:
            load(x0, xv.at[pl.ds(0, seq)])
            load(x1, xv.at[pl.ds(seq, seq)])
        if part == 1:
            load(c0, cv.at[pl.ds(0, seq)])
            load(c1, cv.at[pl.ds(seq, seq)])
    for copy in loads:
        copy.wait()

    tiles = rows // COLS

    def out_copies(t, slot):
        copies = []
        for stage, outs, sem in ((st_mix, (mix0, mix1), mix_sem), (st_ng, (ng0, ng1), ng_sem)):
            for part in range(2):
                copies.append((stage.at[slot, pl.ds(part * 128, 128)], outs, sem.at[slot, part], part))
        return copies

    def start_out(t, slot):
        for src, outs, sem, part in out_copies(t, slot):
            first = t * COLS + part * 128

            @pl.when(first < seq)
            def _():
                pltpu.make_async_copy(src, outs[0].at[pl.ds(pl.multiple_of(first, 128), 128)], sem).start()

            @pl.when(first >= seq)
            def _():
                pltpu.make_async_copy(
                    src, outs[1].at[pl.ds(pl.multiple_of(first - seq, 128), 128)], sem
                ).start()

    def wait_out(slot):
        for src, outs, sem, part in out_copies(0, slot):
            pltpu.make_async_copy(src, outs[0].at[pl.ds(0, 128)], sem).wait()

    def token_tile(t, carry):
        slot = lax.rem(t, 2)
        here = pl.ds(pl.multiple_of(t * COLS, COLS), COLS)
        g = dot_nt(wg[...], xv[here, :])
        u = dot_nt(wu[...], xv[here, :])
        h = dot_nt(wd[...], cv[here, :])
        sig = jax.nn.sigmoid(g)
        act = g * sig * u
        product = act * h
        scale_rows = []
        for k in range(2):
            part = product[k * hidden : (k + 1) * hidden]
            gate_grad[pl.ds(k, 1), here] = jnp.sum(part, axis=0, keepdims=True)
            scale_rows.append(jnp.broadcast_to(gate[pl.ds(k, 1), here], (hidden, COLS)))
        scale = jnp.concatenate(scale_rows, axis=0)
        back = scale * h
        ga_t = (scale * act).astype(BF16)
        pg_t = (back * u * sig * (1.0 + g * (1.0 - sig))).astype(BF16)
        pu_t = (back * g * sig).astype(BF16)
        ga[:, here] = ga_t
        pg[:, here] = pg_t
        pu[:, here] = pu_t

        @pl.when(t >= 2)
        def _():
            wait_out(slot)

        st_mix[slot] = dot_nn(ga_t.T, wd[...]).astype(BF16)
        st_ng[slot] = (dot_nn(pg_t.T, wg[...]) + dot_nn(pu_t.T, wu[...])).astype(BF16)
        start_out(t, slot)
        return carry

    lax.fori_loop(0, tiles, token_tile, 0)

    def wait_dw(slot):
        for part in range(3):
            for k in range(2):
                pltpu.make_async_copy(
                    st_dw.at[slot, part, pl.ds(k * hidden, hidden)],
                    dw_own.at[k, part, :, pl.ds(0, COLS)],
                    dw_sem.at[slot, part, k],
                ).wait()

    def weight_tile(n, slot, src_col, dst, dst_col, first):
        cols = pl.ds(pl.multiple_of(src_col, COLS), COLS)

        @pl.when(jnp.logical_not(first))
        def _():
            wait_dw(slot)

        xs = xv[:, cols]
        st_dw[slot, 0] = dot_nn(pg[...], xs).astype(BF16)
        st_dw[slot, 1] = dot_nn(pu[...], xs).astype(BF16)
        st_dw[slot, 2] = dot_nn(ga[...], cv[:, cols]).astype(BF16)
        for part in range(3):
            for k in range(2):
                pltpu.make_async_copy(
                    st_dw.at[slot, part, pl.ds(k * hidden, hidden)],
                    dst.at[k, part, :, pl.ds(pl.multiple_of(dst_col, COLS), COLS)],
                    dw_sem.at[slot, part, k],
                ).start()

    oth_tiles = (width - own_width) // COLS
    own_tiles = own_width // COLS

    def oth_tile(n, carry):
        weight_tile(n, lax.rem(n, 2), own_width + n * COLS, dw_oth, n * COLS, n < 2)
        return carry

    def own_tile(n, carry):
        weight_tile(n, lax.rem(n + oth_tiles, 2), n * COLS, dw_own, n * COLS, n + oth_tiles < 2)
        return carry

    lax.fori_loop(0, oth_tiles, oth_tile, 0)
    lax.fori_loop(0, own_tiles, own_tile, 0)
    for slot in range(2):
        wait_out(slot)
        wait_dw(slot)


def experts_call(x0, x1, c0, c1, gate, w_own, w_oth):
    seq, width = x0.shape
    rows = 2 * seq
    hidden, own_width = w_own.shape[2], w_own.shape[3]
    any_spec = pl.BlockSpec(memory_space=pl.ANY)
    vmem_spec = pl.BlockSpec(memory_space=pltpu.VMEM)
    out_rows = jax.ShapeDtypeStruct((seq, width), BF16)
    macs = 9 * rows * width * 2 * hidden
    return pl.pallas_call(
        functools.partial(experts_kernel, rows, width, own_width, hidden),
        out_shape=[
            jax.ShapeDtypeStruct(w_own.shape, BF16),
            jax.ShapeDtypeStruct(w_oth.shape, BF16),
            out_rows, out_rows, out_rows, out_rows,
            jax.ShapeDtypeStruct((8, rows), F32),
        ],
        in_specs=[any_spec] * 4 + [vmem_spec] + [any_spec] * 2,
        out_specs=[any_spec] * 6 + [vmem_spec],
        scratch_shapes=[
            pltpu.VMEM((rows, width), BF16),
            pltpu.VMEM((rows, width), BF16),
            pltpu.VMEM((2 * hidden, width), BF16),
            pltpu.VMEM((2 * hidden, width), BF16),
            pltpu.VMEM((2 * hidden, width), BF16),
            pltpu.VMEM((2 * hidden, rows), BF16),
            pltpu.VMEM((2 * hidden, rows), BF16),
            pltpu.VMEM((2 * hidden, rows), BF16),
            pltpu.VMEM((2, COLS, width), BF16),
            pltpu.VMEM((2, COLS, width), BF16),
            pltpu.VMEM((2, 3, 2 * hidden, COLS), BF16),
            pltpu.SemaphoreType.DMA((16,)),
            pltpu.SemaphoreType.DMA((2, 2)),
            pltpu.SemaphoreType.DMA((2, 2)),
            pltpu.SemaphoreType.DMA((2, 3, 2)),
        ],
        cost_estimate=pl.CostEstimate(
            flops=2 * macs, bytes_accessed=8 * rows * width + 16 * hidden * width, transcendentals=rows * hidden
        ),
        compiler_params=pltpu.CompilerParams(vmem_limit_bytes=56 * 2**20),
        name="experts",
    )(x0, x1, c0, c1, gate, w_own, w_oth)


def place_kernel(count, table, *refs):
    sources, out = refs[:count], refs[count]
    which = table[0, pl.program_id(0)]
    for k in range(count):

        @pl.when(which == k)
        def _():
            out[...] = sources[k][...].astype(out.dtype)


def place_call(sources, table, slots, parts, dtype):
    first, length = parts
    hidden, width = sources[0].shape[2:]

    def source_map(k):
        return lambda e, tab: (tab[1 + k, e], first // length, 0, 0)

    return pl.pallas_call(
        functools.partial(place_kernel, len(sources)),
        out_shape=jax.ShapeDtypeStruct((slots, length, hidden, width), dtype),
        grid_spec=pltpu.PrefetchScalarGridSpec(
            num_scalar_prefetch=1,
            grid=(slots,),
            in_specs=[
                pl.BlockSpec((1, length, hidden, width), source_map(k)) for k in range(len(sources))
            ],
            out_specs=pl.BlockSpec((1, length, hidden, width), lambda e, tab: (e, 0, 0, 0)),
        ),
        compiler_params=pltpu.CompilerParams(vmem_limit_bytes=40 * 2**20),
        name="place",
    )(table, *sources)


def routed_table(c, x):
    e = jnp.arange(EXPERTS, dtype=jnp.int32)
    firsts = [4 * c + 2 * x, 4 * c + 2 * (1 - x), 4 * (1 - c) + 2 * x, 4 * (1 - c) + 2 * (1 - x)]
    which = sum(jnp.where(e // 2 * 2 == first, k, 0) for k, first in enumerate(firsts))
    return jnp.stack([which] + [(e > first).astype(jnp.int32) for first in firsts]).astype(jnp.int32)


def shared_table(c, x):
    q = jnp.arange(4, dtype=jnp.int32)
    which = jnp.where(q // 2 == c, 0, 1)

    def blocks(half):
        return jnp.clip(q - 2 * half, 0, 1) ^ x

    return jnp.stack([which, blocks(c), blocks(1 - c)]).astype(jnp.int32)


def shards(
    block_input,
    cotangent,
    piece_starts,
    expert_ids,
    norm_gains,
    qkv_weight,
    qkv_bias,
    out_weight,
    router_weight,
    shared_gate,
    expert_gate_up,
    expert_down,
    shared_gate_up,
    shared_down,
):
    f = lax.axis_index("fsdp")
    owners = lax.axis_size("fsdp")
    r = lax.axis_index("rep")
    c, x = r % 2, r // 2
    shard = norm_gains.shape[1]
    width = owners * shard
    local_width = qkv_weight.shape[2]
    local_heads = local_width // HEAD_DIM
    half_width = local_width // 2
    hidden = expert_gate_up.shape[3]
    scale = HEAD_DIM ** (-0.5)

    def turn(rows):
        return jnp.roll(rows, -f * shard, axis=1)

    def turn_back(rows):
        return jnp.roll(rows, f * shard, axis=1)

    small = jnp.concatenate(
        [norm_gains.reshape(-1), router_weight.T.reshape(-1), shared_gate, qkv_bias.reshape(-1)]
    )
    small_all = jnp.concatenate([small[None], others_of(small[None], f, 0)], axis=0)
    gains = jnp.swapaxes(small_all[:, : 2 * shard].reshape(owners, 2, shard), 0, 1).reshape(2, width)
    gains = gains.astype(F32)
    router = jnp.swapaxes(
        small_all[:, 2 * shard : 11 * shard].reshape(owners, 9, shard), 0, 1
    ).reshape(9, width)
    bias = jnp.roll(small_all[:, 11 * shard :], f, axis=0).reshape(owners, 3, local_heads, -1)
    bias = jnp.moveaxis(bias, 0, 2).reshape(3, 1, local_width).astype(F32)
    ids_pair = jnp.concatenate([expert_ids, swap_core(expert_ids)], axis=0)

    def fetch_halves(weight, hidden_axis, shard_axis):
        mine = lax.dynamic_slice_in_dim(weight, c * half_width, half_width, hidden_axis)
        got = others_of(mine, f, shard_axis)
        peer = swap_core(got)
        both = jnp.where(
            c == 0,
            jnp.concatenate([got, peer], axis=hidden_axis),
            jnp.concatenate([peer, got], axis=hidden_axis),
        )
        return jnp.concatenate([weight, both], axis=shard_axis), got

    qkv_all, qkv_got = fetch_halves(qkv_weight, 2, 1)
    out_all, out_got = fetch_halves(after(out_weight, qkv_got), 0, 1)

    gate_up_t = jnp.transpose(expert_gate_up, (0, 2, 3, 1))
    shared_up_t = jnp.transpose(shared_gate_up, (1, 2, 0))

    def routed_chunk(first):
        return jnp.concatenate(
            [
                lax.dynamic_slice_in_dim(gate_up_t, first, 2, 0),
                lax.dynamic_slice_in_dim(expert_down, first, 2, 0)[:, None],
            ],
            axis=1,
        )

    def shared_chunk(q):
        return jnp.concatenate(
            [
                lax.dynamic_slice_in_dim(shared_up_t, q * hidden, hidden, 1),
                lax.dynamic_slice_in_dim(shared_down, q * hidden, hidden, 0)[None],
            ],
            axis=0,
        )[None]

    first_a, first_b = 4 * c + 2 * x, 4 * c + 2 * (1 - x)
    own_a, own_b = routed_chunk(first_a), routed_chunk(first_b)
    own_s0, own_s1 = shared_chunk(2 * c + x), shared_chunk(2 * c + 1 - x)
    oth_a = others_of(after(own_a, out_got), f, 3)
    oth_b = swap_x(oth_a)
    oth_s0 = others_of(after(own_s0, oth_a), f, 3)
    oth_s1 = swap_x(oth_s0)
    own_s = jnp.concatenate([own_s0, own_s1], axis=0)
    oth_s = jnp.concatenate([oth_s0, oth_s1], axis=0)

    cos_table, sin_table = rope_tables(LENGTH, HEAD_DIM)
    inputs_f = turn(block_input).astype(F32)
    cot_bf = turn(cotangent)
    cot_local = cot_bf.astype(F32)
    inverse_one = lax.rsqrt(jnp.mean(inputs_f * inputs_f, axis=-1, keepdims=True) + EPSILON)
    normed = gather_rows((inputs_f * inverse_one * gains[0]).astype(BF16))
    cot_rows = gather_rows(after(cot_bf, normed))
    cot_peer = swap_core(cot_rows)
    project = jnp.einsum("ld,cde->cle", normed, qkv_all, preferred_element_type=F32) + bias
    query_rows = rotate(
        project[0].reshape(LENGTH, local_heads, HEAD_DIM), cos_table, sin_table
    ).astype(BF16)
    key_rows = rotate(
        project[1].reshape(LENGTH, local_heads, HEAD_DIM), cos_table, sin_table
    ).astype(BF16)
    value_rows = project[2].reshape(LENGTH, local_heads, HEAD_DIM).astype(BF16)
    visible = visible_mask(piece_starts[0], LENGTH, PIECE)

    def attend_scores():
        raw = jnp.einsum("qhd,khd->hqk", query_rows, key_rows, preferred_element_type=F32) * scale
        return jnp.where(visible[None], raw, -1e30)

    scores = attend_scores()
    top_score = jnp.max(scores, axis=-1, keepdims=True)
    weights_exp = jnp.exp(scores - top_score)
    row_total = jnp.sum(weights_exp, axis=-1, keepdims=True)
    probs = weights_exp / row_total
    attended = (
        jnp.einsum("hqk,khd->qhd", probs.astype(BF16), value_rows, preferred_element_type=F32)
        .reshape(LENGTH, local_width)
        .astype(BF16)
    )
    heads_part = jnp.dot(attended, out_all, preferred_element_type=F32).astype(BF16)
    hidden_rows = inputs_f + scatter_rows(heads_part)
    inverse_two = lax.rsqrt(jnp.mean(hidden_rows * hidden_rows, axis=-1, keepdims=True) + EPSILON)
    mixed = gather_rows((hidden_rows * inverse_two * gains[1]).astype(BF16))
    mixed_peer = swap_core(mixed)
    mixed_pair = jnp.concatenate([mixed, mixed_peer], axis=0)

    logits = lax.dot_general(router, mixed_pair, (((1,), (1,)), ((), ())), preferred_element_type=F32)
    router_probs = jax.nn.softmax(logits[:EXPERTS], axis=0)
    shared_scale = jax.nn.sigmoid(logits[EXPERTS:])
    names = jnp.arange(EXPERTS, dtype=jnp.int32)[:, None, None]
    chosen = jnp.any(ids_pair.T[None] == names, axis=1)
    gates = jnp.where(chosen, router_probs, 0.0)

    def gate_rows(first):
        return jnp.pad(lax.dynamic_slice_in_dim(gates, first, 2, 0), ((0, 6), (0, 0)))

    data = (mixed, mixed_peer, cot_rows, cot_peer)
    dw_own_a, dw_oth_a, *rows_a, grad_a = experts_call(*data, gate_rows(first_a), own_a, oth_a)
    shared_rows = jnp.broadcast_to(shared_scale, (8, shared_scale.shape[1]))
    dw_own_s, dw_oth_s, *rows_s, grad_s = experts_call(*data, shared_rows, own_s, oth_s)
    dw_own_b, dw_oth_b, *rows_b, grad_b = experts_call(*data, gate_rows(first_b), own_b, oth_b)

    prob_grad = jnp.zeros_like(router_probs)
    prob_grad = lax.dynamic_update_slice_in_dim(prob_grad, grad_a[:2], first_a, 0)
    prob_grad = lax.dynamic_update_slice_in_dim(prob_grad, grad_b[:2], first_b, 0)
    prob_grad = jnp.where(chosen, prob_grad, 0.0)
    logit_grad = router_probs * (prob_grad - jnp.sum(router_probs * prob_grad, axis=0, keepdims=True))
    scale_logit_grad = (grad_s[0:1] + grad_s[1:2]) * shared_scale * (1.0 - shared_scale)
    small_grad = jnp.concatenate([logit_grad, scale_logit_grad], axis=0)
    high = small_grad.astype(BF16)
    low = (small_grad - high.astype(F32)).astype(BF16)
    small_pair = jnp.concatenate([high, low], axis=0)
    router_both = jnp.dot(small_pair, mixed_pair, preferred_element_type=F32)
    router_grad = router_both[:9] + router_both[9:]
    router_twice = jnp.concatenate([router, router], axis=0)

    def extra(part):
        return lax.dot_general(
            small_pair[:, part * LENGTH : (part + 1) * LENGTH],
            router_twice,
            (((0,), (0,)), ((), ())),
            preferred_element_type=F32,
        )

    def total(index):
        return (
            rows_a[index].astype(F32) + rows_s[index].astype(F32) + rows_b[index].astype(F32)
        )

    normed_for_peer = (total(3) + extra(1)).astype(BF16)
    normed_grad = total(2) + extra(0) + swap_core(normed_for_peer).astype(F32)
    normed_two_grad = scatter_rows(normed_grad.astype(BF16))
    scaled_two = normed_two_grad * gains[1]
    hidden_grad = cot_local + inverse_two * (
        scaled_two
        - hidden_rows
        * inverse_two
        * inverse_two
        * jnp.mean(scaled_two * hidden_rows, axis=-1, keepdims=True)
    )
    gain_two_grad = jnp.sum(normed_two_grad * hidden_rows * inverse_two, axis=0)
    branch_grad = gather_rows(hidden_grad.astype(BF16))

    mixer_for_peer = after(total(1).astype(BF16), branch_grad)
    mixer = (total(0) + swap_core(mixer_for_peer).astype(F32)).astype(BF16)
    result = turn_back((hidden_rows + scatter_rows(mixer)).astype(BF16))

    out_grad = jnp.einsum("lf,ld->fd", attended, branch_grad, preferred_element_type=F32).astype(BF16)
    attended_grad = jnp.einsum("ld,fd->lf", branch_grad, out_all, preferred_element_type=F32)
    attended_grad = attended_grad.astype(BF16).reshape(LENGTH, local_heads, HEAD_DIM)
    probs = jnp.exp(attend_scores() - top_score) / row_total
    value_grad = jnp.einsum("hqk,qhd->khd", probs.astype(BF16), attended_grad, preferred_element_type=F32)
    pgrad_rows = jnp.einsum("qhd,khd->hqk", attended_grad, value_rows, preferred_element_type=F32)
    score_grad = (
        probs * (pgrad_rows - jnp.sum(probs * pgrad_rows, axis=-1, keepdims=True))
    ).astype(BF16)
    query_grad = jnp.einsum("hqk,khd->qhd", score_grad, key_rows, preferred_element_type=F32) * scale
    key_grad = jnp.einsum("hqk,qhd->khd", score_grad, query_rows, preferred_element_type=F32) * scale
    project_grad = jnp.stack(
        [
            rotate(query_grad, cos_table, -sin_table).reshape(LENGTH, local_width),
            rotate(key_grad, cos_table, -sin_table).reshape(LENGTH, local_width),
            value_grad.reshape(LENGTH, local_width),
        ]
    ).astype(BF16)
    bias_grad = jnp.sum(project_grad, axis=1, dtype=F32)
    normed_one_grad = jnp.einsum("cle,cde->ld", project_grad, qkv_all, preferred_element_type=F32)
    input_row_grad = scatter_rows(normed_one_grad.astype(BF16))
    qkv_grad = jnp.einsum("ld,cle->cde", normed, project_grad, preferred_element_type=F32).astype(BF16)
    scaled_one = input_row_grad * gains[0]
    input_grad = hidden_grad + inverse_one * (
        scaled_one
        - inputs_f
        * inverse_one
        * inverse_one
        * jnp.mean(scaled_one * inputs_f, axis=-1, keepdims=True)
    )
    gain_one_grad = jnp.sum(input_row_grad * inputs_f * inverse_one, axis=0)

    def shard_sum(own, other):
        return reduce_fsdp(own, other, f, 3).astype(BF16)

    sum_a = shard_sum(dw_own_a, dw_oth_a)
    sum_s = shard_sum(dw_own_s, dw_oth_s)
    sum_b = shard_sum(dw_own_b, dw_oth_b)
    from_a, from_s, from_b = swap_x(sum_a), swap_x(sum_s), swap_x(sum_b)

    def add(one, two):
        return (one.astype(F32) + two.astype(F32)).astype(BF16)

    total_b = add(sum_b, from_a)
    total_s = add(sum_s, from_s[::-1])
    total_a = add(sum_a, from_b)
    peer_s, peer_b, peer_a = swap_core(total_s), swap_core(total_b), swap_core(total_a)
    table = routed_table(c, x)
    routed = [total_a, total_b, peer_a, peer_b]
    gate_up_out = jnp.transpose(place_call(routed, table, EXPERTS, (0, 2), F32), (0, 3, 1, 2))
    down_out = place_call(routed, table, EXPERTS, (2, 1), F32).reshape(EXPERTS, hidden, shard)
    table_s = shared_table(c, x)
    shared_up_out = place_call([total_s, peer_s], table_s, 4, (0, 2), BF16)
    shared_up_out = (
        jnp.transpose(shared_up_out, (3, 1, 0, 2)).reshape(shard, 2, 4 * hidden).astype(F32)
    )
    shared_down_out = place_call([total_s, peer_s], table_s, 4, (2, 1), F32).reshape(4 * hidden, shard)

    def dense_sum(grad, hidden_axis, shard_axis):
        keep = lax.dynamic_slice_in_dim(grad, c * half_width, half_width, hidden_axis)
        send = lax.dynamic_slice_in_dim(grad, (1 - c) * half_width, half_width, hidden_axis)
        both = add(keep, swap_core(send))
        own = lax.slice_in_dim(both, 0, shard, axis=shard_axis)
        other = lax.slice_in_dim(both, shard, width, axis=shard_axis)
        part = reduce_fsdp(own, other, f, shard_axis).astype(BF16)
        part = add(part, swap_x(part))
        peer = swap_core(part)
        return jnp.where(
            c == 0,
            jnp.concatenate([part, peer], axis=hidden_axis),
            jnp.concatenate([peer, part], axis=hidden_axis),
        ).astype(F32)

    out_out = dense_sum(out_grad, 0, 1)
    qkv_out = dense_sum(qkv_grad, 2, 1)

    early = jnp.concatenate([router_grad, gain_two_grad[None]], axis=0)
    early = sum_small(early[:, :shard], early[:, shard:], f)
    late = sum_small(gain_one_grad[None, :shard], gain_one_grad[None, shard:], f)
    gains_out = jnp.concatenate([late, early[9:10]], axis=0)
    bias_sum = sum_rep(lax.psum(bias_grad, "fsdp") if owners != 2 else bias_grad + swap_y(bias_grad))
    bias_out = lax.dynamic_slice_in_dim(
        bias_sum.reshape(3, local_heads, HEAD_DIM), f * (HEAD_DIM // owners), HEAD_DIM // owners, 2
    )
    return (
        result,
        turn_back(input_grad),
        gains_out,
        qkv_out,
        bias_out,
        out_out,
        early[:EXPERTS].T,
        early[EXPERTS],
        gate_up_out,
        down_out,
        shared_up_out,
        shared_down_out,
    )


def solution(mesh):
    in_specs = (
        P(("rep", "fsdp", "tensor"), None),
        P(("rep", "fsdp", "tensor"), None),
        P(("rep", "fsdp"), None),
        P(("rep", "fsdp"), None),
        P(None, "fsdp"),
        P(None, "fsdp", "tensor"),
        P(None, "tensor", "fsdp"),
        P("tensor", "fsdp"),
        P("fsdp", None),
        P("fsdp"),
        P(None, "fsdp", None, "tensor"),
        P(None, "tensor", "fsdp"),
        P("fsdp", None, "tensor"),
        P("tensor", "fsdp"),
    )
    out_specs = (
        P(("rep", "fsdp", "tensor"), None),
        P(("rep", "fsdp", "tensor"), None),
        P(None, "fsdp"),
        P(None, "fsdp", "tensor"),
        P(None, "tensor", "fsdp"),
        P("tensor", "fsdp"),
        P("fsdp", None),
        P("fsdp"),
        P(None, "fsdp", None, "tensor"),
        P(None, "tensor", "fsdp"),
        P("fsdp", None, "tensor"),
        P("tensor", "fsdp"),
    )
    return jax.shard_map(shards, mesh=mesh, in_specs=in_specs, out_specs=out_specs, check_vma=False)
```

time: 2450 us -> 1290 us (0.53)
  waiting for transfers between devices: 1470 us -> 531 us
  local copies, waits for them, and re-layouts: 503 us -> 128 us
  matrix products: 261 us -> 58 us
  Pallas kernels: 0 us -> 198 us
  starting transfers between devices: 1.91 us -> 197 us
  blocking collectives: 68.3 us -> 0 us
  other arithmetic: 125 us -> 166 us
    all_gather x16 -> x0, waiting for transfers between devices: 909 us -> none  [the longest x1 243 us: fetch_experts(): lax.all_gather(expert_gate_up, 'fsdp', axis=1, tiled=True)]
    ppermute x0 -> x92, waiting for transfers between devices: none -> 531 us  [the longest x13 180 us: swap_y(): return lax.ppermute(a, 'fsdp', [(0, 1), (1, 0)])]
    reduce_scatter x9 -> x0, waiting for transfers between devices: 403 us -> none  [the longest x1 149 us: shards(): lax.psum_scatter(reordered[3].astype(jnp.bfloat16), ('rep', 'fsdp'), scat...]
    convert_element_type x15 -> x5, local copies, waits for them, and re-layouts: 265 us -> 11.4 us  [the longest x1 11.2 us: shards(): jnp.transpose(shared_up_out, (3, 1, 0, 2)).reshape(shard, 2, 4 * hidden)]
    dot_general x27 -> x13, matrix products: 256 us -> 44.4 us  [the longest x1 8.02 us: shards(): jnp.einsum('ld,cde->cle', normed, qkv_all, preferred_element_type=F32)]
    pallas_call x0 -> x7, Pallas kernels: none -> 198 us  [the longest x3 169 us: experts_call(): pl.pallas_call(functools.partial(experts_kernel, rows, width, own_width,...]
    ppermute x0 -> x92, starting transfers between devices: none -> 197 us  [the longest x12 75.1 us: scatter_rows(): lax.ppermute(to_right.astype(BF16), 'tensor', [(i, i + 1) for i in range(...]
    gather x12 -> x0, local copies, waits for them, and re-layouts: 163 us -> none  [the longest x2 51.8 us: shards(): picked = expert_out[target]]
  transfers between devices with their start and end apart: 28 -> 92, of which waited for: 23 -> 37; matrix products, arithmetic and copies ran while one was open for 25% -> 21% of each run, Pallas kernels for 0% -> 9%
where the time goes in v1:
time: 1290 us; the launch traced here: 1280 us
  waiting for transfers between devices  531 us (41%)
  Pallas kernels  198 us (15%)
  starting transfers between devices  197 us (15%)
  other arithmetic  166 us (13%)
  local copies, waits for them, and re-layouts  128 us (10%)
  matrix products  58 us (4%)
    ppermute x13, waiting for transfers between devices, swap_y(): return lax.ppermute(a, 'fsdp', [(0, 1), (1, 0)])  180 us
    pallas_call x3, Pallas kernels, experts_call(): pl.pallas_call(functools.partial(experts_kernel, rows, width, own_width,...  169 us
    ppermute x10, waiting for transfers between devices, swap_x(): return lax.ppermute(a, 'rep', [(i, i ^ 2) for i in range(n)])  161 us
    ppermute x12, waiting for transfers between devices, scatter_rows(): lax.ppermute(to_right.astype(BF16), 'tensor', [(i, i + 1) for i in range(...  75.2 us
    ppermute x12, starting transfers between devices, scatter_rows(): lax.ppermute(to_right.astype(BF16), 'tensor', [(i, i + 1) for i in range(...  75.1 us
    unnamed x161, local copies, waits for them, and re-layouts  61 us
    ppermute x12, starting transfers between devices, gather_rows(): lax.ppermute(right[-1], 'tensor', [(i, i + 1) for i in range(n - 1)])  57.3 us
    ppermute x12, waiting for transfers between devices, scatter_rows(): lax.ppermute(to_left.astype(BF16), 'tensor', [(i, i - 1) for i in range(1...  45.8 us
  transfers between devices with their start and end apart: 92, of which 37 were waited for; matrix products, arithmetic and copies ran while one was open for 21% of the time, Pallas kernels for 9%

profile of v1, /device:TPU:0, one launch (start us, length us, event | category | flops | bytes accessed | tf_op | source)
XLA Modules:
  0.0 1280.5 jit_solution(10556476187976426145)
XLA Ops:
  22.5 5.4 collective-permute-start.3
  32.3 7.4 collective-permute-done.3
  49.8 6.3 collective-permute-done
  80.6 8.0 add_bitcast_fusion
  105.2 7.5 fusion.94
  125.0 10.0 collective-permute-done.11
  141.5 9.2 collective-permute-done.12
  173.4 7.4 collective-permute-done.16
  188.5 7.9 collective-permute-start.24
  200.4 6.9 collective-permute-done.18
  208.6 9.1 constant_dynamic-slice_fusion.11
  230.3 6.0 collective-permute-start.28
  255.7 5.4 collective-permute-start.29
  269.3 20.7 %collective-permute-done.22 = bf16[160,2048]{1,0:T(8,128)(2,1)S(1)} collective-permute-done((bf16[160,2048]{1,0:T(8,128)(2,1)}, bf16[160,2048]{1,0:T(8,128)(2,1)S(1)}, u32[]{:S(2)}, u32[]{:S(2)}) %collective-permute-start.22) | collective-permute-done | bytes 655392 | tf_op jit(solution)/shard_map/ppermute | solution.py:75
  302.5 40.3 %collective-permute-done.33 = bf16[1,3,352,1024]{3,2,1,0:T(8,128)(2,1)} collective-permute-done((bf16[1,3,352,1024]{3,2,1,0:T(8,128)(2,1)S(1)}, bf16[1,3,352,1024]{3,2,1,0:T(8,128)(2,1)}, u32[]{:S(2)}, u32[]{:S(2)}) %collective-permute-start.33) | collective-permute-done | bytes 2162720 | tf_op jit(solution)/shard_map/ppermute | solution.py:56
  350.3 56.4 %experts.3 = (bf16[2,3,352,1024]{3,2,1,0:T(8,128)(2,1)}, bf16[2,3,352,1024]{3,2,1,0:T(8,128)(2,1)}, bf16[640,2048]{1,0:T(8,128)(2,1)}, bf16[640,2048]{1,0:T(8,12...) custom-call(bf16[640,2048]{1,0:T(8,128)(2,1)} %select_dynamic-update-slice_fusion.6.x0, ...), custom_call_target="tpu_custom_call" | custom-call | flops 33218887680 | bytes 32505856 | tf_op jit(solution)/shard_map/experts/pallas_call | solution.py:298
  407.4 56.4 %experts.5 = (bf16[2,3,352,1024]{3,2,1,0:T(8,128)(2,1)}, bf16[2,3,352,1024]{3,2,1,0:T(8,128)(2,1)}, bf16[640,2048]{1,0:T(8,128)(2,1)}, bf16[640,2048]{1,0:T(8,12...) custom-call(bf16[640,2048]{1,0:T(8,128)(2,1)} %select_dynamic-update-slice_fusion.6.x0, ...), custom_call_target="tpu_custom_call" | custom-call | flops 33218887680 | bytes 32505856 | tf_op jit(solution)/shard_map/experts/pallas_call | solution.py:298
  469.4 56.3 %experts.4 = (bf16[2,3,352,1024]{3,2,1,0:T(8,128)(2,1)}, bf16[2,3,352,1024]{3,2,1,0:T(8,128)(2,1)}, bf16[640,2048]{1,0:T(8,128)(2,1)}, bf16[640,2048]{1,0:T(8,12...) custom-call(bf16[640,2048]{1,0:T(8,128)(2,1)} %select_dynamic-update-slice_fusion.6.x0, ...), custom_call_target="tpu_custom_call" | custom-call | flops 33218887680 | bytes 32505856 | tf_op jit(solution)/shard_map/experts/pallas_call | solution.py:298
  552.3 13.5 %collective-permute-done.37 = bf16[160,2048]{1,0:T(8,128)(2,1)S(1)} collective-permute-done((bf16[160,2048]{1,0:T(8,128)(2,1)S(1)}, bf16[160,2048]{1,0:T(8,128)(2,1)S(1)}, u32[]{:S(2)}, u32[]{:S(2)}) %collective-permute-start.37) | collective-permute-done | bytes 655392 | tf_op jit(solution)/shard_map/ppermute | solution.py:99
  570.4 13.4 %collective-permute-done.38 = bf16[160,2048]{1,0:T(8,128)(2,1)S(1)} collective-permute-done((bf16[160,2048]{1,0:T(8,128)(2,1)S(1)}, bf16[160,2048]{1,0:T(8,128)(2,1)S(1)}, u32[]{:S(2)}, u32[]{:S(2)}) %collective-permute-start.38) | collective-permute-done | bytes 655392 | tf_op jit(solution)/shard_map/ppermute | solution.py:99
  592.7 10.5 collective-permute-done.39
  603.3 15.2 %collective-permute-done.42 = bf16[160,2048]{1,0:T(8,128)(2,1)S(1)} collective-permute-done((bf16[160,2048]{1,0:T(8,128)(2,1)S(1)}, bf16[160,2048]{1,0:T(8,128)(2,1)S(1)}, u32[]{:S(2)}, u32[]{:S(2)}) %collective-permute-start.42) | collective-permute-done | bytes 655392 | tf_op jit(solution)/shard_map/ppermute | solution.py:102
  632.5 6.5 collective-permute-done.44
  641.3 39.1 %collective-permute-done.67 = f32[10,1024]{1,0:T(8,128)S(1)} collective-permute-done((f32[10,1024]{1,0:T(8,128)S(1)}, f32[10,1024]{1,0:T(8,128)S(1)}, u32[]{:S(2)}, u32[]{:S(2)}) %collective-permute-start.67) | collective-permute-done | bytes 40992 | tf_op jit(solution)/shard_map/ppermute | solution.py:56
  688.2 6.9 add_convert_fusion.9
  699.1 6.6 add_convert_fusion.5
  711.2 12.4 collective-permute-done.48
  753.6 7.5 bitcast_convert_fusion
  766.9 7.3 convolution_convert_fusion
  779.3 90.2 %collective-permute-done.76 = f32[3,512]{1,0:T(4,128)S(1)} collective-permute-done((f32[3,512]{1,0:T(4,128)S(1)}, f32[3,512]{1,0:T(4,128)S(1)}, u32[]{:S(2)}, u32[]{:S(2)}) %collective-permute-start.76) | collective-permute-done | bytes 6176 | tf_op jit(solution)/shard_map/ppermute | solution.py:56
  879.8 9.3 collective-permute-done.57
  891.0 6.4 add_convert_fusion.1
  900.8 92.6 %collective-permute-done.78 = f32[3,512]{1,0:T(4,128)S(1)} collective-permute-done((f32[3,512]{1,0:T(4,128)S(1)}, f32[3,512]{1,0:T(4,128)S(1)}, u32[]{:S(2)}, u32[]{:S(2)}) %collective-permute-start.78) | collective-permute-done | bytes 6176 | tf_op jit(solution)/shard_map/ppermute | solution.py:61
  994.3 7.5 collective-permute-start.58
  1001.8 12.0 add_convert_fusion.2
  1022.3 13.1 %collective-permute-done.61 = bf16[160,2048]{1,0:T(8,128)(2,1)} collective-permute-done((bf16[160,2048]{1,0:T(8,128)(2,1)}, bf16[160,2048]{1,0:T(8,128)(2,1)}, u32[]{:S(2)}, u32[]{:S(2)}) %collective-permute-start.61) | collective-permute-done | bytes 655392 | tf_op jit(solution)/shard_map/ppermute | solution.py:102
  1056.7 5.8 add_convert_fusion.refs_0_
  1062.5 60.3 %collective-permute-done.64 = f32[1,1024]{1,0:T(1,128)S(1)} collective-permute-done((f32[1,1024]{1,0:T(1,128)S(1)}, f32[1,1024]{1,0:T(1,128)S(1)}, u32[]{:S(2)}, u32[]{:S(2)}) %collective-permute-start.64) | collective-permute-done | bytes 4128 | tf_op jit(solution)/shard_map/ppermute | solution.py:61
  1134.9 8.0 add_convert_fusion.3.refs_0_
  1151.6 20.5 %collective-permute-start.52 = (bf16[160,2048]{1,0:T(8,128)(2,1)S(1)}, bf16[160,2048]{1,0:T(8,128)(2,1)S(1)}, u32[]{:S(2)}, u32[]{:S(2)}) collective-permute-start(bf16[160,2048]{1,0:T(8,128)(2,1)S(1)} %get-tuple-element.150), channel_id=1, source_target_pairs={{0,1},{1,2},{2,3},{4,5},{5,6},{6,7},{8,9},{9,10},{10,11},{12,13},{... | collective-permute-start | bytes 1966088 | tf_op jit(solution)/shard_map/ppermute | solution.py:99
  1172.4 7.9 collective-permute-done.74
  1188.4 10.1 collective-permute-done.55
  1202.1 5.8 convert_bitcast_fusion
  1207.9 11.2 copy.134
  1219.1 17.6 %copy.136 = f32[1024,2,1408]{2,1,0:T(2,128)} copy(f32[1024,2,1408]{0,2,1:T(8,128)} %bitcast.95) | data formatting | bytes 23068672
  1249.3 6.6 copy.135
  1255.9 14.6 %place.4 = f32[8,2,352,1024]{3,2,1,0:T(8,128)} custom-call(s32[5,8]{1,0:T(8,128)S(1)} %stack.8.table, bf16[2,3,352,1024]{3,2,1,0:T(8,128)(2,1)} %add_convert_fusion.3.refs_0_, bf16[2,3,352,1024]{3,2,1,0:T(8,128)(2,1)} %get-tuple-element.117.refs_1_, bf16[2,3,352,1024]{3,2,1,0:T(8,128)(2,1)} %collective-permute-done.87.refs_2_, ...), custom_call_target="tpu_custom_call" | custom-call | tf_op jit(solution)/shard_map/place/pallas_call | solution.py:350
  1270.5 9.7 place.5
  (491 shorter events, 403.0 us)
Async XLA Ops:
  20.5 35.6 %collective-permute-start = (bf16[3,1024,256]{1,2,0:T(8,128)(2,1)}, bf16[3,1024,256]{1,2,0:T(8,128)(2,1)S(1)}, u32[]{:S(2)}, u32[]{:S(2)}) collective-permute-start(bf16[3,1024,256]{1,2,0:T(8,128)(2,1)} %constant_dynamic-slice_fusion.17), channel_id=1, source_target_pairs={{0,4},{4,0},{1,5},{5,1},{2,6},{6,2},{3,7},{7,3},{8,12},{12,8},{9,1... | collective-permute-start | bytes 4718600 | tf_op jit(solution)/shard_map/ppermute | solution.py:56
  171.7 121.6 %collective-permute-start.32 = (bf16[2,3,352,1024]{3,2,1,0:T(8,128)(2,1)}, bf16[2,3,352,1024]{3,2,1,0:T(8,128)(2,1)}, u32[]{:S(2)}, u32[]{:S(2)}) collective-permute-start(bf16[2,3,352,1024]{3,2,1,0:T(8,128)(2,1)} %pad_maximum_fusion.2.w_own), channel_id=1, source_target_pairs={{0,4},{4,0},{1,5},{5,1},{2,6},{6,2},{3,7},{7,3},{8,12},{12,8},{9,1... | collective-permute-start | bytes 12976136 | tf_op jit(solution)/shard_map/ppermute | solution.py:56
  185.5 21.8 %collective-permute-start.18 = (bf16[160,2048]{1,0:T(8,128)(2,1)}, bf16[160,2048]{1,0:T(8,128)(2,1)}, u32[]{:S(2)}, u32[]{:S(2)}) collective-permute-start(bf16[160,2048]{1,0:T(8,128)(2,1)} %get-tuple-element.125), channel_id=1, source_target_pairs={{1,0},{2,1},{3,2},{5,4},{6,5},{7,6},{9,8},{10,9},{11,10},{13,12},{... | collective-permute-start | bytes 1966088 | tf_op jit(solution)/shard_map/ppermute | solution.py:76
  187.2 41.8 %collective-permute-start.25 = (bf16[160,2048]{1,0:T(8,128)(2,1)S(1)}, bf16[160,2048]{1,0:T(8,128)(2,1)}, u32[]{:S(2)}, u32[]{:S(2)}) collective-permute-start(bf16[160,2048]{1,0:T(8,128)(2,1)S(1)} %fusion.44), channel_id=1, source_target_pairs={{1,0},{2,1},{3,2},{5,4},{6,5},{7,6},{9,8},{10,9},{11,10},{13,12},{... | collective-permute-start | bytes 1966088 | tf_op jit(solution)/shard_map/ppermute | solution.py:76
  188.5 41.8 %collective-permute-start.24 = (bf16[160,2048]{1,0:T(8,128)(2,1)S(1)}, bf16[160,2048]{1,0:T(8,128)(2,1)}, u32[]{:S(2)}, u32[]{:S(2)}) collective-permute-start(bf16[160,2048]{1,0:T(8,128)(2,1)S(1)} %fusion.44), channel_id=1, source_target_pairs={{0,1},{1,2},{2,3},{4,5},{5,6},{6,7},{8,9},{9,10},{10,11},{12,13},{... | collective-permute-start | bytes 1966088 | tf_op jit(solution)/shard_map/ppermute | solution.py:75
  196.4 39.9 %collective-permute-start.17 = (bf16[160,2048]{1,0:T(8,128)(2,1)}, bf16[160,2048]{1,0:T(8,128)(2,1)}, u32[]{:S(2)}, u32[]{:S(2)}) collective-permute-start(bf16[160,2048]{1,0:T(8,128)(2,1)} %get-tuple-element.125), channel_id=1, source_target_pairs={{0,1},{1,2},{2,3},{4,5},{5,6},{6,7},{8,9},{9,10},{10,11},{12,13},{... | collective-permute-start | bytes 1966088 | tf_op jit(solution)/shard_map/ppermute | solution.py:75
  207.3 32.9 %collective-permute-start.19 = (bf16[160,2048]{1,0:T(8,128)(2,1)}, bf16[160,2048]{1,0:T(8,128)(2,1)}, u32[]{:S(2)}, u32[]{:S(2)}) collective-permute-start(bf16[160,2048]{1,0:T(8,128)(2,1)} %collective-permute-done.18), channel_id=1, source_target_pairs={{1,0},{2,1},{3,2},{5,4},{6,5},{7,6},{9,8},{10,9},{11,10},{13,12},{... | collective-permute-start | bytes 1966088 | tf_op jit(solution)/shard_map/ppermute | solution.py:76
  229.0 25.4 %collective-permute-start.26 = (bf16[160,2048]{1,0:T(8,128)(2,1)}, bf16[160,2048]{1,0:T(8,128)(2,1)}, u32[]{:S(2)}, u32[]{:S(2)}) collective-permute-start(bf16[160,2048]{1,0:T(8,128)(2,1)} %collective-permute-done.25), channel_id=1, source_target_pairs={{1,0},{2,1},{3,2},{5,4},{6,5},{7,6},{9,8},{10,9},{11,10},{13,12},{... | collective-permute-start | bytes 1966088 | tf_op jit(solution)/shard_map/ppermute | solution.py:76
  230.3 24.1 %collective-permute-start.28 = (bf16[160,2048]{1,0:T(8,128)(2,1)}, bf16[160,2048]{1,0:T(8,128)(2,1)}, u32[]{:S(2)}, u32[]{:S(2)}) collective-permute-start(bf16[160,2048]{1,0:T(8,128)(2,1)} %collective-permute-done.24), channel_id=1, source_target_pairs={{0,1},{1,2},{2,3},{4,5},{5,6},{6,7},{8,9},{9,10},{10,11},{12,13},{... | collective-permute-start | bytes 1966088 | tf_op jit(solution)/shard_map/ppermute | solution.py:75
  254.4 44.2 %collective-permute-start.31 = (s32[640,4]{0,1:T(4,128)S(1)}, s32[640,4]{0,1:T(4,128)S(1)}, u32[]{:S(2)}, u32[]{:S(2)}) collective-permute-start(s32[640,4]{0,1:T(4,128)S(1)} %copy-done.64), channel_id=1, source_target_pairs={{0,8},{8,0},{16,24},{24,16},{1,9},{9,1},{17,25},{25,17},{2,10},{10... | collective-permute-start | bytes 30728 | tf_op jit(solution)/shard_map/ppermute | solution.py:66
  254.4 37.8 %collective-permute-start.27 = (bf16[160,2048]{1,0:T(8,128)(2,1)}, bf16[160,2048]{1,0:T(8,128)(2,1)S(1)}, u32[]{:S(2)}, u32[]{:S(2)}) collective-permute-start(bf16[160,2048]{1,0:T(8,128)(2,1)} %collective-permute-done.26), channel_id=1, source_target_pairs={{1,0},{2,1},{3,2},{5,4},{6,5},{7,6},{9,8},{10,9},{11,10},{13,12},{... | collective-permute-start | bytes 1966088 | tf_op jit(solution)/shard_map/ppermute | solution.py:76
  255.7 40.5 %collective-permute-start.29 = (bf16[160,2048]{1,0:T(8,128)(2,1)}, bf16[160,2048]{1,0:T(8,128)(2,1)S(1)}, u32[]{:S(2)}, u32[]{:S(2)}) collective-permute-start(bf16[160,2048]{1,0:T(8,128)(2,1)} %collective-permute-done.28), channel_id=1, source_target_pairs={{0,1},{1,2},{2,3},{4,5},{5,6},{6,7},{8,9},{9,10},{10,11},{12,13},{... | collective-permute-start | bytes 1966088 | tf_op jit(solution)/shard_map/ppermute | solution.py:75
  261.1 28.9 %collective-permute-start.22 = (bf16[160,2048]{1,0:T(8,128)(2,1)}, bf16[160,2048]{1,0:T(8,128)(2,1)S(1)}, u32[]{:S(2)}, u32[]{:S(2)}) collective-permute-start(bf16[160,2048]{1,0:T(8,128)(2,1)} %collective-permute-done.21), channel_id=1, source_target_pairs={{0,1},{1,2},{2,3},{4,5},{5,6},{6,7},{8,9},{9,10},{10,11},{12,13},{... | collective-permute-start | bytes 1966088 | tf_op jit(solution)/shard_map/ppermute | solution.py:75
  292.2 52.6 %collective-permute-start.23 = (bf16[640,2048]{1,0:T(8,128)(2,1)}, bf16[640,2048]{1,0:T(8,128)(2,1)}, u32[]{:S(2)}, u32[]{:S(2)}) collective-permute-start(bf16[640,2048]{1,0:T(8,128)(2,1)} %select_dynamic-update-slice_fusion.6.x0), channel_id=1, source_target_pairs={{0,8},{8,0},{16,24},{24,16},{1,9},{9,1},{17,25},{25,17},{2,10},{10... | collective-permute-start | bytes 7864328 | tf_op jit(solution)/shard_map/ppermute | solution.py:66
  293.3 49.5 %collective-permute-start.33 = (bf16[1,3,352,1024]{3,2,1,0:T(8,128)(2,1)S(1)}, bf16[1,3,352,1024]{3,2,1,0:T(8,128)(2,1)}, u32[]{:S(2)}, u32[]{:S(2)}) collective-permute-start(bf16[1,3,352,1024]{3,2,1,0:T(8,128)(2,1)S(1)} %maximum_bitcast_fusion), channel_id=1, source_target_pairs={{0,4},{4,0},{1,5},{5,1},{2,6},{6,2},{3,7},{7,3},{8,12},{12,8},{9,1... | collective-permute-start | bytes 6488072 | tf_op jit(solution)/shard_map/ppermute | solution.py:56
  298.3 51.9 %collective-permute-start.30 = (bf16[640,2048]{1,0:T(8,128)(2,1)}, bf16[640,2048]{1,0:T(8,128)(2,1)}, u32[]{:S(2)}, u32[]{:S(2)}) collective-permute-start(bf16[640,2048]{1,0:T(8,128)(2,1)} %select_dynamic-update-slice_fusion.3.c0), channel_id=1, source_target_pairs={{0,8},{8,0},{16,24},{24,16},{1,9},{9,1},{17,25},{25,17},{2,10},{10... | collective-permute-start | bytes 7864328 | tf_op jit(solution)/shard_map/ppermute | solution.py:66
  300.2 107.2 %collective-permute-start.35 = (bf16[2,3,352,1024]{3,2,1,0:T(8,128)(2,1)}, bf16[2,3,352,1024]{3,2,1,0:T(8,128)(2,1)}, u32[]{:S(2)}, u32[]{:S(2)}) collective-permute-start(bf16[2,3,352,1024]{3,2,1,0:T(8,128)(2,1)} %collective-permute-done.32.w_oth), channel_id=1, source_target_pairs={{0,16},{8,24},{16,0},{24,8},{1,17},{9,25},{17,1},{25,9},{2,18},{10... | collective-permute-start | bytes 12976136 | tf_op jit(solution)/shard_map/ppermute | solution.py:61
  342.9 121.8 %collective-permute-start.34 = (bf16[1,3,352,1024]{3,2,1,0:T(8,128)(2,1)}, bf16[1,3,352,1024]{3,2,1,0:T(8,128)(2,1)S(1)}, u32[]{:S(2)}, u32[]{:S(2)}) collective-permute-start(bf16[1,3,352,1024]{3,2,1,0:T(8,128)(2,1)} %collective-permute-done.33), channel_id=1, source_target_pairs={{0,16},{8,24},{16,0},{24,8},{1,17},{9,25},{17,1},{25,9},{2,18},{10... | collective-permute-start | bytes 6488072 | tf_op jit(solution)/shard_map/ppermute | solution.py:61
  585.0 111.0 %collective-permute-start.83 = (bf16[2,3,352,1024]{3,2,1,0:T(8,128)(2,1)}, bf16[2,3,352,1024]{3,2,1,0:T(8,128)(2,1)}, u32[]{:S(2)}, u32[]{:S(2)}) collective-permute-start(bf16[2,3,352,1024]{3,2,1,0:T(8,128)(2,1)} %get-tuple-element.60), channel_id=1, source_target_pairs={{0,4},{4,0},{1,5},{5,1},{2,6},{6,2},{3,7},{7,3},{8,12},{12,8},{9,1... | collective-permute-start | bytes 12976136 | tf_op jit(solution)/shard_map/ppermute | solution.py:56
  591.3 27.1 %collective-permute-start.42 = (bf16[160,2048]{1,0:T(8,128)(2,1)S(1)}, bf16[160,2048]{1,0:T(8,128)(2,1)S(1)}, u32[]{:S(2)}, u32[]{:S(2)}) collective-permute-start(bf16[160,2048]{1,0:T(8,128)(2,1)S(1)} %add_convert_fusion.24), channel_id=1, source_target_pairs={{1,0},{2,1},{3,2},{5,4},{6,5},{7,6},{9,8},{10,9},{11,10},{13,12},{... | collective-permute-start | bytes 1966088 | tf_op jit(solution)/shard_map/ppermute | solution.py:102
  627.9 53.9 %collective-permute-start.43 = (bf16[160,2048]{1,0:T(8,128)(2,1)}, bf16[160,2048]{1,0:T(8,128)(2,1)S(1)}, u32[]{:S(2)}, u32[]{:S(2)}) collective-permute-start(bf16[160,2048]{1,0:T(8,128)(2,1)} %get-tuple-element.120), channel_id=1, source_target_pairs={{0,1},{1,2},{2,3},{4,5},{5,6},{6,7},{8,9},{9,10},{10,11},{12,13},{... | collective-permute-start | bytes 1966088 | tf_op jit(solution)/shard_map/ppermute | solution.py:75
  638.9 47.9 %collective-permute-start.45 = (bf16[160,2048]{1,0:T(8,128)(2,1)S(1)}, bf16[160,2048]{1,0:T(8,128)(2,1)S(1)}, u32[]{:S(2)}, u32[]{:S(2)}) collective-permute-start(bf16[160,2048]{1,0:T(8,128)(2,1)S(1)} %collective-permute-done.44), channel_id=1, source_target_pairs={{1,0},{2,1},{3,2},{5,4},{6,5},{7,6},{9,8},{10,9},{11,10},{13,12},{... | collective-permute-start | bytes 1966088 | tf_op jit(solution)/shard_map/ppermute | solution.py:76
  640.3 40.1 %collective-permute-start.67 = (f32[10,1024]{1,0:T(8,128)S(1)}, f32[10,1024]{1,0:T(8,128)S(1)}, u32[]{:S(2)}, u32[]{:S(2)}) collective-permute-start(f32[10,1024]{1,0:T(8,128)S(1)} %pad_maximum_fusion.29), channel_id=1, source_target_pairs={{0,4},{4,0},{1,5},{5,1},{2,6},{6,2},{3,7},{7,3},{8,12},{12,8},{9,1... | collective-permute-start | bytes 122888 | tf_op jit(solution)/shard_map/ppermute | solution.py:56
  680.5 216.9 %collective-permute-start.84 = (bf16[2,3,352,1024]{3,2,1,0:T(8,128)(2,1)}, bf16[2,3,352,1024]{3,2,1,0:T(8,128)(2,1)}, u32[]{:S(2)}, u32[]{:S(2)}) collective-permute-start(bf16[2,3,352,1024]{3,2,1,0:T(8,128)(2,1)} %get-tuple-element.62), channel_id=1, source_target_pairs={{0,4},{4,0},{1,5},{5,1},{2,6},{6,2},{3,7},{7,3},{8,12},{12,8},{9,1... | collective-permute-start | bytes 12976136 | tf_op jit(solution)/shard_map/ppermute | solution.py:56
  681.8 27.2 %collective-permute-start.47 = (bf16[160,2048]{1,0:T(8,128)(2,1)S(1)}, bf16[160,2048]{1,0:T(8,128)(2,1)S(1)}, u32[]{:S(2)}, u32[]{:S(2)}) collective-permute-start(bf16[160,2048]{1,0:T(8,128)(2,1)S(1)} %collective-permute-done.43), channel_id=1, source_target_pairs={{0,1},{1,2},{2,3},{4,5},{5,6},{6,7},{8,9},{9,10},{10,11},{12,13},{... | collective-permute-start | bytes 1966088 | tf_op jit(solution)/shard_map/ppermute | solution.py:75
  686.9 23.8 %collective-permute-start.46 = (bf16[160,2048]{1,0:T(8,128)(2,1)S(1)}, bf16[160,2048]{1,0:T(8,128)(2,1)S(1)}, u32[]{:S(2)}, u32[]{:S(2)}) collective-permute-start(bf16[160,2048]{1,0:T(8,128)(2,1)S(1)} %collective-permute-done.45), channel_id=1, source_target_pairs={{1,0},{2,1},{3,2},{5,4},{6,5},{7,6},{9,8},{10,9},{11,10},{13,12},{... | collective-permute-start | bytes 1966088 | tf_op jit(solution)/shard_map/ppermute | solution.py:76
  695.1 183.5 %collective-permute-start.89 = (bf16[2,3,352,1024]{3,2,1,0:T(8,128)(2,1)}, bf16[2,3,352,1024]{3,2,1,0:T(8,128)(2,1)}, u32[]{:S(2)}, u32[]{:S(2)}) collective-permute-start(bf16[2,3,352,1024]{3,2,1,0:T(8,128)(2,1)} %get-tuple-element.64), channel_id=1, source_target_pairs={{0,4},{4,0},{1,5},{5,1},{2,6},{6,2},{3,7},{7,3},{8,12},{12,8},{9,1... | collective-permute-start | bytes 12976136 | tf_op jit(solution)/shard_map/ppermute | solution.py:56
  707.3 286.1 %collective-permute-start.86 = (bf16[2,3,352,1024]{3,2,1,0:T(8,128)(2,1)}, bf16[2,3,352,1024]{3,2,1,0:T(8,128)(2,1)}, u32[]{:S(2)}, u32[]{:S(2)}) collective-permute-start(bf16[2,3,352,1024]{3,2,1,0:T(8,128)(2,1)} %add_convert_fusion.5), channel_id=1, source_target_pairs={{0,16},{8,24},{16,0},{24,8},{1,17},{9,25},{17,1},{25,9},{2,18},{10... | collective-permute-start | bytes 12976136 | tf_op jit(solution)/shard_map/ppermute | solution.py:61
  765.9 113.9 %collective-permute-start.59 = (bf16[160,2048]{1,0:T(8,128)(2,1)S(1)}, bf16[160,2048]{1,0:T(8,128)(2,1)S(1)}, u32[]{:S(2)}, u32[]{:S(2)}) collective-permute-start(bf16[160,2048]{1,0:T(8,128)(2,1)S(1)} %get-tuple-element.149), channel_id=1, source_target_pairs={{3,2},{7,6},{11,10},{15,14},{19,18},{23,22},{27,26},{31,30}} | collective-permute-start | bytes 1966088 | tf_op jit(solution)/shard_map/ppermute | solution.py:102
  778.1 91.4 %collective-permute-start.76 = (f32[3,512]{1,0:T(4,128)S(1)}, f32[3,512]{1,0:T(4,128)S(1)}, u32[]{:S(2)}, u32[]{:S(2)}) collective-permute-start(f32[3,512]{1,0:T(4,128)S(1)} %convert_reduce_fusion), channel_id=1, source_target_pairs={{0,4},{4,0},{1,5},{5,1},{2,6},{6,2},{3,7},{7,3},{8,12},{12,8},{9,1... | collective-permute-start | bytes 18440 | tf_op jit(solution)/shard_map/ppermute | solution.py:56
  889.8 149.5 %collective-permute-start.72 = (bf16[3,2048,256]{1,2,0:T(8,128)(2,1)}, bf16[3,2048,256]{1,2,0:T(8,128)(2,1)}, u32[]{:S(2)}, u32[]{:S(2)}) collective-permute-start(bf16[3,2048,256]{1,2,0:T(8,128)(2,1)} %dynamic-slice_bitcast_fusion), channel_id=1, source_target_pairs={{0,8},{8,0},{16,24},{24,16},{1,9},{9,1},{17,25},{25,17},{2,10},{10... | collective-permute-start | bytes 9437192 | tf_op jit(solution)/shard_map/ppermute | solution.py:66
  890.3 104.1 %collective-permute-start.60 = (bf16[160,2048]{1,0:T(8,128)(2,1)S(1)}, bf16[160,2048]{1,0:T(8,128)(2,1)S(1)}, u32[]{:S(2)}, u32[]{:S(2)}) collective-permute-start(bf16[160,2048]{1,0:T(8,128)(2,1)S(1)} %get-tuple-element.147), channel_id=1, source_target_pairs={{2,1},{3,2},{6,5},{7,6},{10,9},{11,10},{14,13},{15,14},{18,17},{19... | collective-permute-start | bytes 1966088 | tf_op jit(solution)/shard_map/ppermute | solution.py:102
  897.4 158.9 %collective-permute-start.90 = (bf16[2,3,352,1024]{3,2,1,0:T(8,128)(2,1)}, bf16[2,3,352,1024]{3,2,1,0:T(8,128)(2,1)}, u32[]{:S(2)}, u32[]{:S(2)}) collective-permute-start(bf16[2,3,352,1024]{3,2,1,0:T(8,128)(2,1)} %add_convert_fusion.1), channel_id=1, source_target_pairs={{0,16},{8,24},{16,0},{24,8},{1,17},{9,25},{17,1},{25,9},{2,18},{10... | collective-permute-start | bytes 12976136 | tf_op jit(solution)/shard_map/ppermute | solution.py:61
  897.5 95.8 %collective-permute-start.78 = (f32[3,512]{1,0:T(4,128)S(1)}, f32[3,512]{1,0:T(4,128)S(1)}, u32[]{:S(2)}, u32[]{:S(2)}) collective-permute-start(f32[3,512]{1,0:T(4,128)S(1)} %add.597), channel_id=1, source_target_pairs={{0,16},{8,24},{16,0},{24,8},{1,17},{9,25},{17,1},{25,9},{2,18},{10... | collective-permute-start | bytes 18440 | tf_op jit(solution)/shard_map/ppermute | solution.py:61
  993.3 52.8 %collective-permute-start.49 = (bf16[640,2048]{1,0:T(8,128)(2,1)}, bf16[640,2048]{1,0:T(8,128)(2,1)}, u32[]{:S(2)}, u32[]{:S(2)}) collective-permute-start(bf16[640,2048]{1,0:T(8,128)(2,1)} %add_convert_fusion.9), channel_id=1, source_target_pairs={{0,8},{8,0},{16,24},{24,16},{1,9},{9,1},{17,25},{25,17},{2,10},{10... | collective-permute-start | bytes 7864328 | tf_op jit(solution)/shard_map/ppermute | solution.py:66
  993.3 22.7 %collective-permute-start.80 = (bf16[256,1024]{1,0:T(8,128)(2,1)}, bf16[256,1024]{1,0:T(8,128)(2,1)S(1)}, u32[]{:S(2)}, u32[]{:S(2)}) collective-permute-start(bf16[256,1024]{1,0:T(8,128)(2,1)} %slice.182), channel_id=1, source_target_pairs={{0,4},{4,0},{1,5},{5,1},{2,6},{6,2},{3,7},{7,3},{8,12},{12,8},{9,1... | collective-permute-start | bytes 1572872 | tf_op jit(solution)/shard_map/ppermute | solution.py:56
  994.3 22.0 %collective-permute-start.58 = (bf16[160,2048]{1,0:T(8,128)(2,1)S(1)}, bf16[160,2048]{1,0:T(8,128)(2,1)}, u32[]{:S(2)}, u32[]{:S(2)}) collective-permute-start(bf16[160,2048]{1,0:T(8,128)(2,1)S(1)} %get-tuple-element.146), channel_id=1, source_target_pairs={{0,1},{1,2},{2,3},{4,5},{5,6},{6,7},{8,9},{9,10},{10,11},{12,13},{... | collective-permute-start | bytes 1966088 | tf_op jit(solution)/shard_map/ppermute | solution.py:99
  1016.0 118.5 %collective-permute-start.85 = (bf16[2,3,352,1024]{3,2,1,0:T(8,128)(2,1)}, bf16[2,3,352,1024]{3,2,1,0:T(8,128)(2,1)}, u32[]{:S(2)}, u32[]{:S(2)}) collective-permute-start(bf16[2,3,352,1024]{3,2,1,0:T(8,128)(2,1)} %get-tuple-element.118), channel_id=1, source_target_pairs={{0,16},{8,24},{16,0},{24,8},{1,17},{9,25},{17,1},{25,9},{2,18},{10... | collective-permute-start | bytes 12976136 | tf_op jit(solution)/shard_map/ppermute | solution.py:61
  1035.4 87.4 %collective-permute-start.81 = (bf16[256,1024]{1,0:T(8,128)(2,1)S(1)}, bf16[256,1024]{1,0:T(8,128)(2,1)S(1)}, u32[]{:S(2)}, u32[]{:S(2)}) collective-permute-start(bf16[256,1024]{1,0:T(8,128)(2,1)S(1)} %add_convert_fusion.35), channel_id=1, source_target_pairs={{0,16},{8,24},{16,0},{24,8},{1,17},{9,25},{17,1},{25,9},{2,18},{10... | collective-permute-start | bytes 1572872 | tf_op jit(solution)/shard_map/ppermute | solution.py:61
  1046.1 82.4 %collective-permute-start.73 = (bf16[3,1024,256]{1,2,0:T(8,128)(2,1)}, bf16[3,1024,256]{1,2,0:T(8,128)(2,1)}, u32[]{:S(2)}, u32[]{:S(2)}) collective-permute-start(bf16[3,1024,256]{1,2,0:T(8,128)(2,1)} %slice.180), channel_id=1, source_target_pairs={{0,4},{4,0},{1,5},{5,1},{2,6},{6,2},{3,7},{7,3},{8,12},{12,8},{9,1... | collective-permute-start | bytes 4718600 | tf_op jit(solution)/shard_map/ppermute | solution.py:56
  1052.4 74.3 %collective-permute-start.50 = (bf16[160,2048]{1,0:T(8,128)(2,1)S(1)}, bf16[160,2048]{1,0:T(8,128)(2,1)S(1)}, u32[]{:S(2)}, u32[]{:S(2)}) collective-permute-start(bf16[160,2048]{1,0:T(8,128)(2,1)S(1)} %get-tuple-element.152), channel_id=1, source_target_pairs={{0,1},{4,5},{8,9},{12,13},{16,17},{20,21},{24,25},{28,29}} | collective-permute-start | bytes 1966088 | tf_op jit(solution)/shard_map/ppermute | solution.py:99
  1056.3 66.5 %collective-permute-start.64 = (f32[1,1024]{1,0:T(1,128)S(1)}, f32[1,1024]{1,0:T(1,128)S(1)}, u32[]{:S(2)}, u32[]{:S(2)}) collective-permute-start(f32[1,1024]{1,0:T(1,128)S(1)} %add.582), channel_id=1, source_target_pairs={{0,16},{8,24},{16,0},{24,8},{1,17},{9,25},{17,1},{25,9},{2,18},{10... | collective-permute-start | bytes 12296 | tf_op jit(solution)/shard_map/ppermute | solution.py:61
  1122.8 133.1 %collective-permute-start.88 = (bf16[2,3,352,1024]{3,2,1,0:T(8,128)(2,1)}, bf16[2,3,352,1024]{3,2,1,0:T(8,128)(2,1)}, u32[]{:S(2)}, u32[]{:S(2)}) collective-permute-start(bf16[2,3,352,1024]{3,2,1,0:T(8,128)(2,1)} %get-tuple-element.117.refs_1_), channel_id=1, source_target_pairs={{0,8},{8,0},{16,24},{24,16},{1,9},{9,1},{17,25},{25,17},{2,10},{10... | collective-permute-start | bytes 12976136 | tf_op jit(solution)/shard_map/ppermute | solution.py:66
  1126.8 73.3 %collective-permute-start.91 = (bf16[2,3,352,1024]{3,2,1,0:T(8,128)(2,1)S(1)}, bf16[2,3,352,1024]{3,2,1,0:T(8,128)(2,1)S(1)}, u32[]{:S(2)}, u32[]{:S(2)}) collective-permute-start(bf16[2,3,352,1024]{3,2,1,0:T(8,128)(2,1)S(1)} %add_convert_fusion.refs_0_), channel_id=1, source_target_pairs={{0,8},{8,0},{16,24},{24,16},{1,9},{9,1},{17,25},{25,17},{2,10},{10... | collective-permute-start | bytes 12976136 | tf_op jit(solution)/shard_map/ppermute | solution.py:66
  1143.7 36.6 %collective-permute-start.74 = (bf16[3,1024,256]{1,2,0:T(8,128)(2,1)S(1)}, bf16[3,1024,256]{1,2,0:T(8,128)(2,1)S(1)}, u32[]{:S(2)}, u32[]{:S(2)}) collective-permute-start(bf16[3,1024,256]{1,2,0:T(8,128)(2,1)S(1)} %add_convert_fusion.11), channel_id=1, source_target_pairs={{0,16},{8,24},{16,0},{24,8},{1,17},{9,25},{17,1},{25,9},{2,18},{10... | collective-permute-start | bytes 4718600 | tf_op jit(solution)/shard_map/ppermute | solution.py:61
  1147.1 108.8 %collective-permute-start.87 = (bf16[2,3,352,1024]{3,2,1,0:T(8,128)(2,1)}, bf16[2,3,352,1024]{3,2,1,0:T(8,128)(2,1)}, u32[]{:S(2)}, u32[]{:S(2)}) collective-permute-start(bf16[2,3,352,1024]{3,2,1,0:T(8,128)(2,1)} %add_convert_fusion.3.refs_0_), channel_id=1, source_target_pairs={{0,8},{8,0},{16,24},{24,16},{1,9},{9,1},{17,25},{25,17},{2,10},{10... | collective-permute-start | bytes 12976136 | tf_op jit(solution)/shard_map/ppermute | solution.py:66
  1151.6 34.4 %collective-permute-start.52 = (bf16[160,2048]{1,0:T(8,128)(2,1)S(1)}, bf16[160,2048]{1,0:T(8,128)(2,1)S(1)}, u32[]{:S(2)}, u32[]{:S(2)}) collective-permute-start(bf16[160,2048]{1,0:T(8,128)(2,1)S(1)} %get-tuple-element.150), channel_id=1, source_target_pairs={{0,1},{1,2},{2,3},{4,5},{5,6},{6,7},{8,9},{9,10},{10,11},{12,13},{... | collective-permute-start | bytes 1966088 | tf_op jit(solution)/shard_map/ppermute | solution.py:99
  1186.0 58.6 %collective-permute-start.75 = (bf16[3,1024,256]{1,2,0:T(8,128)(2,1)S(1)}, bf16[3,1024,256]{1,2,0:T(8,128)(2,1)}, u32[]{:S(2)}, u32[]{:S(2)}) collective-permute-start(bf16[3,1024,256]{1,2,0:T(8,128)(2,1)S(1)} %add_convert_fusion.10), channel_id=1, source_target_pairs={{0,8},{8,0},{16,24},{24,16},{1,9},{9,1},{17,25},{25,17},{2,10},{10... | collective-permute-start | bytes 4718600 | tf_op jit(solution)/shard_map/ppermute | solution.py:66
  (118 other events, 2111.6 us)

commit v2 on v1

--- a/solution.py
+++ b/solution.py
@@ -15,6 +15,7 @@
 BF16 = jnp.bfloat16
 F32 = jnp.float32
 COLS = 256
+MESH = pl.DeviceIdType.MESH
 
 
 def rope_tables(length, head_dim):
@@ -66,43 +67,296 @@
     return lax.ppermute(a, "rep", [(i, i ^ 1) for i in range(n)])
 
 
-def gather_rows(block):
+CHUNK = 32
+
+
+def device(axis, index):
+    return {axis: index}
+
+
+def rows_kernel(n, rows, with_core_in, with_scatter, with_gather, with_core_out, middle, extra_count, extra_out, *refs):
+    refs = list(refs)
+    take = refs.pop
+    part = take(0)
+    part_peer = take(0) if with_core_in else None
+    extras = [take(0) for _ in range(extra_count)]
+    outs = [take(0) for _ in range(extra_out)]
+    full = take(0) if with_gather else None
+    full_peer = take(0) if with_core_out else None
+    chunks = rows // CHUNK
+    z = lax.axis_index("tensor")
+    r = lax.axis_index("rep")
+    core = r + 1 - 2 * lax.rem(r, 2)
+    has_left, has_right = z > 0, z < n - 1
+    pairs = with_core_in or with_core_out
+    if with_core_in:
+        core_buf, core_in_send, core_in_recv = take(0), take(0), take(0)
+    if with_scatter:
+        in_bufs, out_bufs = (take(0), take(0)), (take(0), take(0))
+        sc_send, sc_recv = take(0), take(0)
+    if with_gather:
+        ga_send, ga_recv = take(0), take(0)
+    if with_core_out:
+        core_out_send, core_out_recv = take(0), take(0)
+
+    barrier = pltpu.get_barrier_semaphore()
+
+    @pl.when(has_left)
+    def _():
+        pl.semaphore_signal(barrier, inc=1, device_id=device("tensor", z - 1), device_id_type=MESH)
+
+    @pl.when(has_right)
+    def _():
+        pl.semaphore_signal(barrier, inc=1, device_id=device("tensor", z + 1), device_id_type=MESH)
+
+    if pairs:
+        pl.semaphore_signal(barrier, inc=1, device_id=device("rep", core), device_id_type=MESH)
+    greeted = jnp.where(has_left, 1, 0) + jnp.where(has_right, 1, 0) + (1 if pairs else 0)
+    pl.semaphore_wait(barrier, greeted)
+
+    def chunk_at(block, i):
+        return pl.ds(pl.multiple_of(block * rows + i * CHUNK, CHUNK), CHUNK)
+
+    def chunk_in(i):
+        return pl.ds(pl.multiple_of(i * CHUNK, CHUNK), CHUNK)
+
+    def remote(src, dst, send, recv, axis, index):
+        return pltpu.make_async_remote_copy(
+            src_ref=src, dst_ref=dst, send_sem=send, recv_sem=recv,
+            device_id=device(axis, index), device_id_type=MESH,
+        )
+
+    def core_in_copy(block, i):
+        here = chunk_at(block, i)
+        return remote(
+            part_peer.at[here], core_buf.at[here], core_in_send.at[block, i], core_in_recv.at[block, i], "rep", core
+        )
+
+    def scatter_copy(way, m, i):
+        here = chunk_in(i)
+        return remote(
+            out_bufs[way].at[m, here], in_bufs[way].at[m, here], sc_send.at[way, m, i], sc_recv.at[way, m, i],
+            "tensor", z + 1 - 2 * way,
+        )
+
+    def gather_copy(way, k, i):
+        here = chunk_at(z - k + 2 * k * way, i)
+        return remote(
+            full.at[here], full.at[here], ga_send.at[way, k, i], ga_recv.at[way, k, i], "tensor", z + 1 - 2 * way
+        )
+
+    def core_out_copy(block, i):
+        here = chunk_at(block, i)
+        return remote(
+            full.at[here], full_peer.at[here], core_out_send.at[block, i], core_out_recv.at[block, i], "rep", core
+        )
+
+    def all_chunks(body):
+        def step(i, carry):
+            body(i)
+            return carry
+
+        lax.fori_loop(0, chunks, step, 0)
+
+    if with_core_in:
+
+        @all_chunks
+        def _(i):
+            for block in range(n):
+                core_in_copy(block, i).start()
+
+    def term(block, i):
+        here = chunk_at(block, i)
+        value = part[here, :].astype(F32)
+        if with_core_in:
+            core_in_copy(block, i).wait_recv()
+            value = value + core_buf[here, :].astype(F32)
+        return value
+
+    def inside(i):
+        return (i >= 0) & (i < chunks)
+
+    def scatter_step(way, i, has_source, does_send):
+        for m in range(n - 1):
+            block = n - 1 - m if way == 0 else m
+            here = chunk_in(i)
+
+            @pl.when(inside(i) & does_send(block))
+            def _():
+                value = term(block, i)
+
+                @pl.when(has_source)
+                def _():
+                    scatter_copy(way, m, i).wait_recv()
+                    out_bufs[way][m, here, :] = (value + in_bufs[way][m, here, :].astype(F32)).astype(BF16)
+
+                @pl.when(jnp.logical_not(has_source))
+                def _():
+                    out_bufs[way][m, here, :] = value.astype(BF16)
+
+                scatter_copy(way, m, i).start()
+
+    def own_step(i):
+        @pl.when(inside(i))
+        def _():
+            here = chunk_in(i)
+            if with_scatter:
+                total[...] = term(z, i)
+
+                @pl.when(has_left)
+                def _():
+                    m = n - 1 - z
+                    scatter_copy(0, m, i).wait_recv()
+                    total[...] += in_bufs[0][m, here, :].astype(F32)
+
+                @pl.when(has_right)
+                def _():
+                    scatter_copy(1, z, i).wait_recv()
+                    total[...] += in_bufs[1][z, here, :].astype(F32)
+
+                sent = middle(total[...], here, extras, outs)
+            else:
+                sent = part[here, :]
+            if with_gather:
+                full[chunk_at(z, i), :] = sent
+
+                @pl.when(has_right)
+                def _():
+                    gather_copy(0, 0, i).start()
+
+                @pl.when(has_left)
+                def _():
+                    gather_copy(1, 0, i).start()
+
+                if with_core_out:
+                    core_out_copy(z, i).start()
+
+    def gather_step(k, i):
+        for way in range(2):
+            comes = z - k >= 0 if way == 0 else z + k <= n - 1
+            goes = has_right if way == 0 else has_left
+
+            @pl.when(inside(i) & comes)
+            def _():
+                landed = full.at[chunk_at(z - k + 2 * k * way, i)]
+                remote(
+                    landed, landed, ga_send.at[way, k - 1, i], ga_recv.at[way, k - 1, i], "tensor", z + 1 - 2 * way
+                ).wait_recv()
+                if k < n - 1:
+
+                    @pl.when(goes)
+                    def _():
+                        gather_copy(way, k, i).start()
+
+                if with_core_out:
+                    core_out_copy(z - k + 2 * k * way, i).start()
+
+    lead = n - 1 if with_scatter else 0
+    if with_scatter:
+        total = take(0)
+
+    def tick(t, carry):
+        if with_scatter:
+            scatter_step(0, t - z, has_left, lambda block: block > z)
+            scatter_step(1, t - (n - 1 - z), has_right, lambda block: block < z)
+        own_step(t - lead)
+        if with_gather:
+            for k in range(1, n):
+                gather_step(k, t - lead - k)
+        return carry
+
+    lax.fori_loop(0, chunks + lead + (n - 1 if with_gather else 0), tick, 0)
+
+    @all_chunks
+    def _(i):
+        if with_core_in:
+            for block in range(n):
+                core_in_copy(block, i).wait_send()
+        for way in range(2):
+            goes = has_right if way == 0 else has_left
+            if with_scatter:
+                for m in range(n - 1):
+                    block = n - 1 - m if way == 0 else m
+
+                    @pl.when(goes & ((block > z) if way == 0 else (block < z)))
+                    def _():
+                        scatter_copy(way, m, i).wait_send()
+
+            if with_gather:
+                for k in range(n - 1):
+                    has = z - k >= 0 if way == 0 else z + k <= n - 1
+
+                    @pl.when(goes & has)
+                    def _():
+                        gather_copy(way, k, i).wait_send()
+
+        if with_core_out:
+            for block in range(n):
+                core_out_copy(block, i).wait_send()
+                core_out_copy(block, i).wait_recv()
+
+
+def rows_call(
+    collective_id, part, part_peer=None, extras=(), scatter=True, gather=True, core_out=False, middle=None, out_types=()
+):
     n = lax.axis_size("tensor")
-    z = lax.axis_index("tensor")
-    rows = block.shape[0]
-    right, left = [block], [block]
-    for _ in range(n - 1):
-        right.append(lax.ppermute(right[-1], "tensor", [(i, i + 1) for i in range(n - 1)]))
-        left.append(lax.ppermute(left[-1], "tensor", [(i, i - 1) for i in range(1, n)]))
-    out = jnp.zeros((n * rows,) + block.shape[1:], block.dtype)
-    out = lax.dynamic_update_slice_in_dim(out, block, z * rows, 0)
-    for k in range(1, n):
-        piece = jnp.where(z >= k, right[k], left[n - k])
-        out = lax.dynamic_update_slice_in_dim(out, piece, lax.rem(z - k + n, n) * rows, 0)
-    return out
-
-
-def scatter_rows(total):
-    n = lax.axis_size("tensor")
-    z = lax.axis_index("tensor")
-    rows = total.shape[0] // n
-
-    def block(b):
-        return lax.dynamic_slice_in_dim(total, jnp.clip(b, 0, n - 1) * rows, rows, 0).astype(F32)
-
-    right = left = None
-    for s in range(n - 1):
-        to_right, to_left = block(n - 1 - s + z), block(s - (n - 1) + z)
-        if s > 0:
-            to_right = to_right + right.astype(F32)
-            to_left = to_left + left.astype(F32)
-        right = lax.ppermute(
-            to_right.astype(BF16), "tensor", [(i, i + 1) for i in range(n - 1) if i <= s]
-        )
-        left = lax.ppermute(
-            to_left.astype(BF16), "tensor", [(i, i - 1) for i in range(1, n) if n - 1 - i <= s]
-        )
-    return block(z) + right.astype(F32) + left.astype(F32)
+    width = part.shape[1]
+    rows = part.shape[0] // n if scatter else part.shape[0]
+    chunks = rows // CHUNK
+    vmem_spec = pl.BlockSpec(memory_space=pltpu.VMEM)
+    full = jax.ShapeDtypeStruct((n * rows, width), BF16)
+    out_shape = list(out_types) + ([full] if gather else []) + ([full] if core_out else [])
+    scratch = []
+    if part_peer is not None:
+        scratch += [pltpu.VMEM((n * rows, width), BF16)] + [pltpu.SemaphoreType.DMA((n, chunks))] * 2
+    if scatter:
+        scratch += [pltpu.VMEM((n - 1, rows, width), BF16)] * 4
+        scratch += [pltpu.SemaphoreType.DMA((2, n - 1, chunks))] * 2
+    if gather:
+        scratch += [pltpu.SemaphoreType.DMA((2, n - 1, chunks))] * 2
+    if core_out:
+        scratch += [pltpu.SemaphoreType.DMA((n, chunks))] * 2
+    if scatter:
+        scratch += [pltpu.VMEM((CHUNK, width), F32)]
+    operands = [part] + ([part_peer] if part_peer is not None else []) + list(extras)
+    return pl.pallas_call(
+        functools.partial(
+            rows_kernel, n, rows, part_peer is not None, scatter, gather, core_out, middle, len(extras), len(out_types)
+        ),
+        out_shape=out_shape,
+        in_specs=[vmem_spec] * len(operands),
+        out_specs=[vmem_spec] * len(out_shape),
+        scratch_shapes=scratch,
+        compiler_params=pltpu.CompilerParams(
+            collective_id=collective_id, has_side_effects=True, vmem_limit_bytes=48 * 2**20
+        ),
+        name="rows",
+    )(*operands)
+
+
+def norm_middle(total, here, extras, outs):
+    inputs, gain = extras
+    hidden = inputs[here, :].astype(F32) + total
+    outs[0][here, :] = hidden
+    inverse = lax.rsqrt(jnp.mean(hidden * hidden, axis=-1, keepdims=True) + EPSILON)
+    return (hidden * inverse * gain[...]).astype(BF16)
+
+
+def norm_back_middle(total, here, extras, outs):
+    hidden_ref, cot, gain = extras
+    hidden = hidden_ref[here, :]
+    inverse = lax.rsqrt(jnp.mean(hidden * hidden, axis=-1, keepdims=True) + EPSILON)
+    scaled = total * gain[...]
+    grad = cot[here, :].astype(F32) + inverse * (
+        scaled - hidden * inverse * inverse * jnp.mean(scaled * hidden, axis=-1, keepdims=True)
+    )
+    outs[0][here, :] = total
+    outs[1][here, :] = grad
+    return grad.astype(BF16)
+
+
+def plain_middle(total, here, extras, outs):
+    outs[0][here, :] = total
 
 
 def others_of(own, f, axis):
@@ -121,13 +375,18 @@
     return lax.psum_scatter(whole, "fsdp", scatter_dimension=axis, tiled=True).astype(F32)
 
 
-def sum_small(own, other, f):
+def sum_small(values, f, shard):
+    total = sum_rep_first(sum_tensor(values))
     if lax.axis_size("fsdp") == 2:
-        total = own + swap_y(other)
+        total = total[:, :shard] + swap_y(total[:, shard:])
     else:
-        whole = jnp.roll(jnp.concatenate([own, other], axis=1), f * own.shape[1], axis=1)
+        whole = jnp.roll(total, f * shard, axis=1)
         total = lax.psum_scatter(whole, "fsdp", scatter_dimension=1, tiled=True)
-    return sum_tensor(sum_rep(total))
+    return total + swap_x(total)
+
+
+def sum_rep_first(total):
+    return total + swap_core(total)
 
 
 def sum_rep(total):
@@ -154,7 +413,7 @@
 
 def experts_kernel(
     rows, width, own_width, hidden,
-    x0, x1, c0, c1, gate, w_own, w_oth,
+    x0, x1, c0, c1, gate, w_own0, w_own1, w_oth0, w_oth1,
     dw_own, dw_oth, mix0, mix1, ng0, ng1, gate_grad,
     xv, cv, wg, wu, wd, ga, pg, pu, st_mix, st_ng, st_dw, in_sem, mix_sem, ng_sem, dw_sem,
 ):
@@ -169,8 +428,8 @@
     for part, w in ((0, wg), (1, wu), (2, wd)):
         for k in range(2):
             r = pl.ds(k * hidden, hidden)
-            load(w_own.at[k, part], w.at[r, pl.ds(0, own_width)])
-            load(w_oth.at[k, part], w.at[r, pl.ds(own_width, width - own_width)])
+            load((w_own0, w_own1)[k].at[part], w.at[r, pl.ds(0, own_width)])
+            load((w_oth0, w_oth1)[k].at[part], w.at[r, pl.ds(own_width, width - own_width)])
         if part == 0:
             load(x0, xv.at[pl.ds(0, seq)])
             load(x1, xv.at[pl.ds(seq, seq)])
@@ -290,7 +549,7 @@
 def experts_call(x0, x1, c0, c1, gate, w_own, w_oth):
     seq, width = x0.shape
     rows = 2 * seq
-    hidden, own_width = w_own.shape[2], w_own.shape[3]
+    hidden, own_width = w_own[0].shape[1:]
     any_spec = pl.BlockSpec(memory_space=pl.ANY)
     vmem_spec = pl.BlockSpec(memory_space=pltpu.VMEM)
     out_rows = jax.ShapeDtypeStruct((seq, width), BF16)
@@ -298,12 +557,12 @@
     return pl.pallas_call(
         functools.partial(experts_kernel, rows, width, own_width, hidden),
         out_shape=[
-            jax.ShapeDtypeStruct(w_own.shape, BF16),
-            jax.ShapeDtypeStruct(w_oth.shape, BF16),
+            jax.ShapeDtypeStruct((2, 3, hidden, own_width), BF16),
+            jax.ShapeDtypeStruct((2, 3, hidden, width - own_width), BF16),
             out_rows, out_rows, out_rows, out_rows,
             jax.ShapeDtypeStruct((8, rows), F32),
         ],
-        in_specs=[any_spec] * 4 + [vmem_spec] + [any_spec] * 2,
+        in_specs=[any_spec] * 4 + [vmem_spec] + [any_spec] * 4,
         out_specs=[any_spec] * 6 + [vmem_spec],
         scratch_shapes=[
             pltpu.VMEM((rows, width), BF16),
@@ -327,7 +586,7 @@
         ),
         compiler_params=pltpu.CompilerParams(vmem_limit_bytes=56 * 2**20),
         name="experts",
-    )(x0, x1, c0, c1, gate, w_own, w_oth)
+    )(x0, x1, c0, c1, gate, *w_own, *w_oth)
 
 
 def place_kernel(count, table, *refs):
@@ -464,22 +723,17 @@
 
     first_a, first_b = 4 * c + 2 * x, 4 * c + 2 * (1 - x)
     own_a, own_b = routed_chunk(first_a), routed_chunk(first_b)
-    own_s0, own_s1 = shared_chunk(2 * c + x), shared_chunk(2 * c + 1 - x)
-    oth_a = others_of(after(own_a, out_got), f, 3)
-    oth_b = swap_x(oth_a)
-    oth_s0 = others_of(after(own_s0, oth_a), f, 3)
-    oth_s1 = swap_x(oth_s0)
-    own_s = jnp.concatenate([own_s0, own_s1], axis=0)
-    oth_s = jnp.concatenate([oth_s0, oth_s1], axis=0)
+    own_s = jnp.concatenate([shared_chunk(2 * c + x), shared_chunk(2 * c + 1 - x)], axis=0)
 
     cos_table, sin_table = rope_tables(LENGTH, HEAD_DIM)
-    inputs_f = turn(block_input).astype(F32)
-    cot_bf = turn(cotangent)
-    cot_local = cot_bf.astype(F32)
+    inputs = turn(block_input)
+    inputs_f = inputs.astype(F32)
+    cot = turn(cotangent)
     inverse_one = lax.rsqrt(jnp.mean(inputs_f * inputs_f, axis=-1, keepdims=True) + EPSILON)
-    normed = gather_rows((inputs_f * inverse_one * gains[0]).astype(BF16))
-    cot_rows = gather_rows(after(cot_bf, normed))
+    (normed,) = rows_call(0, (inputs_f * inverse_one * gains[0]).astype(BF16), scatter=False)
+    cot_rows = lax.all_gather(after(cot, normed), "tensor", axis=0, tiled=True)
     cot_peer = swap_core(cot_rows)
+    oth_a = others_of(after(own_a, normed, qkv_got), f, 3)
     project = jnp.einsum("ld,cde->cle", normed, qkv_all, preferred_element_type=F32) + bias
     query_rows = rotate(
         project[0].reshape(LENGTH, local_heads, HEAD_DIM), cos_table, sin_table
@@ -489,6 +743,8 @@
     ).astype(BF16)
     value_rows = project[2].reshape(LENGTH, local_heads, HEAD_DIM).astype(BF16)
     visible = visible_mask(piece_starts[0], LENGTH, PIECE)
+    oth_s = others_of(after(own_s, query_rows, out_got), f, 3)
+    oth_b = swap_x(oth_a)
 
     def attend_scores():
         raw = jnp.einsum("qhd,khd->hqk", query_rows, key_rows, preferred_element_type=F32) * scale
@@ -505,10 +761,10 @@
         .astype(BF16)
     )
     heads_part = jnp.dot(attended, out_all, preferred_element_type=F32).astype(BF16)
-    hidden_rows = inputs_f + scatter_rows(heads_part)
-    inverse_two = lax.rsqrt(jnp.mean(hidden_rows * hidden_rows, axis=-1, keepdims=True) + EPSILON)
-    mixed = gather_rows((hidden_rows * inverse_two * gains[1]).astype(BF16))
-    mixed_peer = swap_core(mixed)
+    block_f32 = jax.ShapeDtypeStruct(inputs.shape, F32)
+    hidden_rows, mixed, mixed_peer = rows_call(
+        1, heads_part, extras=(inputs, gains[1:2]), core_out=True, middle=norm_middle, out_types=[block_f32]
+    )
     mixed_pair = jnp.concatenate([mixed, mixed_peer], axis=0)
 
     logits = lax.dot_general(router, mixed_pair, (((1,), (1,)), ((), ())), preferred_element_type=F32)
@@ -522,10 +778,10 @@
         return jnp.pad(lax.dynamic_slice_in_dim(gates, first, 2, 0), ((0, 6), (0, 0)))
 
     data = (mixed, mixed_peer, cot_rows, cot_peer)
-    dw_own_a, dw_oth_a, *rows_a, grad_a = experts_call(*data, gate_rows(first_a), own_a, oth_a)
+    dw_own_a, dw_oth_a, *rows_a, grad_a = experts_call(*data, gate_rows(first_a), (own_a[0], own_a[1]), (oth_a[0], oth_a[1]))
     shared_rows = jnp.broadcast_to(shared_scale, (8, shared_scale.shape[1]))
-    dw_own_s, dw_oth_s, *rows_s, grad_s = experts_call(*data, shared_rows, own_s, oth_s)
-    dw_own_b, dw_oth_b, *rows_b, grad_b = experts_call(*data, gate_rows(first_b), own_b, oth_b)
+    dw_own_s, dw_oth_s, *rows_s, grad_s = experts_call(*data, shared_rows, (own_s[0], own_s[1]), (oth_s[0], oth_s[1]))
+    dw_own_b, dw_oth_b, *rows_b, grad_b = experts_call(*data, gate_rows(first_b), (own_b[0], own_b[1]), (oth_b[0], oth_b[1]))
 
     prob_grad = jnp.zeros_like(router_probs)
     prob_grad = lax.dynamic_update_slice_in_dim(prob_grad, grad_a[:2], first_a, 0)
@@ -554,23 +810,21 @@
             rows_a[index].astype(F32) + rows_s[index].astype(F32) + rows_b[index].astype(F32)
         )
 
-    normed_for_peer = (total(3) + extra(1)).astype(BF16)
-    normed_grad = total(2) + extra(0) + swap_core(normed_for_peer).astype(F32)
-    normed_two_grad = scatter_rows(normed_grad.astype(BF16))
-    scaled_two = normed_two_grad * gains[1]
-    hidden_grad = cot_local + inverse_two * (
-        scaled_two
-        - hidden_rows
-        * inverse_two
-        * inverse_two
-        * jnp.mean(scaled_two * hidden_rows, axis=-1, keepdims=True)
-    )
+    normed_two_grad, hidden_grad, branch_grad = rows_call(
+        2,
+        (total(2) + extra(0)).astype(BF16),
+        part_peer=(total(3) + extra(1)).astype(BF16),
+        extras=(hidden_rows, cot, gains[1:2]),
+        middle=norm_back_middle,
+        out_types=[block_f32, block_f32],
+    )
+    inverse_two = lax.rsqrt(jnp.mean(hidden_rows * hidden_rows, axis=-1, keepdims=True) + EPSILON)
     gain_two_grad = jnp.sum(normed_two_grad * hidden_rows * inverse_two, axis=0)
-    branch_grad = gather_rows(hidden_grad.astype(BF16))
 
     mixer_for_peer = after(total(1).astype(BF16), branch_grad)
     mixer = (total(0) + swap_core(mixer_for_peer).astype(F32)).astype(BF16)
-    result = turn_back((hidden_rows + scatter_rows(mixer)).astype(BF16))
+    mixer_local = lax.psum_scatter(mixer, "tensor", scatter_dimension=0, tiled=True).astype(F32)
+    result = turn_back((hidden_rows + mixer_local).astype(BF16))
 
     out_grad = jnp.einsum("lf,ld->fd", attended, branch_grad, preferred_element_type=F32).astype(BF16)
     attended_grad = jnp.einsum("ld,fd->lf", branch_grad, out_all, preferred_element_type=F32)
@@ -592,7 +846,9 @@
     ).astype(BF16)
     bias_grad = jnp.sum(project_grad, axis=1, dtype=F32)
     normed_one_grad = jnp.einsum("cle,cde->ld", project_grad, qkv_all, preferred_element_type=F32)
-    input_row_grad = scatter_rows(normed_one_grad.astype(BF16))
+    (input_row_grad,) = rows_call(
+        3, normed_one_grad.astype(BF16), gather=False, middle=plain_middle, out_types=[block_f32]
+    )
     qkv_grad = jnp.einsum("ld,cle->cde", normed, project_grad, preferred_element_type=F32).astype(BF16)
     scaled_one = input_row_grad * gains[0]
     input_grad = hidden_grad + inverse_one * (
@@ -648,10 +904,8 @@
     out_out = dense_sum(out_grad, 0, 1)
     qkv_out = dense_sum(qkv_grad, 2, 1)
 
-    early = jnp.concatenate([router_grad, gain_two_grad[None]], axis=0)
-    early = sum_small(early[:, :shard], early[:, shard:], f)
-    late = sum_small(gain_one_grad[None, :shard], gain_one_grad[None, shard:], f)
-    gains_out = jnp.concatenate([late, early[9:10]], axis=0)
+    small_sums = jnp.concatenate([router_grad, gain_one_grad[None], gain_two_grad[None]], axis=0)
+    small_sums = sum_small(small_sums, f, shard)
     bias_sum = sum_rep(lax.psum(bias_grad, "fsdp") if owners != 2 else bias_grad + swap_y(bias_grad))
     bias_out = lax.dynamic_slice_in_dim(
         bias_sum.reshape(3, local_heads, HEAD_DIM), f * (HEAD_DIM // owners), HEAD_DIM // owners, 2
@@ -659,12 +913,12 @@
     return (
         result,
         turn_back(input_grad),
-        gains_out,
+        small_sums[9:],
         qkv_out,
         bias_out,
         out_out,
-        early[:EXPERTS].T,
-        early[EXPERTS],
+        small_sums[:EXPERTS].T,
+        small_sums[EXPERTS],
         gate_up_out,
         down_out,
         shared_up_out,

time: 1290 us -> 1050 us (0.81)
  waiting for transfers between devices: 531 us -> 191 us
  Pallas kernels: 198 us -> 486 us
  starting transfers between devices: 197 us -> 25.1 us
  other arithmetic: 166 us -> 138 us
    pallas_call x0 -> x4, Pallas kernels: none -> 282 us  [rows_call(): pl.pallas_call(functools.partial(rows_kernel, n, rows, part_peer is not N...]
    ppermute x48 -> x0, waiting for transfers between devices: 182 us -> none  [the longest x12 75.2 us: scatter_rows(): lax.ppermute(to_right.astype(BF16), 'tensor', [(i, i + 1) for i in range(...]
    ppermute x13 -> x12, waiting for transfers between devices: 180 us -> 16 us  [swap_y(): return lax.ppermute(a, 'fsdp', [(0, 1), (1, 0)])]
    ppermute x48 -> x0, starting transfers between devices: 160 us -> none  [the longest x12 75.1 us: scatter_rows(): lax.ppermute(to_right.astype(BF16), 'tensor', [(i, i + 1) for i in range(...]
    dynamic_update_slice x15 -> x0, other arithmetic: 22.6 us -> none  [the longest x12 17.9 us: gather_rows(): lax.dynamic_update_slice_in_dim(out, piece, lax.rem(z - k + n, n) * rows, 0)]
    convert_element_type x15 -> x1, other arithmetic: 20.9 us -> 0.22 us  [shards(): (inputs_f * inverse_one * gains[0]).astype(BF16)]
    squeeze x0 -> x3, local copies, waits for them, and re-layouts: none -> 13.3 us  [the longest x1 5.25 us: shards(): oth_a[1]]
    ppermute x10 -> x8, waiting for transfers between devices: 161 us -> 165 us  [swap_x(): return lax.ppermute(a, 'rep', [(i, i ^ 2) for i in range(n)])]
  transfers between devices with their start and end apart: 92 -> 38, of which waited for: 37 -> 11; matrix products, arithmetic and copies ran while one was open for 21% -> 30% of each run, Pallas kernels for 9% -> 44%
where the time goes in v2:
time: 1050 us; the launch traced here: 1040 us
  Pallas kernels  486 us (46%)
  waiting for transfers between devices  191 us (18%)
  other arithmetic  138 us (13%)
  local copies, waits for them, and re-layouts  133 us (13%)
  matrix products  55.4 us (5%)
  starting transfers between devices  25.1 us (2%)
  between operations  15.4 us (1%)
    pallas_call x4, Pallas kernels, rows_call(): pl.pallas_call(functools.partial(rows_kernel, n, rows, part_peer is not N...  282 us
    pallas_call x3, Pallas kernels, experts_call(): pl.pallas_call(functools.partial(experts_kernel, rows, width, own_width,...  170 us
    ppermute x8, waiting for transfers between devices, swap_x(): return lax.ppermute(a, 'rep', [(i, i ^ 2) for i in range(n)])  165 us
    unnamed x151, local copies, waits for them, and re-layouts  58.9 us
    convert_element_type x7, other arithmetic, add(): return (one.astype(F32) + two.astype(F32)).astype(BF16)  38.1 us
    pallas_call x4, Pallas kernels, place_call(): pl.pallas_call(functools.partial(place_kernel, len(sources)), out_shape=j...  34.5 us
  transfers between devices with their start and end apart: 38, of which 11 were waited for; matrix products, arithmetic and copies ran while one was open for 30% of the time, Pallas kernels for 44%

profile of v2, /device:TPU:0, one launch (start us, length us, event | category | flops | bytes accessed | tf_op | source)
XLA Modules:
  0.0 1043.2 jit_solution(12917822779397948154)
XLA Ops:
  13.8 4.7 copy.110
  43.3 9.7 constant_dynamic-slice_fusion.4
  53.0 4.9 copy.157
  57.9 4.9 copy.156
  62.7 3.9 fusion.91
  79.0 11.9 %collective-permute-done.3 = bf16[256,1024]{1,0:T(8,128)(2,1)} collective-permute-done((bf16[256,1024]{1,0:T(8,128)(2,1)S(1)}, bf16[256,1024]{1,0:T(8,128)(2,1)}, u32[]{:S(2)}, u32[]{:S(2)}) %collective-permute-start.3) | collective-permute-done | bytes 524320 | tf_op jit(solution)/shard_map/ppermute | solution.py:57
  92.0 47.2 %rows.4 = bf16[640,2048]{1,0:T(8,128)(2,1)S(1)} custom-call(bf16[160,2048]{1,0:T(8,128)(2,1)S(1)} %fusion.37.refs_0_), custom_call_target="tpu_custom_call" | custom-call | tf_op jit(solution)/shard_map/rows/pallas_call | solution.py:322
  143.9 3.8 maximum_select_fusion
  148.2 5.1 add_bitcast_fusion
  165.7 3.7 subtract_convert_fusion.2
  172.6 5.3 fusion.99
  177.9 4.0 fusion.31
  185.2 94.1 %rows.5 = (f32[160,2048]{1,0:T(8,128)S(1)}, bf16[640,2048]{1,0:T(8,128)(2,1)S(1)}, bf16[640,2048]{1,0:T(8,128)(2,1)}) custom-call(bf16[640,2048]{1,0:T(8,128)(2,1)} %convolution_convert_fusion.1.refs_0_, bf16[160,2048]{1,0:T(8,128)(2,1)S(1)} %get-tuple-element.132.refs_1_, f32[1,2048]{1,0:T(1,128)S(1)} %bitcast.128), custom_call_target="tpu_custom_call" | custom-call | tf_op jit(solution)/shard_map/rows/pallas_call | solution.py:322
  290.3 5.2 slice_bitcast_fusion.4
  295.6 56.4 %experts.3 = (bf16[2,3,352,1024]{3,2,1,0:T(8,128)(2,1)}, bf16[2,3,352,1024]{3,2,1,0:T(8,128)(2,1)}, bf16[640,2048]{1,0:T(8,128)(2,1)}, bf16[640,2048]{1,0:T(8,12...) custom-call(bf16[640,2048]{1,0:T(8,128)(2,1)} %copy-done.2, ...), custom_call_target="tpu_custom_call" | custom-call | flops 33218887680 | bytes 32505856 | tf_op jit(solution)/shard_map/experts/pallas_call | solution.py:557
  354.4 5.2 slice_bitcast_fusion.2
  360.2 56.5 %experts.4 = (bf16[2,3,352,1024]{3,2,1,0:T(8,128)(2,1)}, bf16[2,3,352,1024]{3,2,1,0:T(8,128)(2,1)}, bf16[640,2048]{1,0:T(8,128)(2,1)}, bf16[640,2048]{1,0:T(8,12...) custom-call(bf16[640,2048]{1,0:T(8,128)(2,1)} %copy-done.2, ...), custom_call_target="tpu_custom_call" | custom-call | flops 33218887680 | bytes 32505856 | tf_op jit(solution)/shard_map/experts/pallas_call | solution.py:557
  421.1 56.8 %experts.5 = (bf16[2,3,352,1024]{3,2,1,0:T(8,128)(2,1)}, bf16[2,3,352,1024]{3,2,1,0:T(8,128)(2,1)}, bf16[640,2048]{1,0:T(8,128)(2,1)}, bf16[640,2048]{1,0:T(8,12...) custom-call(bf16[640,2048]{1,0:T(8,128)(2,1)} %copy-done.2, ...), custom_call_target="tpu_custom_call" | custom-call | flops 33218887680 | bytes 32505856 | tf_op jit(solution)/shard_map/experts/pallas_call | solution.py:557
  480.4 5.4 add_convert_fusion.7.refs_1_
  488.6 92.7 %rows.6 = (f32[160,2048]{1,0:T(8,128)S(1)}, f32[160,2048]{1,0:T(8,128)S(1)}, bf16[640,2048]{1,0:T(8,128)(2,1)}) custom-call(bf16[640,2048]{1,0:T(8,128)(2,1)} %add_convert_fusion.8.refs_0_, bf16[640,2048]{1,0:T(8,128)(2,1)} %add_convert_fusion.7.refs_1_, f32[160,2048]{1,0:T(8,128)S(1)} %get-tuple-element.46.refs_2_, bf16[160,2048]{1,0:T(8,128)(2,1)S(1)} %copy-done, ...), custom_call_target="tpu_custom_call" | custom-call | tf_op jit(solution)/shard_map/rows/pallas_call | solution.py:322
  581.4 6.8 add_convert_fusion.9
  590.3 3.9 multiply_reduce_fusion
  594.1 3.8 multiply_convert_fusion
  600.6 8.1 add_convert_fusion.5
  626.9 7.5 convolution_convert_fusion
  642.8 6.5 add_convert_fusion.1
  650.8 5.7 add_convert_fusion.6
  656.5 48.6 %collective-permute-done.30 = bf16[2,3,352,1024]{3,2,1,0:T(8,128)(2,1)} collective-permute-done((bf16[2,3,352,1024]{3,2,1,0:T(8,128)(2,1)}, bf16[2,3,352,1024]{3,2,1,0:T(8,128)(2,1)}, u32[]{:S(2)}, u32[]{:S(2)}) %collective-permute-start.30) | collective-permute-done | bytes 4325408 | tf_op jit(solution)/shard_map/ppermute | solution.py:62
  705.1 12.0 %add_convert_fusion.2 = (bf16[2,3,352,1024]{3,2,1,0:T(8,128)(2,1)}, bf16[2,3,352,1024]{3,2,1,0:T(8,128)(2,1)}) fusion(bf16[2,3,352,1024]{3,2,1,0:T(8,128)(2,1)} %collective-permute-done.30, bf16[2,3,352,1024]{3,2,1,0:T(8,128)(2,1)} %collective-permute-done.28, bf16[2,3,352,1024]{3,2,1,0:T(8,128)(2,1)} %get-tuple-element.73), kind=kLoop, calls=%fused_computation.4 | loop fusion | flops 17301504 | bytes 21626880 | tf_op jit(solution)/shard_map/convert_element_type | solution.py:872
  717.9 7.8 bitcast_convert_fusion.refs_0_
  731.3 47.5 %rows.7 = f32[160,2048]{1,0:T(8,128)S(1)} custom-call(bf16[640,2048]{1,0:T(8,128)(2,1)S(1)} %bitcast_convert_fusion.refs_0_), custom_call_target="tpu_custom_call" | custom-call | tf_op jit(solution)/shard_map/rows/pallas_call | solution.py:322
  792.5 5.3 collective-permute-done.34
  797.8 8.1 add_convert_fusion.refs_0_
  807.7 82.8 %collective-permute-done.29 = bf16[2,3,352,1024]{3,2,1,0:T(8,128)(2,1)} collective-permute-done((bf16[2,3,352,1024]{3,2,1,0:T(8,128)(2,1)}, bf16[2,3,352,1024]{3,2,1,0:T(8,128)(2,1)}, u32[]{:S(2)}, u32[]{:S(2)}) %collective-permute-start.29) | collective-permute-done | bytes 4325408 | tf_op jit(solution)/shard_map/ppermute | solution.py:62
  890.5 8.0 add_convert_fusion.3.refs_0_
  901.3 23.0 %collective-permute-done.18 = bf16[3,1024,256]{1,2,0:T(8,128)(2,1)} collective-permute-done((bf16[3,1024,256]{1,2,0:T(8,128)(2,1)}, bf16[3,1024,256]{1,2,0:T(8,128)(2,1)}, u32[]{:S(2)}, u32[]{:S(2)}) %collective-permute-start.18) | collective-permute-done | bytes 1572896 | tf_op jit(solution)/shard_map/ppermute | solution.py:62
  924.2 3.7 add_convert_fusion.10
  929.8 5.4 collective-permute-done.22
  936.6 7.0 collective-permute-done.12
  953.3 5.2 fusion.8
  958.5 6.8 copy.138
  967.1 4.4 place.6
  971.5 5.8 convert_bitcast_fusion
  977.3 11.2 %copy.137 = f32[1024,2,4,352]{0,3,2,1:T(8,128)} copy(f32[1024,2,4,352]{0,3,1,2:T(8,128)} %convert_bitcast_fusion) | data formatting | bytes 23068672 | tf_op jit(solution)/shard_map/convert_element_type | solution.py:885
  988.5 17.6 %copy.139 = f32[1024,2,1408]{2,1,0:T(2,128)} copy(f32[1024,2,1408]{0,2,1:T(8,128)} %bitcast.130) | data formatting | bytes 23068672
  1006.1 5.7 place.7
  1011.8 9.7 place.5
  1021.5 14.6 %place.4 = f32[8,2,352,1024]{3,2,1,0:T(8,128)} custom-call(s32[5,8]{1,0:T(8,128)S(1)} %stack.8.table, bf16[2,3,352,1024]{3,2,1,0:T(8,128)(2,1)} %add_convert_fusion.3.refs_0_, bf16[2,3,352,1024]{3,2,1,0:T(8,128)(2,1)} %get-tuple-element.127.refs_1_, bf16[2,3,352,1024]{3,2,1,0:T(8,128)(2,1)} %collective-permute-done.31.refs_2_, ...), custom_call_target="tpu_custom_call" | custom-call | tf_op jit(solution)/shard_map/place/pallas_call | solution.py:609
  (339 shorter events, 163.6 us)
Async XLA Ops:
  7.2 273.7 %all-gather.2.cloned.1.call-start = ((), (), s32[]{:S(2)}) async-start(), calls=%async_computation.1 | async-start | bytes 3276800 | tf_op jit(solution)/shard_map/all_gather | solution.py:734
  7.2 65.4 %collective-permute-start.6 = (s32[640,4]{0,1:T(4,128)}, s32[640,4]{0,1:T(4,128)}, u32[]{:S(2)}, u32[]{:S(2)}) collective-permute-start(s32[640,4]{0,1:T(4,128)} %param.19), channel_id=1, source_target_pairs={{0,8},{8,0},{16,24},{24,16},{1,9},{9,1},{17,25},{25,17},{2,10},{10... | collective-permute-start | bytes 30728 | tf_op jit(solution)/shard_map/ppermute | solution.py:67
  11.3 62.1 %collective-permute-start.2 = (bf16[1,12032]{1,0:T(2,128)(2,1)}, bf16[1,12032]{1,0:T(2,128)(2,1)}, u32[]{:S(2)}, u32[]{:S(2)}) collective-permute-start(bf16[1,12032]{1,0:T(2,128)(2,1)} %broadcast_in_dim.116), channel_id=1, source_target_pairs={{0,4},{4,0},{1,5},{5,1},{2,6},{6,2},{3,7},{7,3},{8,12},{12,8},{9,1... | collective-permute-start | bytes 72200 | tf_op jit(solution)/shard_map/ppermute | solution.py:57
  21.1 53.1 %collective-permute-start = (bf16[3,1024,256]{1,2,0:T(8,128)(2,1)}, bf16[3,1024,256]{1,2,0:T(8,128)(2,1)}, u32[]{:S(2)}, u32[]{:S(2)}) collective-permute-start(bf16[3,1024,256]{1,2,0:T(8,128)(2,1)} %constant_dynamic-slice_fusion.9), channel_id=1, source_target_pairs={{0,4},{4,0},{1,5},{5,1},{2,6},{6,2},{3,7},{7,3},{8,12},{12,8},{9,1... | collective-permute-start | bytes 4718600 | tf_op jit(solution)/shard_map/ppermute | solution.py:57
  38.6 52.7 %copy-start.47 = (f32[160]{0:T(256)}, f32[160]{0:T(256)S(1)}, u32[]{:S(2)}) copy-start(f32[160]{0:T(256)S(1)} %add_rsqrt_fusion.1) | copy-start | bytes 1924
  74.2 69.7 %collective-permute-start.1 = (bf16[3,1024,256]{1,2,0:T(8,128)(2,1)}, bf16[3,1024,256]{1,2,0:T(8,128)(2,1)}, u32[]{:S(2)}, u32[]{:S(2)}) collective-permute-start(bf16[3,1024,256]{1,2,0:T(8,128)(2,1)} %collective-permute-done), channel_id=1, source_target_pairs={{0,8},{8,0},{16,24},{24,16},{1,9},{9,1},{17,25},{25,17},{2,10},{10... | collective-permute-start | bytes 4718600 | tf_op jit(solution)/shard_map/ppermute | solution.py:67
  76.2 14.7 %collective-permute-start.3 = (bf16[256,1024]{1,0:T(8,128)(2,1)S(1)}, bf16[256,1024]{1,0:T(8,128)(2,1)}, u32[]{:S(2)}, u32[]{:S(2)}) collective-permute-start(bf16[256,1024]{1,0:T(8,128)(2,1)S(1)} %constant_dynamic-slice_fusion.7), channel_id=1, source_target_pairs={{0,4},{4,0},{1,5},{5,1},{2,6},{6,2},{3,7},{7,3},{8,12},{12,8},{9,1... | collective-permute-start | bytes 1572872 | tf_op jit(solution)/shard_map/ppermute | solution.py:57
  90.9 49.9 %collective-permute-start.4 = (bf16[256,1024]{1,0:T(8,128)(2,1)}, bf16[256,1024]{1,0:T(8,128)(2,1)}, u32[]{:S(2)}, u32[]{:S(2)}) collective-permute-start(bf16[256,1024]{1,0:T(8,128)(2,1)} %collective-permute-done.3), channel_id=1, source_target_pairs={{0,8},{8,0},{16,24},{24,16},{1,9},{9,1},{17,25},{25,17},{2,10},{10... | collective-permute-start | bytes 1572872 | tf_op jit(solution)/shard_map/ppermute | solution.py:67
  139.2 759.4 %reduce-scatter.2.cloned.1.call-start = ((), (), s32[]{:S(2)}) async-start(), calls=%async_computation.2 | async-start | bytes 3276800 | tf_op jit(solution)/shard_map/reduce_scatter | solution.py:826
  139.3 149.3 %collective-permute-start.7 = (bf16[2,3,352,1024]{3,2,1,0:T(8,128)(2,1)}, bf16[2,3,352,1024]{3,2,1,0:T(8,128)(2,1)}, u32[]{:S(2)}, u32[]{:S(2)}) collective-permute-start(bf16[2,3,352,1024]{3,2,1,0:T(8,128)(2,1)} %pad_maximum_fusion.1), channel_id=1, source_target_pairs={{0,4},{4,0},{1,5},{5,1},{2,6},{6,2},{3,7},{7,3},{8,12},{12,8},{9,1... | collective-permute-start | bytes 12976136 | tf_op jit(solution)/shard_map/ppermute | solution.py:57
  172.1 182.2 %collective-permute-start.8 = (bf16[2,3,352,1024]{3,2,1,0:T(8,128)(2,1)}, bf16[2,3,352,1024]{3,2,1,0:T(8,128)(2,1)}, u32[]{:S(2)}, u32[]{:S(2)}) collective-permute-start(bf16[2,3,352,1024]{3,2,1,0:T(8,128)(2,1)} %pad_maximum_fusion.2), channel_id=1, source_target_pairs={{0,4},{4,0},{1,5},{5,1},{2,6},{6,2},{3,7},{7,3},{8,12},{12,8},{9,1... | collective-permute-start | bytes 12976136 | tf_op jit(solution)/shard_map/ppermute | solution.py:57
  280.9 14.7 %collective-permute-start.5 = (bf16[640,2048]{1,0:T(8,128)(2,1)}, bf16[640,2048]{1,0:T(8,128)(2,1)}, u32[]{:S(2)}, u32[]{:S(2)}) collective-permute-start(bf16[640,2048]{1,0:T(8,128)(2,1)} %all-gather.2.cloned.1.call-done.c0), channel_id=1, source_target_pairs={{0,8},{8,0},{16,24},{24,16},{1,9},{9,1},{17,25},{25,17},{2,10},{10... | collective-permute-start | bytes 7864328 | tf_op jit(solution)/shard_map/ppermute | solution.py:67
  288.6 129.6 %collective-permute-start.9 = (bf16[2,3,352,1024]{3,2,1,0:T(8,128)(2,1)}, bf16[2,3,352,1024]{3,2,1,0:T(8,128)(2,1)S(1)}, u32[]{:S(2)}, u32[]{:S(2)}) collective-permute-start(bf16[2,3,352,1024]{3,2,1,0:T(8,128)(2,1)} %collective-permute-done.7), channel_id=1, source_target_pairs={{0,16},{8,24},{16,0},{24,8},{1,17},{9,25},{17,1},{25,9},{2,18},{10... | collective-permute-start | bytes 12976136 | tf_op jit(solution)/shard_map/ppermute | solution.py:62
  352.0 248.5 %collective-permute-start.27 = (bf16[2,3,352,1024]{3,2,1,0:T(8,128)(2,1)}, bf16[2,3,352,1024]{3,2,1,0:T(8,128)(2,1)}, u32[]{:S(2)}, u32[]{:S(2)}) collective-permute-start(bf16[2,3,352,1024]{3,2,1,0:T(8,128)(2,1)} %get-tuple-element.72), channel_id=1, source_target_pairs={{0,4},{4,0},{1,5},{5,1},{2,6},{6,2},{3,7},{7,3},{8,12},{12,8},{9,1... | collective-permute-start | bytes 12976136 | tf_op jit(solution)/shard_map/ppermute | solution.py:57
  416.7 225.5 %collective-permute-start.33 = (bf16[2,3,352,1024]{3,2,1,0:T(8,128)(2,1)}, bf16[2,3,352,1024]{3,2,1,0:T(8,128)(2,1)}, u32[]{:S(2)}, u32[]{:S(2)}) collective-permute-start(bf16[2,3,352,1024]{3,2,1,0:T(8,128)(2,1)} %get-tuple-element.76), channel_id=1, source_target_pairs={{0,4},{4,0},{1,5},{5,1},{2,6},{6,2},{3,7},{7,3},{8,12},{12,8},{9,1... | collective-permute-start | bytes 12976136 | tf_op jit(solution)/shard_map/ppermute | solution.py:57
  421.1 59.3 %copy-start.31 = (bf16[640,2048]{1,0:T(8,128)(2,1)S(1)}, bf16[640,2048]{1,0:T(8,128)(2,1)}, u32[]{:S(2)}) copy-start(bf16[640,2048]{1,0:T(8,128)(2,1)} %get-tuple-element.64) | copy-start | bytes 7864324
  478.8 177.7 %collective-permute-start.28 = (bf16[2,3,352,1024]{3,2,1,0:T(8,128)(2,1)}, bf16[2,3,352,1024]{3,2,1,0:T(8,128)(2,1)}, u32[]{:S(2)}, u32[]{:S(2)}) collective-permute-start(bf16[2,3,352,1024]{3,2,1,0:T(8,128)(2,1)} %get-tuple-element.74), channel_id=1, source_target_pairs={{0,4},{4,0},{1,5},{5,1},{2,6},{6,2},{3,7},{7,3},{8,12},{12,8},{9,1... | collective-permute-start | bytes 12976136 | tf_op jit(solution)/shard_map/ppermute | solution.py:57
  488.6 92.8 %copy-start.15 = (bf16[640,2048]{1,0:T(8,128)(2,1)S(1)}, bf16[640,2048]{1,0:T(8,128)(2,1)}, u32[]{:S(2)}) copy-start(bf16[640,2048]{1,0:T(8,128)(2,1)} %get-tuple-element.55) | copy-start | bytes 7864324
  488.6 101.6 %slice-start.2 = ((s8[6553600]{0:T(1024)(128)(4,1)}), s8[4194304]{0:T(1024)(128)(4,1)S(1)}, s32[]{:S(2)}) async-start(s8[6553600]{0:T(1024)(128)(4,1)} %bitcast.135), calls=%async_computation.5 | async-start | bytes 8388608
  588.3 61.0 %collective-permute-start.10 = (bf16[640,2048]{1,0:T(8,128)(2,1)}, bf16[640,2048]{1,0:T(8,128)(2,1)}, u32[]{:S(2)}, u32[]{:S(2)}) collective-permute-start(bf16[640,2048]{1,0:T(8,128)(2,1)} %add_convert_fusion.9), channel_id=1, source_target_pairs={{0,8},{8,0},{16,24},{24,16},{1,9},{9,1},{17,25},{25,17},{2,10},{10... | collective-permute-start | bytes 7864328 | tf_op jit(solution)/shard_map/ppermute | solution.py:67
  608.7 96.5 %collective-permute-start.30 = (bf16[2,3,352,1024]{3,2,1,0:T(8,128)(2,1)}, bf16[2,3,352,1024]{3,2,1,0:T(8,128)(2,1)}, u32[]{:S(2)}, u32[]{:S(2)}) collective-permute-start(bf16[2,3,352,1024]{3,2,1,0:T(8,128)(2,1)} %add_convert_fusion.5), channel_id=1, source_target_pairs={{0,16},{8,24},{16,0},{24,8},{1,17},{9,25},{17,1},{25,9},{2,18},{10... | collective-permute-start | bytes 12976136 | tf_op jit(solution)/shard_map/ppermute | solution.py:62
  639.1 86.5 %collective-permute-start.16 = (bf16[3,2048,256]{1,2,0:T(8,128)(2,1)}, bf16[3,2048,256]{1,2,0:T(8,128)(2,1)}, u32[]{:S(2)}, u32[]{:S(2)}) collective-permute-start(bf16[3,2048,256]{1,2,0:T(8,128)(2,1)} %dynamic-slice_bitcast_fusion), channel_id=1, source_target_pairs={{0,8},{8,0},{16,24},{24,16},{1,9},{9,1},{17,25},{25,17},{2,10},{10... | collective-permute-start | bytes 9437192 | tf_op jit(solution)/shard_map/ppermute | solution.py:67
  642.2 141.8 %collective-permute-start.23 = (bf16[256,2048]{1,0:T(8,128)(2,1)}, bf16[256,2048]{1,0:T(8,128)(2,1)}, u32[]{:S(2)}, u32[]{:S(2)}) collective-permute-start(bf16[256,2048]{1,0:T(8,128)(2,1)} %constant_dynamic-slice_fusion.1), channel_id=1, source_target_pairs={{0,8},{8,0},{16,24},{24,16},{1,9},{9,1},{17,25},{25,17},{2,10},{10... | collective-permute-start | bytes 3145736 | tf_op jit(solution)/shard_map/ppermute | solution.py:67
  649.3 148.5 %collective-permute-start.34 = (bf16[2,3,352,1024]{3,2,1,0:T(8,128)(2,1)}, bf16[2,3,352,1024]{3,2,1,0:T(8,128)(2,1)}, u32[]{:S(2)}, u32[]{:S(2)}) collective-permute-start(bf16[2,3,352,1024]{3,2,1,0:T(8,128)(2,1)} %add_convert_fusion.1), channel_id=1, source_target_pairs={{0,16},{8,24},{16,0},{24,8},{1,17},{9,25},{17,1},{25,9},{2,18},{10... | collective-permute-start | bytes 12976136 | tf_op jit(solution)/shard_map/ppermute | solution.py:62
  717.2 173.3 %collective-permute-start.29 = (bf16[2,3,352,1024]{3,2,1,0:T(8,128)(2,1)}, bf16[2,3,352,1024]{3,2,1,0:T(8,128)(2,1)}, u32[]{:S(2)}, u32[]{:S(2)}) collective-permute-start(bf16[2,3,352,1024]{3,2,1,0:T(8,128)(2,1)} %get-tuple-element.128), channel_id=1, source_target_pairs={{0,16},{8,24},{16,0},{24,8},{1,17},{9,25},{17,1},{25,9},{2,18},{10... | collective-permute-start | bytes 12976136 | tf_op jit(solution)/shard_map/ppermute | solution.py:62
  730.2 57.3 %collective-permute-start.17 = (bf16[3,1024,256]{1,2,0:T(8,128)(2,1)}, bf16[3,1024,256]{1,2,0:T(8,128)(2,1)}, u32[]{:S(2)}, u32[]{:S(2)}) collective-permute-start(bf16[3,1024,256]{1,2,0:T(8,128)(2,1)} %slice.225), channel_id=1, source_target_pairs={{0,4},{4,0},{1,5},{5,1},{2,6},{6,2},{3,7},{7,3},{8,12},{12,8},{9,1... | collective-permute-start | bytes 4718600 | tf_op jit(solution)/shard_map/ppermute | solution.py:57
  731.2 47.5 %copy-start.22 = (bf16[1,640,512]{2,1,0:T(8,128)(2,1)S(1)}, bf16[1,640,512]{2,1,0:T(8,128)(2,1)}, u32[]{:S(2)}) copy-start(bf16[1,640,512]{2,1,0:T(8,128)(2,1)} %copy.134) | copy-start | bytes 1966084
  731.2 47.5 %copy-start.25 = (bf16[1,640,512]{2,1,0:T(8,128)(2,1)S(1)}, bf16[1,640,512]{2,1,0:T(8,128)(2,1)}, u32[]{:S(2)}) copy-start(bf16[1,640,512]{2,1,0:T(8,128)(2,1)} %copy.132) | copy-start | bytes 1966084
  731.2 47.5 %copy-start.26 = (bf16[1,640,512]{2,1,0:T(8,128)(2,1)S(1)}, bf16[1,640,512]{2,1,0:T(8,128)(2,1)}, u32[]{:S(2)}) copy-start(bf16[1,640,512]{2,1,0:T(8,128)(2,1)} %copy.133) | copy-start | bytes 1966084
  731.3 49.7 %copy-start.46 = (f32[1,8,2,128]{3,1,2,0:T(8,128)S(1)}, f32[1,8,2,128]{3,1,2,0:T(8,128)}, u32[]{:S(2)}) copy-start(f32[1,8,2,128]{3,1,2,0:T(8,128)} %copy-done.45) | copy-start | bytes 24580
  731.3 49.7 %copy-start.48 = (f32[160]{0:T(256)S(1)}, f32[160]{0:T(256)}, u32[]{:S(2)}) copy-start(f32[160]{0:T(256)} %copy-done.47) | copy-start | bytes 1924
  779.1 3.7 collective-permute-start.20
  782.8 1.2 collective-permute-start.21
  785.7 20.2 %collective-permute-start.24 = (bf16[256,1024]{1,0:T(8,128)(2,1)S(1)}, bf16[256,1024]{1,0:T(8,128)(2,1)S(1)}, u32[]{:S(2)}, u32[]{:S(2)}) collective-permute-start(bf16[256,1024]{1,0:T(8,128)(2,1)S(1)} %slice.227), channel_id=1, source_target_pairs={{0,4},{4,0},{1,5},{5,1},{2,6},{6,2},{3,7},{7,3},{8,12},{12,8},{9,1... | collective-permute-start | bytes 1572872 | tf_op jit(solution)/shard_map/ppermute | solution.py:57
  790.7 133.5 %collective-permute-start.18 = (bf16[3,1024,256]{1,2,0:T(8,128)(2,1)}, bf16[3,1024,256]{1,2,0:T(8,128)(2,1)}, u32[]{:S(2)}, u32[]{:S(2)}) collective-permute-start(bf16[3,1024,256]{1,2,0:T(8,128)(2,1)} %add_convert_fusion.11), channel_id=1, source_target_pairs={{0,16},{8,24},{16,0},{24,8},{1,17},{9,25},{17,1},{25,9},{2,18},{10... | collective-permute-start | bytes 4718600 | tf_op jit(solution)/shard_map/ppermute | solution.py:62
  805.9 161.2 %collective-permute-start.35 = (bf16[2,3,352,1024]{3,2,1,0:T(8,128)(2,1)}, bf16[2,3,352,1024]{3,2,1,0:T(8,128)(2,1)}, u32[]{:S(2)}, u32[]{:S(2)}) collective-permute-start(bf16[2,3,352,1024]{3,2,1,0:T(8,128)(2,1)} %add_convert_fusion.refs_0_), channel_id=1, source_target_pairs={{0,8},{8,0},{16,24},{24,16},{1,9},{9,1},{17,25},{25,17},{2,10},{10... | collective-permute-start | bytes 12976136 | tf_op jit(solution)/shard_map/ppermute | solution.py:67
  806.9 128.2 %collective-permute-start.25 = (bf16[256,1024]{1,0:T(8,128)(2,1)}, bf16[256,1024]{1,0:T(8,128)(2,1)}, u32[]{:S(2)}, u32[]{:S(2)}) collective-permute-start(bf16[256,1024]{1,0:T(8,128)(2,1)} %add_convert_fusion.19), channel_id=1, source_target_pairs={{0,16},{8,24},{16,0},{24,8},{1,17},{9,25},{17,1},{25,9},{2,18},{10... | collective-permute-start | bytes 1572872 | tf_op jit(solution)/shard_map/ppermute | solution.py:62
  807.5 91.1 %copy-start.50 = (f32[160]{0:T(256)S(1)}, f32[160]{0:T(256)}, u32[]{:S(2)}) copy-start(f32[160]{0:T(256)} %add_rsqrt_fusion) | copy-start | bytes 1924
  807.5 204.3 %collective-permute-start.32 = (bf16[2,3,352,1024]{3,2,1,0:T(8,128)(2,1)}, bf16[2,3,352,1024]{3,2,1,0:T(8,128)(2,1)}, u32[]{:S(2)}, u32[]{:S(2)}) collective-permute-start(bf16[2,3,352,1024]{3,2,1,0:T(8,128)(2,1)} %get-tuple-element.127.refs_1_), channel_id=1, source_target_pairs={{0,8},{8,0},{16,24},{24,16},{1,9},{9,1},{17,25},{25,17},{2,10},{10... | collective-permute-start | bytes 12976136 | tf_op jit(solution)/shard_map/ppermute | solution.py:67
  898.6 113.2 %collective-permute-start.31 = (bf16[2,3,352,1024]{3,2,1,0:T(8,128)(2,1)}, bf16[2,3,352,1024]{3,2,1,0:T(8,128)(2,1)}, u32[]{:S(2)}, u32[]{:S(2)}) collective-permute-start(bf16[2,3,352,1024]{3,2,1,0:T(8,128)(2,1)} %add_convert_fusion.3.refs_0_), channel_id=1, source_target_pairs={{0,8},{8,0},{16,24},{24,16},{1,9},{9,1},{17,25},{25,17},{2,10},{10... | collective-permute-start | bytes 12976136 | tf_op jit(solution)/shard_map/ppermute | solution.py:67
  924.2 5.0 collective-permute-start.11
  929.2 5.9 collective-permute-start.22
  935.2 18.2 %collective-permute-start.19 = (bf16[3,1024,256]{1,2,0:T(8,128)(2,1)}, bf16[3,1024,256]{1,2,0:T(8,128)(2,1)}, u32[]{:S(2)}, u32[]{:S(2)}) collective-permute-start(bf16[3,1024,256]{1,2,0:T(8,128)(2,1)} %add_convert_fusion.10), channel_id=1, source_target_pairs={{0,8},{8,0},{16,24},{24,16},{1,9},{9,1},{17,25},{25,17},{2,10},{10... | collective-permute-start | bytes 4718600 | tf_op jit(solution)/shard_map/ppermute | solution.py:67
  935.2 8.5 collective-permute-start.12
  943.6 2.5 collective-permute-start.26
  946.1 2.3 collective-permute-start.13
  948.4 4.3 collective-permute-start.14
  952.7 12.5 %collective-permute-start.15 = (f32[11,1024]{1,0:T(8,128)S(1)}, f32[11,1024]{1,0:T(8,128)S(1)}, u32[]{:S(2)}, u32[]{:S(2)}) collective-permute-start(f32[11,1024]{1,0:T(8,128)S(1)} %slice_add_fusion.1), channel_id=1, source_target_pairs={{0,16},{8,24},{16,0},{24,8},{1,17},{9,25},{17,1},{25,9},{2,18},{10... | collective-permute-start | bytes 135176 | tf_op jit(solution)/shard_map/ppermute | solution.py:62
  (57 other events, 342.2 us)
Sparse Core Ops, SparseCore 0:
  139.3 54.1 all-gather.1
  656.6 48.4 reduce-scatter.1

commit v3 on v2

v3 whole, which is shorter than its diff:
```python
import functools

import jax
import jax.numpy as jnp
from jax import lax
from jax.experimental import pallas as pl
from jax.experimental.pallas import tpu as pltpu
from jax.sharding import PartitionSpec as P

HEAD_DIM = 128
EXPERTS = 8
LENGTH = 640
PIECE = 256
EPSILON = 1e-06
BF16 = jnp.bfloat16
F32 = jnp.float32
COLS = 256
MESH = pl.DeviceIdType.MESH
CHEAP = pl.CostEstimate(flops=1, bytes_accessed=1, transcendentals=0)


def rope_tables(length, head_dim):
    half_dim = head_dim // 2
    frequency = 1000000.0 ** (-jnp.arange(half_dim, dtype=F32) * (2.0 / head_dim))
    angles = jnp.arange(length, dtype=F32)[:, None] * frequency[None, :]
    return (jnp.cos(angles), jnp.sin(angles))


def after(value, *others):
    return lax.optimization_barrier((value,) + others)[0]


def swap_y(a):
    return lax.ppermute(a, "fsdp", [(0, 1), (1, 0)])


def swap_x(a):
    n = lax.axis_size("rep")
    return lax.ppermute(a, "rep", [(i, i ^ 2) for i in range(n)])


def swap_core(a):
    n = lax.axis_size("rep")
    return lax.ppermute(a, "rep", [(i, i ^ 1) for i in range(n)])


CHUNK = 16


def device(axis, index):
    return {axis: index}


def rows_kernel(
    n, rows, part_count, with_core_in, with_thin, with_scatter, with_gather, with_core_out, middle, extra_count, extra_out, bulk_count, *refs
):
    refs = list(refs)
    take = refs.pop
    parts = [take(0) for _ in range(part_count)]
    peer_parts = [take(0) for _ in range(part_count)] if with_core_in else None
    thin, thin_peer, thin_matrix = (take(0), take(0), take(0)) if with_thin else (None, None, None)
    extras = [take(0) for _ in range(extra_count)]
    bulk_src = [take(0) for _ in range(bulk_count)]
    outs = [take(0) for _ in range(extra_out)]
    full = take(0) if with_gather else None
    full_peer = take(0) if with_core_out else None
    bulk_dst = [take(0) for _ in range(bulk_count)]
    chunks = rows // CHUNK
    z = lax.axis_index("tensor")
    r = lax.axis_index("rep")
    core = r + 1 - 2 * lax.rem(r, 2)
    has_left, has_right = z > 0, z < n - 1
    pairs = with_core_in or with_core_out
    if bulk_count:
        bulk_send, bulk_recv = take(0), take(0)
    if with_core_in:
        core_src, core_buf, core_in_send, core_in_recv = take(0), take(0), take(0), take(0)
    if with_scatter:
        in_bufs, out_bufs = (take(0), take(0)), (take(0), take(0))
        sc_send, sc_recv = take(0), take(0)
    if with_gather:
        ga_send, ga_recv = take(0), take(0)
    if with_core_out:
        core_out_send, core_out_recv = take(0), take(0)

    barrier = pltpu.get_barrier_semaphore()

    @pl.when(has_left)
    def _():
        pl.semaphore_signal(barrier, inc=1, device_id=device("tensor", z - 1), device_id_type=MESH)

    @pl.when(has_right)
    def _():
        pl.semaphore_signal(barrier, inc=1, device_id=device("tensor", z + 1), device_id_type=MESH)

    if pairs:
        pl.semaphore_signal(barrier, inc=1, device_id=device("rep", core), device_id_type=MESH)
    across = r + 2 - 4 * (r // 2)
    if bulk_count:
        pl.semaphore_signal(barrier, inc=1, device_id=device("rep", across), device_id_type=MESH)
    greeted = jnp.where(has_left, 1, 0) + jnp.where(has_right, 1, 0) + int(pairs) + int(bulk_count > 0)
    pl.semaphore_wait(barrier, greeted)

    def chunk_at(block, i):
        return pl.ds(pl.multiple_of(block * rows + i * CHUNK, CHUNK), CHUNK)

    def chunk_in(i):
        return pl.ds(pl.multiple_of(i * CHUNK, CHUNK), CHUNK)

    def remote(src, dst, send, recv, axis, index):
        return pltpu.make_async_remote_copy(
            src_ref=src, dst_ref=dst, send_sem=send, recv_sem=recv,
            device_id=device(axis, index), device_id_type=MESH,
        )

    def bulk_copy(k):
        return remote(bulk_src[k], bulk_dst[k], bulk_send.at[k], bulk_recv.at[k], "rep", across)

    for k in range(bulk_count):
        bulk_copy(k).start()

    def core_in_copy(block, i):
        here = chunk_at(block, i)
        return remote(
            core_src.at[here], core_buf.at[here], core_in_send.at[block, i], core_in_recv.at[block, i], "rep", core
        )

    def scatter_copy(way, m, i):
        here = chunk_in(i)
        return remote(
            out_bufs[way].at[m, here], in_bufs[way].at[m, here], sc_send.at[way, m, i], sc_recv.at[way, m, i],
            "tensor", z + 1 - 2 * way,
        )

    def gather_copy(way, k, i):
        here = chunk_at(z - k + 2 * k * way, i)
        return remote(
            full.at[here], full.at[here], ga_send.at[way, k, i], ga_recv.at[way, k, i], "tensor", z + 1 - 2 * way
        )

    def core_out_copy(block, i):
        here = chunk_at(block, i)
        return remote(
            full.at[here], full_peer.at[here], core_out_send.at[block, i], core_out_recv.at[block, i], "rep", core
        )

    def all_chunks(body):
        def step(i, carry):
            body(i)
            return carry

        lax.fori_loop(0, chunks, step, 0)

    def sum_terms(arrays, small, here):
        value = arrays[0][here, :].astype(F32)
        for more in arrays[1:]:
            value = value + more[here, :].astype(F32)
        if with_thin:
            value = value + dot_nn(small[here, :], thin_matrix[...])
        return value

    def core_in_step(i):
        @pl.when(i < chunks)
        def _():
            for block in range(n):
                here = chunk_at(block, i)
                core_src[here, :] = sum_terms(peer_parts, thin_peer, here).astype(BF16)
                core_in_copy(block, i).start()

    ahead = 2
    if with_core_in:
        for i in range(ahead):
            core_in_step(i)

    def term(block, i):
        here = chunk_at(block, i)
        value = sum_terms(parts, thin, here)
        if with_core_in:
            core_in_copy(block, i).wait_recv()
            value = value + core_buf[here, :].astype(F32)
        return value

    def inside(i):
        return (i >= 0) & (i < chunks)

    def scatter_step(way, i, has_source, does_send):
        for m in range(n - 1):
            scatter_message(way, m, i - m, has_source, does_send(n - 1 - m if way == 0 else m))

    def scatter_message(way, m, i, has_source, does_send):
        block = n - 1 - m if way == 0 else m
        here = chunk_in(i)

        @pl.when(inside(i) & does_send)
        def _():
            value = term(block, i)

            @pl.when(has_source)
            def _():
                scatter_copy(way, m, i).wait_recv()
                out_bufs[way][m, here, :] = (value + in_bufs[way][m, here, :].astype(F32)).astype(BF16)

            @pl.when(jnp.logical_not(has_source))
            def _():
                out_bufs[way][m, here, :] = value.astype(BF16)

            scatter_copy(way, m, i).start()

    def own_step(i):
        @pl.when(inside(i))
        def _():
            here = chunk_in(i)
            if with_scatter:
                total[...] = term(z, i)

                @pl.when(has_left)
                def _():
                    m = n - 1 - z
                    scatter_copy(0, m, i).wait_recv()
                    total[...] += in_bufs[0][m, here, :].astype(F32)

                @pl.when(has_right)
                def _():
                    scatter_copy(1, z, i).wait_recv()
                    total[...] += in_bufs[1][z, here, :].astype(F32)

                sent = middle(total[...], here, extras, outs)
            else:
                sent = parts[0][here, :]
            if with_gather:
                full[chunk_at(z, i), :] = sent

                @pl.when(has_right)
                def _():
                    gather_copy(0, 0, i).start()

                @pl.when(has_left)
                def _():
                    gather_copy(1, 0, i).start()

                if with_core_out:
                    core_out_copy(z, i).start()

    def gather_step(k, i):
        for way in range(2):
            comes = z - k >= 0 if way == 0 else z + k <= n - 1
            goes = has_right if way == 0 else has_left

            @pl.when(inside(i) & comes)
            def _():
                landed = full.at[chunk_at(z - k + 2 * k * way, i)]
                remote(
                    landed, landed, ga_send.at[way, k - 1, i], ga_recv.at[way, k - 1, i], "tensor", z + 1 - 2 * way
                ).wait_recv()
                if k < n - 1:

                    @pl.when(goes)
                    def _():
                        gather_copy(way, k, i).start()

                if with_core_out:
                    core_out_copy(z - k + 2 * k * way, i).start()

    lead = n - 1 if with_scatter else 0
    if with_scatter:
        total = take(0)

    def tick(t, carry):
        if with_core_in:
            core_in_step(t + ahead)
        if with_scatter:
            scatter_step(0, t - z, has_left, lambda block: block > z)
            scatter_step(1, t - (n - 1 - z), has_right, lambda block: block < z)
        own_step(t - lead)
        if with_gather:
            for k in range(1, n):
                gather_step(k, t - lead - k)
        return carry

    lax.fori_loop(0, chunks + lead + (n - 1 if with_gather else 0), tick, 0)

    @all_chunks
    def _(i):
        if with_core_in:
            for block in range(n):
                core_in_copy(block, i).wait_send()
        for way in range(2):
            goes = has_right if way == 0 else has_left
            if with_scatter:
                for m in range(n - 1):
                    block = n - 1 - m if way == 0 else m

                    @pl.when(goes & ((block > z) if way == 0 else (block < z)))
                    def _():
                        scatter_copy(way, m, i).wait_send()

            if with_gather:
                for k in range(n - 1):
                    has = z - k >= 0 if way == 0 else z + k <= n - 1

                    @pl.when(goes & has)
                    def _():
                        gather_copy(way, k, i).wait_send()

        if with_core_out:
            for block in range(n):
                core_out_copy(block, i).wait_send()
                core_out_copy(block, i).wait_recv()

    for k in range(bulk_count):
        bulk_copy(k).wait()


def rows_call(
    collective_id, parts, peer_parts=(), thin=(), extras=(), bulk=(), scatter=True, gather=True, core_out=False, middle=None,
    out_types=(),
):
    n = lax.axis_size("tensor")
    width = parts[0].shape[1]
    rows = parts[0].shape[0] // n if scatter else parts[0].shape[0]
    chunks = rows // CHUNK
    vmem_spec = pl.BlockSpec(memory_space=pltpu.VMEM)
    full = jax.ShapeDtypeStruct((n * rows, width), BF16)
    out_shape = list(out_types) + ([full] if gather else []) + ([full] if core_out else [])
    vmem_outs = len(out_shape)
    out_shape += [jax.ShapeDtypeStruct(a.shape, a.dtype) for a in bulk]
    any_spec = pl.BlockSpec(memory_space=pl.ANY)
    scratch = [pltpu.SemaphoreType.DMA((len(bulk),))] * 2 if bulk else []
    if peer_parts:
        scratch += [pltpu.VMEM((n * rows, width), BF16)] * 2 + [pltpu.SemaphoreType.DMA((n, chunks))] * 2
    if scatter:
        scratch += [pltpu.VMEM((n - 1, rows, width), BF16)] * 4
        scratch += [pltpu.SemaphoreType.DMA((2, n - 1, chunks))] * 2
    if gather:
        scratch += [pltpu.SemaphoreType.DMA((2, n - 1, chunks))] * 2
    if core_out:
        scratch += [pltpu.SemaphoreType.DMA((n, chunks))] * 2
    if scatter:
        scratch += [pltpu.VMEM((CHUNK, width), F32)]
    operands = [*parts, *peer_parts, *thin, *extras]
    vmem_ins = len(operands)
    operands += list(bulk)
    return pl.pallas_call(
        functools.partial(
            rows_kernel, n, rows, len(parts), bool(peer_parts), bool(thin), scatter, gather, core_out, middle, len(extras), len(out_types), len(bulk)
        ),
        out_shape=out_shape,
        in_specs=[vmem_spec] * vmem_ins + [any_spec] * len(bulk),
        out_specs=[vmem_spec] * vmem_outs + [any_spec] * len(bulk),
        scratch_shapes=scratch,
        compiler_params=pltpu.CompilerParams(
            collective_id=collective_id, has_side_effects=True, vmem_limit_bytes=56 * 2**20
        ),
        cost_estimate=CHEAP,
        name="rows",
    )(*operands)


def norm_middle(total, here, extras, outs):
    inputs, gain = extras
    hidden = inputs[here, :].astype(F32) + total
    outs[0][here, :] = hidden
    inverse = lax.rsqrt(jnp.mean(hidden * hidden, axis=-1, keepdims=True) + EPSILON)
    return (hidden * inverse * gain[...]).astype(BF16)


def norm_back_middle(total, here, extras, outs):
    hidden_ref, cot, gain = extras
    hidden = hidden_ref[here, :]
    inverse = lax.rsqrt(jnp.mean(hidden * hidden, axis=-1, keepdims=True) + EPSILON)
    scaled = total * gain[...]
    grad = cot[here, :].astype(F32) + inverse * (
        scaled - hidden * inverse * inverse * jnp.mean(scaled * hidden, axis=-1, keepdims=True)
    )
    outs[0][here, :] = total
    outs[1][here, :] = grad
    return grad.astype(BF16)


def plain_middle(total, here, extras, outs):
    outs[0][here, :] = total


def others_of(own, f, axis):
    if lax.axis_size("fsdp") == 2:
        return swap_y(own)
    whole = lax.all_gather(own, "fsdp", axis=axis, tiled=True)
    size = own.shape[axis]
    turned = jnp.roll(whole, -f * size, axis=axis)
    return lax.slice_in_dim(turned, size, whole.shape[axis], axis=axis)


def reduce_fsdp(own, other, f, axis, add):
    if lax.axis_size("fsdp") == 2:
        return add(own, swap_y(other))
    whole = jnp.roll(jnp.concatenate([own, other], axis=axis), f * own.shape[axis], axis=axis)
    return lax.psum_scatter(whole, "fsdp", scatter_dimension=axis, tiled=True)


def sum_small(values, per_tensor, f, shard):
    total = sum_rep_first(jnp.concatenate([sum_tensor(values), per_tensor], axis=0))
    if lax.axis_size("fsdp") == 2:
        total = total[:, :shard] + swap_y(total[:, shard:])
    else:
        whole = jnp.roll(total, f * shard, axis=1)
        total = lax.psum_scatter(whole, "fsdp", scatter_dimension=1, tiled=True)
    return total


def sum_rep_first(total):
    return total + swap_core(total)


def sum_tensor(total):
    n = lax.axis_size("tensor")
    step = 1
    while step < n:
        total = total + lax.ppermute(total, "tensor", [(i, i ^ step) for i in range(n)])
        step *= 2
    return total


def dot_nt(a, b):
    return lax.dot_general(a, b, (((1,), (1,)), ((), ())), preferred_element_type=F32)


def dot_nn(a, b):
    return lax.dot_general(a, b, (((1,), (0,)), ((), ())), preferred_element_type=F32)


def mask_rows(starts, length):
    key = lax.broadcasted_iota(jnp.int32, (length, length), 0)
    query = lax.broadcasted_iota(jnp.int32, (length, length), 1)
    visible = key <= query
    for piece in range(2):
        first = starts[0, piece]
        visible |= (jnp.minimum(key, query) >= first) & (jnp.maximum(key, query) < first + PIECE)
    return jnp.where(visible, 0.0, -1e30).astype(F32)


def attend_kernel(
    heads, own_width, starts, rows, w_own, w_oth, bias, cos, sin, out_own, out_oth,
    q_out, k_out, v_out, attended, stats, part, mask,
):
    length = rows.shape[0]
    scale = HEAD_DIM ** (-0.5)
    for c, out in ((0, q_out), (1, k_out), (2, v_out)):
        project = dot_nn(rows[:, :own_width], w_own[c]) + dot_nn(rows[:, own_width:], w_oth[c]) + bias[c : c + 1, :]
        for h in range(heads):
            here = slice(h * HEAD_DIM, (h + 1) * HEAD_DIM)
            values = project[:, here]
            if c < 2:
                values = values * cos[...] + pltpu.roll(values, HEAD_DIM // 2, 1) * sin[...]
            out[:, here] = values.astype(BF16)
    mask[...] = mask_rows(starts, length)

    def one_head(h, carry):
        here = pl.ds(pl.multiple_of(h * HEAD_DIM, HEAD_DIM), HEAD_DIM)
        scores = dot_nt(k_out[:, here], q_out[:, here]) * scale + mask[...]
        top = jnp.max(scores, axis=0, keepdims=True)
        weights = jnp.exp(scores - top)
        inverse = 1.0 / jnp.sum(weights, axis=0, keepdims=True)
        probs = (weights * inverse).astype(BF16)
        attended[:, here] = dot_nn(v_out[:, here].T, probs).T.astype(BF16)
        stats[pl.ds(h, 1), :] = top
        stats[pl.ds(heads + h, 1), :] = inverse
        return carry

    lax.fori_loop(0, heads, one_head, 0)
    part[:, :own_width] = dot_nn(attended[...], out_own[...]).astype(BF16)
    part[:, own_width:] = dot_nn(attended[...], out_oth[...]).astype(BF16)


def attend_back_kernel(
    heads, own_width, starts, grad, w_own, w_oth, cos, sin, out_own, out_oth, q, k, v, stats,
    project_grad, bias_grad, rows_grad, mask, attended_grad,
):
    length = grad.shape[0]
    scale = HEAD_DIM ** (-0.5)
    attended_grad[...] = (
        dot_nt(grad[:, :own_width], out_own[...]) + dot_nt(grad[:, own_width:], out_oth[...])
    ).astype(BF16)
    mask[...] = mask_rows(starts, length)

    def turn_back(values):
        return values * cos[...] - pltpu.roll(values, HEAD_DIM // 2, 1) * sin[...]

    def one_head(h, carry):
        here = pl.ds(pl.multiple_of(h * HEAD_DIM, HEAD_DIM), HEAD_DIM)
        queries, keys, grads = q[:, here], k[:, here], attended_grad[:, here]
        scores = dot_nt(keys, queries) * scale + mask[...]
        probs = jnp.exp(scores - stats[pl.ds(h, 1), :]) * stats[pl.ds(heads + h, 1), :]
        value_grad = dot_nn(probs.astype(BF16), grads)
        probs_grad = dot_nt(v[:, here], grads)
        mean = jnp.sum(probs * probs_grad, axis=0, keepdims=True)
        score_grad = (probs * (probs_grad - mean)).astype(BF16)
        key_grad = dot_nn(score_grad, queries) * scale
        query_grad = dot_nn(score_grad.T, keys) * scale
        project_grad[0, :, here] = turn_back(query_grad).astype(BF16)
        project_grad[1, :, here] = turn_back(key_grad).astype(BF16)
        project_grad[2, :, here] = value_grad.astype(BF16)
        return carry

    lax.fori_loop(0, heads, one_head, 0)
    total_own = total_oth = None
    for c in range(3):
        grads = project_grad[c]
        bias_grad[c : c + 1, :] = jnp.sum(grads.astype(F32), axis=0, keepdims=True)
        own, oth = dot_nt(grads, w_own[c]), dot_nt(grads, w_oth[c])
        total_own = own if c == 0 else total_own + own
        total_oth = oth if c == 0 else total_oth + oth
    rows_grad[:, :own_width] = total_own.astype(BF16)
    rows_grad[:, own_width:] = total_oth.astype(BF16)


def attention_call(kernel, name, operands, out_shape, heads, own_width, length, more_scratch=()):
    vmem_spec = pl.BlockSpec(memory_space=pltpu.VMEM)
    return pl.pallas_call(
        functools.partial(kernel, heads, own_width),
        out_shape=out_shape,
        in_specs=[pl.BlockSpec(memory_space=pltpu.SMEM)] + [vmem_spec] * (len(operands) - 1),
        out_specs=[vmem_spec] * len(out_shape),
        scratch_shapes=[pltpu.VMEM((length, length), F32), *more_scratch],
        cost_estimate=CHEAP,
        compiler_params=pltpu.CompilerParams(vmem_limit_bytes=56 * 2**20),
        name=name,
    )(*operands)


def experts_kernel(rows, width, own_width, hidden, direct, *refs):
    if direct:
        first, x0, x1, c0, c1, gate, gate_up, down, w_oth, *refs = refs
    else:
        x0, x1, c0, c1, gate, w_own, w_oth, *refs = refs
    dw_own, dw_oth, mix0, mix1, ng0, ng1, gate_grad, *refs = refs
    xv, cv, wgu, wd, ga, pre, ga_t, pre_t, st_mix, st_ng, st_dw, w_sem, x_sem, c_sem, out_sem, dw_sem = refs
    seq = rows // 2
    both = 2 * hidden
    oth_width = width - own_width

    def w_copies(part):
        copies = []
        for k in range(2):
            if direct:
                own = gate_up.at[first[0] + k, part] if part < 2 else down.at[first[0] + k]
            else:
                own = w_own.at[k, part]
            to = wd.at[pl.ds(k * hidden, hidden)] if part == 2 else wgu.at[pl.ds(part * both + k * hidden, hidden)]
            copies.append(pltpu.make_async_copy(own, to.at[:, pl.ds(0, own_width)], w_sem.at[part, k, 0]))
            copies.append(
                pltpu.make_async_copy(w_oth.at[k, part], to.at[:, pl.ds(own_width, oth_width)], w_sem.at[part, k, 1])
            )
        return copies

    def row_copies(sources, to, sem):
        return [
            pltpu.make_async_copy(sources[s], to.at[pl.ds(s * seq, seq)], sem.at[s]) for s in range(2)
        ]

    x_copies, c_copies = row_copies((x0, x1), xv, x_sem), row_copies((c0, c1), cv, c_sem)
    order = [x_copies[0], *w_copies(0), *w_copies(1), c_copies[0], *w_copies(2), x_copies[1], c_copies[1]]
    for copy in order:
        copy.start()
    for copy in order[:-2]:
        copy.wait()

    def token_tile(t, carry):
        @pl.when(t == seq // COLS)
        def _():
            x_copies[1].wait()
            c_copies[1].wait()

        here = pl.ds(pl.multiple_of(t * COLS, COLS), COLS)
        gu = dot_nt(wgu[...], xv[here, :])
        h = dot_nt(wd[...], cv[here, :])
        g, u = gu[:both], gu[both:]
        sig = jax.nn.sigmoid(g)
        act = g * sig * u
        product = act * h
        scale_rows = []
        for k in range(2):
            part = product[k * hidden : (k + 1) * hidden]
            gate_grad[pl.ds(k, 1), here] = jnp.sum(part, axis=0, keepdims=True)
            scale_rows.append(jnp.broadcast_to(gate[pl.ds(k, 1), here], (hidden, COLS)))
        scale = jnp.concatenate(scale_rows, axis=0)
        back = scale * h
        ga_here = (scale * act).astype(BF16)
        pg_here = (back * u * sig * (1.0 + g * (1.0 - sig))).astype(BF16)
        pu_here = (back * g * sig).astype(BF16)
        ga[:, here] = ga_here
        pre[:both, here] = pg_here
        pre[both:, here] = pu_here
        ga_t[here, :] = ga_here.T
        pre_t[here, :both] = pg_here.T
        pre_t[here, both:] = pu_here.T
        return carry

    lax.fori_loop(0, rows // COLS, token_tile, 0)

    def row_outs(slot, cols):
        return [
            pltpu.make_async_copy(stage.at[slot, pl.ds(s * seq, seq)], outs[s].at[:, cols], out_sem.at[slot, i, s])
            for i, (stage, outs) in enumerate(((st_mix, (mix0, mix1)), (st_ng, (ng0, ng1))))
            for s in range(2)
        ]

    def weight_outs(slot, dst, cols):
        return [
            pltpu.make_async_copy(
                st_dw.at[slot, pl.ds((part * 2 + k) * hidden, hidden)], dst.at[k, part, :, cols], dw_sem.at[slot, part, k]
            )
            for part in range(3)
            for k in range(2)
        ]

    def wait_slot(slot):
        for copy in row_outs(slot, pl.ds(0, COLS)) + weight_outs(slot, dw_own, pl.ds(0, COLS)):
            copy.wait()

    def column_tile(n, slot, src_col, dst, dst_col):
        cols = pl.ds(pl.multiple_of(src_col, COLS), COLS)

        @pl.when(n >= 2)
        def _():
            wait_slot(slot)

        st_dw[slot, : 2 * both] = dot_nn(pre[...], xv[:, cols]).astype(BF16)
        st_dw[slot, 2 * both :] = dot_nn(ga[...], cv[:, cols]).astype(BF16)
        for copy in weight_outs(slot, dst, pl.ds(pl.multiple_of(dst_col, COLS), COLS)):
            copy.start()
        st_ng[slot] = dot_nn(pre_t[...], wgu[:, cols]).astype(BF16)
        st_mix[slot] = dot_nn(ga_t[...], wd[:, cols]).astype(BF16)
        for copy in row_outs(slot, cols):
            copy.start()

    oth_tiles, own_tiles = oth_width // COLS, own_width // COLS

    def oth_tile(n, carry):
        column_tile(n, lax.rem(n, 2), own_width + n * COLS, dw_oth, n * COLS)
        return carry

    def own_tile(n, carry):
        column_tile(n + oth_tiles, lax.rem(n + oth_tiles, 2), n * COLS, dw_own, n * COLS)
        return carry

    lax.fori_loop(0, oth_tiles, oth_tile, 0)
    lax.fori_loop(0, own_tiles, own_tile, 0)
    for slot in range(2):
        wait_slot(slot)


def experts_call(x0, x1, c0, c1, gate, w_own, w_oth):
    direct = isinstance(w_own, tuple)
    seq, width = x0.shape
    rows = 2 * seq
    hidden, own_width = (w_own[1] if direct else w_own).shape[2:]
    smem_spec = pl.BlockSpec(memory_space=pltpu.SMEM)
    own_operands = w_own[1:] if direct else (w_own,)
    any_spec = pl.BlockSpec(memory_space=pl.ANY)
    vmem_spec = pl.BlockSpec(memory_space=pltpu.VMEM)
    out_rows = jax.ShapeDtypeStruct((seq, width), BF16)
    return pl.pallas_call(
        functools.partial(experts_kernel, rows, width, own_width, hidden, direct),
        out_shape=[
            jax.ShapeDtypeStruct((2, 3, hidden, own_width), BF16),
            jax.ShapeDtypeStruct((2, 3, hidden, width - own_width), BF16),
            out_rows, out_rows, out_rows, out_rows,
            jax.ShapeDtypeStruct((8, rows), F32),
        ],
        in_specs=[smem_spec] * direct + [any_spec] * 4 + [vmem_spec] + [any_spec] * (len(own_operands) + 1),
        out_specs=[any_spec] * 6 + [vmem_spec],
        scratch_shapes=[
            pltpu.VMEM((rows, width), BF16),
            pltpu.VMEM((rows, width), BF16),
            pltpu.VMEM((4 * hidden, width), BF16),
            pltpu.VMEM((2 * hidden, width), BF16),
            pltpu.VMEM((2 * hidden, rows), BF16),
            pltpu.VMEM((4 * hidden, rows), BF16),
            pltpu.VMEM((rows, 2 * hidden), BF16),
            pltpu.VMEM((rows, 4 * hidden), BF16),
            pltpu.VMEM((2, rows, COLS), BF16),
            pltpu.VMEM((2, rows, COLS), BF16),
            pltpu.VMEM((2, 6 * hidden, COLS), BF16),
            pltpu.SemaphoreType.DMA((3, 2, 2)),
            pltpu.SemaphoreType.DMA((2,)),
            pltpu.SemaphoreType.DMA((2,)),
            pltpu.SemaphoreType.DMA((2, 2, 2)),
            pltpu.SemaphoreType.DMA((2, 3, 2)),
        ],
        cost_estimate=CHEAP,
        compiler_params=pltpu.CompilerParams(vmem_limit_bytes=58 * 2**20),
        name="experts",
    )(*([w_own[0]] if direct else []), x0, x1, c0, c1, gate, *own_operands, w_oth)


def sum_kernel(*refs):
    total = refs[0][...].astype(F32)
    for ref in refs[1:-1]:
        total = total + ref[...].astype(F32)
    refs[-1][...] = total.astype(BF16)


def sum_call(arrays, steps, flip=-1):
    rows, columns = arrays[0].shape
    block = (rows // steps, columns)

    def spec(k):
        if k == flip:
            return pl.BlockSpec(block, lambda i: (lax.rem(i + steps // 2, steps), 0))
        return pl.BlockSpec(block, lambda i: (i, 0))

    return pl.pallas_call(
        sum_kernel,
        out_shape=jax.ShapeDtypeStruct((rows, columns), BF16),
        grid=(steps,),
        in_specs=[spec(k) for k in range(len(arrays))],
        out_specs=spec(-2),
        cost_estimate=CHEAP,
        compiler_params=pltpu.CompilerParams(vmem_limit_bytes=40 * 2**20),
        name="sums",
    )(*arrays)


def add_experts(one, two, flip=False):
    flat = [a.reshape(-1, a.shape[-1]) for a in (one, two)]
    return sum_call(flat, 4, 1 if flip else -1).reshape(one.shape)


def dense_kernel(half, own_width, core, rows, project_grad, attended, branch_grad, *outs):
    qkv_own, qkv_oth, qkv_send, out_own, out_oth, out_send, rows_t = outs
    rows_t[...] = rows[...].T
    for keep in (False, True):
        cols = pl.ds(pl.multiple_of((core[0] if keep else 1 - core[0]) * half, half), half)
        for c in range(3):
            grad = dot_nn(rows_t[...], project_grad[c, :, cols]).astype(BF16)
            if keep:
                qkv_own[c] = grad[:own_width]
                qkv_oth[c] = grad[own_width:]
            else:
                qkv_send[c] = grad
        grad = dot_nn(attended[:, cols].T, branch_grad[...]).astype(BF16)
        if keep:
            out_own[...] = grad[:, :own_width]
            out_oth[...] = grad[:, own_width:]
        else:
            out_send[...] = grad


def dense_call(core, rows, project_grad, attended, branch_grad, own_width):
    length, width = rows.shape
    half = attended.shape[1] // 2
    vmem_spec = pl.BlockSpec(memory_space=pltpu.VMEM)
    shapes = [(3, own_width, half), (3, width - own_width, half), (3, width, half)]
    shapes += [(half, own_width), (half, width - own_width), (half, width)]
    return pl.pallas_call(
        functools.partial(dense_kernel, half, own_width),
        out_shape=[jax.ShapeDtypeStruct(shape, BF16) for shape in shapes],
        in_specs=[pl.BlockSpec(memory_space=pltpu.SMEM)] + [vmem_spec] * 4,
        out_specs=[vmem_spec] * 6,
        scratch_shapes=[pltpu.VMEM((width, length), BF16)],
        cost_estimate=CHEAP,
        compiler_params=pltpu.CompilerParams(vmem_limit_bytes=48 * 2**20),
        name="dense_grads",
    )(core, rows, project_grad, attended, branch_grad)


def place_kernel(table, mine, peer, *refs):
    out = refs[-1]
    which = table[1, pl.program_id(0)]

    @pl.when(which == 0)
    def _():
        out[...] = mine[...].astype(F32)

    @pl.when(which == 1)
    def _():
        out[...] = peer[...].astype(F32)


def place_call(mine, peer, c, first, parts, base=None):
    at, length = parts
    hidden, width = mine.shape[2:]
    half = EXPERTS // 2
    step = jnp.arange(4, dtype=jnp.int32)
    which = (step // 2 != c).astype(jnp.int32)

    def blocks(own_half):
        return jnp.clip(step - 2 * own_half, 0, 1)

    table = jnp.stack([step // 2 * half + first + step % 2, which, blocks(c), blocks(1 - c)]).astype(jnp.int32)

    def source(row):
        return pl.BlockSpec((1, length, hidden, width), lambda e, tab: (tab[row, e], at // length, 0, 0))

    return pl.pallas_call(
        place_kernel,
        out_shape=jax.ShapeDtypeStruct((EXPERTS, length, hidden, width), F32),
        grid_spec=pltpu.PrefetchScalarGridSpec(
            num_scalar_prefetch=1,
            grid=(4,),
            in_specs=[source(2), source(3)] + [pl.BlockSpec(memory_space=pl.ANY)] * (base is not None),
            out_specs=pl.BlockSpec((1, length, hidden, width), lambda e, tab: (tab[0, e], 0, 0, 0)),
        ),
        input_output_aliases={} if base is None else {3: 0},
        cost_estimate=CHEAP,
        compiler_params=pltpu.CompilerParams(vmem_limit_bytes=40 * 2**20),
        name="place",
    )(table, mine, peer, *([] if base is None else [base]))


def shared_kernel(table, mine, peer, up, down):
    def quarter(q, part):
        block = table[q]
        return jnp.where(table[4 + q] == 0, mine[block, part].astype(F32), peer[block, part].astype(F32))

    for part in range(2):
        up[:, part, :] = jnp.concatenate([quarter(q, part) for q in range(4)], axis=0).T
    down[...] = jnp.concatenate([quarter(q, 2) for q in range(4)], axis=0)


def shared_call(mine, peer, c, x):
    hidden, width = mine.shape[2:]
    q = jnp.arange(4, dtype=jnp.int32)
    table = jnp.concatenate([(q % 2) ^ x, (q // 2 != c).astype(jnp.int32)]).astype(jnp.int32)
    source = pl.BlockSpec((2, 3, hidden, 128), lambda n, tab: (0, 0, 0, n))
    return pl.pallas_call(
        shared_kernel,
        out_shape=[
            jax.ShapeDtypeStruct((width, 2, 4 * hidden), F32),
            jax.ShapeDtypeStruct((4 * hidden, width), F32),
        ],
        grid_spec=pltpu.PrefetchScalarGridSpec(
            num_scalar_prefetch=1,
            grid=(width // 128,),
            in_specs=[source, source],
            out_specs=[
                pl.BlockSpec((128, 2, 4 * hidden), lambda n, tab: (n, 0, 0)),
                pl.BlockSpec((4 * hidden, 128), lambda n, tab: (0, n)),
            ],
        ),
        cost_estimate=CHEAP,
        compiler_params=pltpu.CompilerParams(vmem_limit_bytes=40 * 2**20),
        name="shared",
    )(table, mine, peer)


def shards(
    block_input,
    cotangent,
    piece_starts,
    expert_ids,
    norm_gains,
    qkv_weight,
    qkv_bias,
    out_weight,
    router_weight,
    shared_gate,
    expert_gate_up,
    expert_down,
    shared_gate_up,
    shared_down,
):
    f = lax.axis_index("fsdp")
    owners = lax.axis_size("fsdp")
    r = lax.axis_index("rep")
    c, x = r % 2, r // 2
    shard = norm_gains.shape[1]
    width = owners * shard
    local_width = qkv_weight.shape[2]
    local_heads = local_width // HEAD_DIM
    half_width = local_width // 2
    hidden = expert_gate_up.shape[3]
    scale = HEAD_DIM ** (-0.5)

    def turn(rows):
        return jnp.roll(rows, -f * shard, axis=1)

    def turn_back(rows):
        return jnp.roll(rows, f * shard, axis=1)

    small = jnp.concatenate(
        [norm_gains.reshape(-1), router_weight.T.reshape(-1), shared_gate, qkv_bias.reshape(-1)]
    )
    small_all = jnp.concatenate([small[None], others_of(small[None], f, 0)], axis=0)
    gains = jnp.swapaxes(small_all[:, : 2 * shard].reshape(owners, 2, shard), 0, 1).reshape(2, width)
    gains = gains.astype(F32)
    router = jnp.swapaxes(
        small_all[:, 2 * shard : 11 * shard].reshape(owners, 9, shard), 0, 1
    ).reshape(9, width)
    bias = jnp.roll(small_all[:, 11 * shard :], f, axis=0).reshape(owners, 3, local_heads, -1)
    bias = jnp.moveaxis(bias, 0, 2).reshape(3, local_width).astype(F32)
    cos_table, sin_table = rope_tables(LENGTH, HEAD_DIM)
    inputs = turn(block_input)
    inputs_f = inputs.astype(F32)
    cot = turn(cotangent)
    inverse_one = lax.rsqrt(jnp.mean(inputs_f * inputs_f, axis=-1, keepdims=True) + EPSILON)
    normed_local = (inputs_f * inverse_one * gains[0]).astype(BF16)
    normed = lax.all_gather(normed_local, "tensor", axis=0, tiled=True)
    gate_up_t = jnp.transpose(after(expert_gate_up, normed_local), (0, 2, 3, 1))

    quarter = local_width // 4

    def fetch_quarters(weight, hidden_axis, shard_axis):
        mine = lax.dynamic_slice_in_dim(weight, r * quarter, quarter, hidden_axis)
        got = others_of(mine, f, shard_axis)
        pair = jnp.stack([got, swap_x(got)])
        peers = swap_core(pair)
        pair = jnp.where(x == 0, pair, pair[::-1])
        peers = jnp.where(x == 0, peers, peers[::-1])
        order = jnp.where(c == 0, jnp.stack([pair, peers], 1), jnp.stack([peers, pair], 1))
        return jnp.concatenate([order[i, j] for i in range(2) for j in range(2)], axis=hidden_axis), got

    qkv_oth, qkv_got = fetch_quarters(qkv_weight, 2, 1)
    out_oth, out_got = fetch_quarters(out_weight, 0, 1)


    def routed_chunk(first, gate_up_t):
        return jnp.concatenate(
            [
                lax.dynamic_slice_in_dim(gate_up_t, first, 2, 0),
                lax.dynamic_slice_in_dim(expert_down, first, 2, 0)[:, None],
            ],
            axis=1,
        )

    def shared_chunk(q, shared_up_t, shared_down):
        return jnp.concatenate(
            [
                lax.dynamic_slice_in_dim(shared_up_t, q * hidden, hidden, 1),
                lax.dynamic_slice_in_dim(shared_down, q * hidden, hidden, 0)[None],
            ],
            axis=0,
        )[None]

    first_a, first_b = 4 * c + 2 * x, 4 * c + 2 * (1 - x)
    shared_gate_up, shared_down, expert_ids = lax.optimization_barrier(
        (shared_gate_up, shared_down, expert_ids, normed_local)
    )[:3]
    ids_pair = jnp.concatenate([expert_ids, swap_core(expert_ids)], axis=0)
    shared_up_t = jnp.stack([shared_gate_up[:, 0].T, shared_gate_up[:, 1].T])
    own_s = jnp.concatenate([shared_chunk(q, shared_up_t, shared_down) for q in (2 * c + x, 2 * c + 1 - x)], axis=0)
    own_a = routed_chunk(first_a, after(gate_up_t, own_s))
    own_b = (jnp.reshape(first_b, (1,)).astype(jnp.int32), gate_up_t, expert_down)

    oth_a = others_of(after(own_a, qkv_got, out_got), f, 3)
    cos_rows = jnp.concatenate([cos_table, cos_table], axis=1)
    sin_rows = jnp.concatenate([-sin_table, sin_table], axis=1)
    normed = after(normed, own_s, ids_pair, cos_rows, sin_rows, bias, qkv_oth, out_oth)
    cot_rows = lax.all_gather(after(cot, normed), "tensor", axis=0, tiled=True)
    oth_s = others_of(after(own_s, normed), f, 3)

    heads_rows = jax.ShapeDtypeStruct((LENGTH, local_width), BF16)
    all_rows = jax.ShapeDtypeStruct((LENGTH, width), BF16)
    query_rows, key_rows, value_rows, attended, stats, heads_part = attention_call(
        attend_kernel,
        "attend",
        [piece_starts, normed, qkv_weight, qkv_oth, bias, cos_rows, sin_rows, out_weight, out_oth],
        [heads_rows] * 4 + [jax.ShapeDtypeStruct((2 * local_heads, LENGTH), F32), all_rows],
        local_heads,
        shard,
        LENGTH,
    )
    block_f32 = jax.ShapeDtypeStruct(inputs.shape, F32)
    hidden_rows, mixed, mixed_peer = rows_call(
        1, [heads_part], extras=(inputs, gains[1:2]), core_out=True, middle=norm_middle, out_types=[block_f32]
    )
    cot_rows = after(cot_rows, mixed)
    cot_peer = swap_core(cot_rows)
    oth_b = swap_x(after(oth_a, mixed))
    mixed_pair = jnp.concatenate([mixed, mixed_peer], axis=0)

    logits = lax.dot_general(router, mixed_pair, (((1,), (1,)), ((), ())), preferred_element_type=F32)
    router_probs = jax.nn.softmax(logits[:EXPERTS], axis=0)
    shared_scale = jax.nn.sigmoid(logits[EXPERTS:])
    names = jnp.arange(EXPERTS, dtype=jnp.int32)[:, None, None]
    chosen = jnp.any(ids_pair.T[None] == names, axis=1)
    gates = jnp.where(chosen, router_probs, 0.0)

    def gate_rows(first):
        return jnp.pad(lax.dynamic_slice_in_dim(gates, first, 2, 0), ((0, 6), (0, 0)))

    data = (mixed, mixed_peer, cot_rows, cot_peer)
    dw_own_a, dw_oth_a, *rows_a, grad_a = experts_call(*data, gate_rows(first_a), own_a, oth_a)
    shared_rows = after(jnp.broadcast_to(shared_scale, (8, shared_scale.shape[1])), grad_a)
    dw_own_s, dw_oth_s, *rows_s, grad_s = experts_call(*data, shared_rows, own_s, oth_s)
    dw_own_b, dw_oth_b, *rows_b, grad_b = experts_call(
        *data, after(gate_rows(first_b), grad_s), own_b, oth_b
    )

    prob_grad = jnp.zeros_like(router_probs)
    prob_grad = lax.dynamic_update_slice_in_dim(prob_grad, grad_a[:2], first_a, 0)
    prob_grad = lax.dynamic_update_slice_in_dim(prob_grad, grad_b[:2], first_b, 0)
    prob_grad = jnp.where(chosen, prob_grad, 0.0)
    logit_grad = router_probs * (prob_grad - jnp.sum(router_probs * prob_grad, axis=0, keepdims=True))
    scale_logit_grad = (grad_s[0:1] + grad_s[1:2]) * shared_scale * (1.0 - shared_scale)
    small_grad = jnp.concatenate([logit_grad, scale_logit_grad], axis=0)
    high = small_grad.astype(BF16)
    low = (small_grad - high.astype(F32)).astype(BF16)
    small_pair = jnp.concatenate([high, low], axis=0)
    router_both = jnp.dot(small_pair, mixed_pair, preferred_element_type=F32)
    router_grad = router_both[:9] + router_both[9:]
    thin = jnp.pad(small_pair, ((0, 128 - small_pair.shape[0]), (0, 0))).T
    thin_matrix = jnp.pad(jnp.concatenate([router, router], axis=0), ((0, 128 - small_pair.shape[0]), (0, 0)))

    def add(one, two):
        return (one.astype(F32) + two.astype(F32)).astype(BF16)

    def shard_sum(own, other):
        return reduce_fsdp(own, other, f, 3, add_experts)

    sum_a = shard_sum(dw_own_a, dw_oth_a)
    from_a = swap_x(sum_a)
    normed_two_grad, hidden_grad, branch_grad = rows_call(
        2,
        [after(rows_a[2], sum_a), rows_s[2], rows_b[2]],
        [rows_a[3], rows_s[3], rows_b[3]],
        [thin[:LENGTH], thin[LENGTH:], thin_matrix],
        extras=(hidden_rows, cot, gains[1:2]),
        middle=norm_back_middle,
        out_types=[block_f32, block_f32],
    )
    inverse_two = lax.rsqrt(jnp.mean(hidden_rows * hidden_rows, axis=-1, keepdims=True) + EPSILON)
    gain_two_grad = jnp.sum(normed_two_grad * hidden_rows * inverse_two, axis=0)

    sum_s = shard_sum(after(dw_own_s, branch_grad), dw_oth_s)
    branch_grad = after(branch_grad, sum_s)
    from_s = swap_x(sum_s)
    project_grad, bias_grad, normed_one_grad = attention_call(
        attend_back_kernel,
        "attend_back",
        [
            piece_starts, branch_grad, qkv_weight, qkv_oth, cos_rows, sin_rows, out_weight, out_oth,
            query_rows, key_rows, value_rows, stats,
        ],
        [
            jax.ShapeDtypeStruct((3, LENGTH, local_width), BF16),
            jax.ShapeDtypeStruct((3, local_width), F32),
            all_rows,
        ],
        local_heads,
        shard,
        LENGTH,
        [pltpu.VMEM((LENGTH, local_width), BF16)],
    )
    (input_row_grad,) = rows_call(
        3, [after(normed_one_grad, from_a)], gather=False, middle=plain_middle, out_types=[block_f32]
    )
    out_grad = jnp.einsum("lf,ld->fd", attended, branch_grad, preferred_element_type=F32).astype(BF16)
    sum_b = shard_sum(after(dw_own_b, input_row_grad), dw_oth_b)
    from_b = swap_x(sum_b)
    total_b = add_experts(sum_b, from_a)
    peer_b = swap_core(total_b)
    input_row_grad, project_grad, attended, branch_grad = lax.optimization_barrier(
        (input_row_grad, project_grad, attended, branch_grad, sum_b)
    )[:4]
    qkv_own, qkv_more, qkv_send, out_own, out_more, out_send = dense_call(
        jnp.reshape(c, (1,)).astype(jnp.int32), normed, project_grad, attended, branch_grad, shard
    )

    qkv_peer, out_peer = swap_core(qkv_send), swap_core(out_send)
    total_s = add_experts(after(sum_s, qkv_send, total_b), from_s, flip=True)
    peer_s = swap_core(total_s)

    def fsdp_part(own, more, peer, shard_axis):
        own, more, peer = lax.optimization_barrier((own, more, peer, total_s))[:3]
        more = add(more, lax.slice_in_dim(peer, shard, width, axis=shard_axis))
        own = add(own, lax.slice_in_dim(peer, 0, shard, axis=shard_axis))
        return reduce_fsdp(own, more, f, shard_axis, add), more

    (qkv_part, qkv_both), (out_part, out_both) = (
        fsdp_part(qkv_own, qkv_more, qkv_peer, 1),
        fsdp_part(out_own, out_more, out_peer, 1),
    )

    input_row_grad = after(input_row_grad, qkv_both, out_both)
    scaled_one = input_row_grad * gains[0]
    input_grad = hidden_grad + inverse_one * (
        scaled_one
        - inputs_f
        * inverse_one
        * inverse_one
        * jnp.mean(scaled_one * inputs_f, axis=-1, keepdims=True)
    )
    gain_one_grad = jnp.sum(input_row_grad * inputs_f * inverse_one, axis=0)

    mixes = [lax.optimization_barrier((row[0], row[1], qkv_send))[:2] for row in (rows_a, rows_s, rows_b)]
    mixer_peer = swap_core(sum_call([mix[1] for mix in mixes], 5))
    mixer = sum_call([mix[0] for mix in mixes] + [mixer_peer], 5)
    mixer_local = lax.psum_scatter(mixer, "tensor", scatter_dimension=0, tiled=True)

    per_shard = HEAD_DIM // owners
    bias_parts = jnp.moveaxis(bias_grad.reshape(3, local_heads, owners, per_shard), 2, 0).reshape(owners, -1)
    bias_parts = jnp.pad(jnp.roll(bias_parts, -f, axis=0), ((0, 0), (0, shard - 3 * local_heads * per_shard)))
    small_sums = jnp.concatenate([router_grad, gain_one_grad[None], gain_two_grad[None]], axis=0)
    small_here = sum_small(small_sums, bias_parts.reshape(1, width), f, shard)
    small_sums = small_here + swap_x(small_here)
    bias_out = small_sums[11, : 3 * local_heads * per_shard].reshape(3, local_heads, per_shard)

    shared_up_out, shared_down_out = shared_call(after(total_s, qkv_part, out_part), peer_s, c, x)
    gate_up_out = place_call(after(total_b, shared_up_out), peer_b, c, 2 * (1 - x), (0, 2))
    down_out = place_call(total_b, peer_b, c, 2 * (1 - x), (2, 1))
    total_a = add_experts(after(sum_a, qkv_part, out_part, gate_up_out, down_out, small_here), from_b)
    peer_a = swap_core(total_a)

    def core_join(part, hidden_axis):
        part = add(part, after(swap_x(part), total_a))
        peer = swap_core(part)
        return jnp.where(
            c == 0,
            jnp.concatenate([part, peer], axis=hidden_axis),
            jnp.concatenate([peer, part], axis=hidden_axis),
        ).astype(F32)

    qkv_out, out_out = core_join(qkv_part, 2), core_join(out_part, 0)
    result = turn_back((hidden_rows + after(mixer_local, qkv_out).astype(F32)).astype(BF16))
    gate_up_out = place_call(total_a, peer_a, c, 2 * x, (0, 2), gate_up_out)
    gate_up_out = jnp.transpose(gate_up_out, (0, 3, 1, 2))
    down_out = place_call(total_a, peer_a, c, 2 * x, (2, 1), down_out).reshape(EXPERTS, hidden, shard)

    return (
        result,
        turn_back(input_grad),
        small_sums[9:11],
        qkv_out,
        bias_out,
        out_out,
        small_sums[:EXPERTS].T,
        small_sums[EXPERTS],
        gate_up_out,
        down_out,
        shared_up_out,
        shared_down_out,
    )


def solution(mesh):
    in_specs = (
        P(("rep", "fsdp", "tensor"), None),
        P(("rep", "fsdp", "tensor"), None),
        P(("rep", "fsdp"), None),
        P(("rep", "fsdp"), None),
        P(None, "fsdp"),
        P(None, "fsdp", "tensor"),
        P(None, "tensor", "fsdp"),
        P("tensor", "fsdp"),
        P("fsdp", None),
        P("fsdp"),
        P(None, "fsdp", None, "tensor"),
        P(None, "tensor", "fsdp"),
        P("fsdp", None, "tensor"),
        P("tensor", "fsdp"),
    )
    out_specs = (
        P(("rep", "fsdp", "tensor"), None),
        P(("rep", "fsdp", "tensor"), None),
        P(None, "fsdp"),
        P(None, "fsdp", "tensor"),
        P(None, "tensor", "fsdp"),
        P("tensor", "fsdp"),
        P("fsdp", None),
        P("fsdp"),
        P(None, "fsdp", None, "tensor"),
        P(None, "tensor", "fsdp"),
        P("fsdp", None, "tensor"),
        P("tensor", "fsdp"),
    )
    return jax.shard_map(shards, mesh=mesh, in_specs=in_specs, out_specs=out_specs, check_vma=False)
```

time: 1050 us -> 754 us (0.72)
  waiting for transfers between devices: 191 us -> 87 us
  other arithmetic: 138 us -> 45.8 us
  local copies, waits for them, and re-layouts: 133 us -> 57 us
  matrix products: 55.4 us -> 2.25 us
  Pallas kernels: 486 us -> 506 us
    ppermute x8 -> x9, waiting for transfers between devices: 165 us -> 37.2 us  [swap_x(): return lax.ppermute(a, 'rep', [(i, i ^ 2) for i in range(n)])]
    dot_general x13 -> x0, matrix products: 47.8 us -> none  [the longest x2 8.2 us: extra(): lax.dot_general(small_pair[:, part * LENGTH:(part + 1) * LENGTH], router_...]
    pallas_call x8 -> x19, Pallas kernels: 316 us -> 360 us  [the longest x3 234 us: rows_call(): pl.pallas_call(functools.partial(rows_kernel, n, rows, len(parts), bool(p...]
    convert_element_type x14 -> x7, other arithmetic: 48.7 us -> 8.8 us  [the longest x2 6.45 us: core_join(): return jnp.where(c == 0, jnp.concatenate([part, peer], axis=hidden_axis),...]
    unnamed x151 -> x99, local copies, waits for them, and re-layouts: 58.9 us -> 22 us
    ppermute x12 -> x11, waiting for transfers between devices: 16 us -> 42.3 us  [swap_y(): return lax.ppermute(a, 'fsdp', [(0, 1), (1, 0)])]
    convert_element_type x7 -> x6, other arithmetic: 38.1 us -> 12.2 us  [add(): return (one.astype(F32) + two.astype(F32)).astype(BF16)]
    pallas_call x3, Pallas kernels: 170 us -> 147 us  [experts_call(): pl.pallas_call(functools.partial(experts_kernel, rows, width, own_width,...]
  transfers between devices with their start and end apart: 38 -> 38, of which waited for: 11 -> 10; matrix products, arithmetic and copies ran while one was open for 30% -> 11% of each run, Pallas kernels for 44% -> 66%
where the time goes in v3:
time: 754 us; the launch traced here: 745 us
  Pallas kernels  506 us (67%)
  waiting for transfers between devices  87 us (12%)
  local copies, waits for them, and re-layouts  57 us (8%)
  other arithmetic  45.8 us (6%)
  starting transfers between devices  31.6 us (4%)
  between operations  14.9 us (2%)
    pallas_call x3, Pallas kernels, rows_call(): pl.pallas_call(functools.partial(rows_kernel, n, rows, len(parts), bool(p...  234 us
    pallas_call x3, Pallas kernels, experts_call(): pl.pallas_call(functools.partial(experts_kernel, rows, width, own_width,...  147 us
    ppermute x11, waiting for transfers between devices, swap_y(): return lax.ppermute(a, 'fsdp', [(0, 1), (1, 0)])  42.3 us
    pallas_call x8, Pallas kernels, sum_call(): pl.pallas_call(sum_kernel, out_shape=jax.ShapeDtypeStruct((rows, columns)...  38.6 us
    ppermute x9, waiting for transfers between devices, swap_x(): return lax.ppermute(a, 'rep', [(i, i ^ 2) for i in range(n)])  37.2 us
    pallas_call x2, Pallas kernels, attention_call(): pl.pallas_call(functools.partial(kernel, heads, own_width), out_shape=out...  36.3 us
    pallas_call x4, Pallas kernels, place_call(): pl.pallas_call(place_kernel, out_shape=jax.ShapeDtypeStruct((EXPERTS, len...  28 us
    unnamed x99, local copies, waits for them, and re-layouts  22 us
  transfers between devices with their start and end apart: 38, of which 10 were waited for; matrix products, arithmetic and copies ran while one was open for 11% of the time, Pallas kernels for 66%

profile of v3, /device:TPU:0, one launch (start us, length us, event | category | flops | bytes accessed | tf_op | source)
XLA Modules:
  0.0 744.9 jit_solution(17968218453947755753)
XLA Ops:
  10.2 3.0 collective-permute-start
  15.5 2.1 collective-permute-start.2
  22.9 14.9 %copy.71 = bf16[1024,2,1408]{0,2,1:T(8,128)(2,1)} copy(bf16[1024,2,1408]{2,1,0:T(2,128)(2,1)} %param.28) | data formatting | bytes 11534336 | tf_op jit(solution)/shard_map/optimization_barrier | solution.py:936
  37.8 3.3 slice_bitcast_fusion
  46.4 2.4 pad_maximum_fusion.refs_5_
  48.8 18.3 %collective-permute-done.6 = bf16[128,1024]{1,0:T(8,128)(2,1)S(1)} collective-permute-done((bf16[128,1024]{1,0:T(8,128)(2,1)S(1)}, bf16[128,1024]{1,0:T(8,128)(2,1)S(1)}, u32[]{:S(2)}, u32[]{:S(2)}) %collective-permute-start.6) | collective-permute-done | bytes 262176 | tf_op jit(solution)/shard_map/ppermute | solution.py:39
  72.0 2.3 fusion.2
  75.0 1.8 pad_maximum_fusion.2.w_oth
  79.8 2.1 constant_dynamic-slice_fusion.2
  81.9 2.4 pad_maximum_fusion.1.refs_5_
  87.0 16.9 %attend.1 = (bf16[640,512]{1,0:T(8,128)(2,1)}, bf16[640,512]{1,0:T(8,128)(2,1)}, bf16[640,512]{1,0:T(8,128)(2,1)}, bf16[640,512]{1,0:T(8,128)(2,1)}, f32[8,640]{1,0:T(8,128)}, /*index=5*/bf16[640,2048]{1,0:T(8,128)(2,1)}) custom-call(s32[1,2]{1,0:T(1,128)} %starts.3, bf16[640,2048]{1,0:T(8,128)(2,1)} %all-gather.3.cloned.1.call-done.rows, ...), custom_call_target="tpu_custom_call" | custom-call | flops 1 | bytes 1 | tf_op jit(solution)/shard_map/attend/pallas_call | solution.py:518
  103.9 100.5 %rows.3 = (f32[160,2048]{1,0:T(8,128)}, bf16[640,2048]{1,0:T(8,128)(2,1)}, bf16[640,2048]{1,0:T(8,128)(2,1)}) custom-call(bf16[640,2048]{1,0:T(8,128)(2,1)} %get-tuple-element.103.refs_0_, bf16[160,2048]{1,0:T(8,128)(2,1)} %copy-done.21, f32[1,2048]{1,0:T(1,128)} %bitcast.144), custom_call_target="tpu_custom_call" | custom-call | flops 1 | bytes 1 | tf_op jit(solution)/shard_map/rows/pallas_call | solution.py:343
  205.1 2.2 constant_dynamic-update-slice_fusion.3
  214.3 48.5 %experts.3 = (bf16[2,3,352,1024]{3,2,1,0:T(8,128)(2,1)}, bf16[2,3,352,1024]{3,2,1,0:T(8,128)(2,1)}, bf16[640,2048]{1,0:T(8,128)(2,1)}, bf16[640,2048]{1,0:T(8,12...) custom-call(bf16[640,2048]{1,0:T(8,128)(2,1)} %get-tuple-element.105.refs_0_.refs_1_, ...), custom_call_target="tpu_custom_call" | custom-call | flops 1 | bytes 1 | tf_op jit(solution)/shard_map/experts/pallas_call | solution.py:662
  265.0 8.6 %collective-permute-done.11.refs_6_ = bf16[2,3,352,1024]{3,2,1,0:T(8,128)(2,1)} collective-permute-done((bf16[2,3,352,1024]{3,2,1,0:T(8,128)(2,1)}, bf16[2,3,352,1024]{3,2,1,0:T(8,128)(2,1)}, u32[]{:S(2)}, u32[]{:S(2)}) %collective-permute-start.11) | collective-permute-done | bytes 4325408 | tf_op jit(solution)/shard_map/ppermute | solution.py:34
  273.7 48.7 %experts.4 = (bf16[2,3,352,1024]{3,2,1,0:T(8,128)(2,1)}, bf16[2,3,352,1024]{3,2,1,0:T(8,128)(2,1)}, bf16[640,2048]{1,0:T(8,128)(2,1)}, bf16[640,2048]{1,0:T(8,12...) custom-call(bf16[640,2048]{1,0:T(8,128)(2,1)} %get-tuple-element.105.refs_0_.refs_1_, ...), custom_call_target="tpu_custom_call" | custom-call | flops 1 | bytes 1 | tf_op jit(solution)/shard_map/experts/pallas_call | solution.py:662
  325.5 49.3 %experts.5 = (bf16[2,3,352,1024]{3,2,1,0:T(8,128)(2,1)}, bf16[2,3,352,1024]{3,2,1,0:T(8,128)(2,1)}, bf16[640,2048]{1,0:T(8,128)(2,1)}, bf16[640,2048]{1,0:T(8,12...) custom-call(s32[1]{0:T(128)} %bitcast.39.refs_0_, ...), custom_call_target="tpu_custom_call" | custom-call | flops 1 | bytes 1 | tf_op jit(solution)/shard_map/experts/pallas_call | solution.py:662
  377.1 5.2 sums.8
  385.7 84.1 %rows.4 = (f32[160,2048]{1,0:T(8,128)}, f32[160,2048]{1,0:T(8,128)}, bf16[640,2048]{1,0:T(8,128)(2,1)}) custom-call(bf16[640,2048]{1,0:T(8,128)(2,1)} %get-tuple-element.117.refs_0_, bf16[640,2048]{1,0:T(8,128)(2,1)} %get-tuple-element.121.refs_1_, bf16[640,2048]{1,0:T(8,128)(2,1)} %get-tuple-element.125.refs_2_, ...), custom_call_target="tpu_custom_call" | custom-call | flops 1 | bytes 1 | tf_op jit(solution)/shard_map/rows/pallas_call | solution.py:343
  469.9 5.1 sums.9
  475.6 19.4 %attend_back.1 = (bf16[3,640,512]{2,1,0:T(8,128)(2,1)}, f32[3,512]{1,0:T(4,128)}, bf16[640,2048]{1,0:T(8,128)(2,1)}) custom-call(s32[1,2]{1,0:T(1,128)} %starts.3, bf16[640,2048]{1,0:T(8,128)(2,1)} %get-tuple-element.148.grad.branch_grad, bf16[3,1024,512]{2,1,0:T(8,128)(2,1)} %w_own.3, bf16[3,1024,512]{2,1,0:T(8,128)(2,1)} %pad_maximum_fusion.2.w_oth, ...), custom_call_target="tpu_custom_call" | custom-call | flops 1 | bytes 1 | tf_op jit(solution)/shard_map/attend_back/pallas_call | solution.py:518
  495.0 49.4 %rows.5 = f32[160,2048]{1,0:T(8,128)} custom-call(bf16[640,2048]{1,0:T(8,128)(2,1)} %get-tuple-element.140.refs_0_), custom_call_target="tpu_custom_call" | custom-call | flops 1 | bytes 1 | tf_op jit(solution)/shard_map/rows/pallas_call | solution.py:343
  544.4 6.2 collective-permute-done.15
  550.6 3.5 sums.10.refs_0_
  554.0 2.0 copy-done
  556.1 10.0 %dense_grads.1 = (bf16[3,1024,256]{2,1,0:T(8,128)(2,1)S(1)}, bf16[3,1024,256]{2,1,0:T(8,128)(2,1)S(1)}, bf16[3,2048,256]{2,1,0:T(8,128)(2,1)}, bf16[256,1024]{1,...) custom-call(s32[1]{0:T(128)} %bitcast.35.core, ...), custom_call_target="tpu_custom_call" | custom-call | flops 1 | bytes 1 | tf_op jit(solution)/shard_map/dense_grads/pallas_call | solution.py:755
  571.5 2.3 copy-done.1
  573.8 6.0 sums.13
  581.5 6.2 sums.14
  589.6 2.0 add_convert_fusion.7
  591.7 3.1 add_convert_fusion.2
  596.5 4.9 collective-permute-done.25
  609.6 5.5 sums.12
  617.7 21.3 %collective-permute-done.19 = bf16[3,1024,256]{2,1,0:T(8,128)(2,1)} collective-permute-done((bf16[3,1024,256]{2,1,0:T(8,128)(2,1)}, bf16[3,1024,256]{2,1,0:T(8,128)(2,1)}, u32[]{:S(2)}, u32[]{:S(2)}) %collective-permute-start.19) | collective-permute-done | bytes 1572896 | tf_op jit(solution)/shard_map/ppermute | solution.py:34
  640.5 2.5 add_convert_fusion.1
  643.0 6.1 collective-permute-done.22
  649.7 2.1 add_convert_fusion.6
  652.5 5.7 place.5.refs_0_
  658.2 12.9 %shared.1 = (f32[1024,2,1408]{2,1,0:T(2,128)}, f32[1408,1024]{1,0:T(8,128)}) custom-call(s32[8]{0:T(128)S(1)} %pad_add_fusion.6.table, bf16[2,3,352,1024]{3,2,1,0:T(8,128)(2,1)} %bitcast.51.mine, bf16[2,3,352,1024]{3,2,1,0:T(8,128)(2,1)} %collective-permute-done.23.peer), custom_call_target="tpu_custom_call" | custom-call | flops 1 | bytes 1 | tf_op jit(solution)/shard_map/shared/pallas_call | solution.py:826
  671.0 8.3 %place.4.refs_0_ = f32[8,2,352,1024]{3,2,1,0:T(8,128)} custom-call(s32[4,4]{1,0:T(4,128)S(1)} %get-tuple-element.212.table, bf16[2,3,352,1024]{3,2,1,0:T(8,128)(2,1)} %bitcast.48.mine, bf16[2,3,352,1024]{3,2,1,0:T(8,128)(2,1)} %collective-permute-done.24.peer), custom_call_target="tpu_custom_call" | custom-call | flops 1 | bytes 1 | tf_op jit(solution)/shard_map/place/pallas_call | solution.py:795
  679.3 6.1 sums.15
  687.8 12.6 %collective-permute-done.20 = bf16[3,1024,256]{2,1,0:T(8,128)(2,1)} collective-permute-done((bf16[3,1024,256]{2,1,0:T(8,128)(2,1)S(1)}, bf16[3,1024,256]{2,1,0:T(8,128)(2,1)}, u32[]{:S(2)}, u32[]{:S(2)}) %collective-permute-start.20) | collective-permute-done | bytes 1572896 | tf_op jit(solution)/shard_map/ppermute | solution.py:39
  700.3 2.2 add_convert_fusion
  704.9 6.3 collective-permute-done.32
  715.3 1.8 fusion.19
  717.0 4.7 fusion
  724.2 5.7 place.7
  729.9 8.3 %place.6 = f32[8,2,352,1024]{3,2,1,0:T(8,128)} custom-call(s32[4,4]{1,0:T(4,128)S(1)} %get-tuple-element.211.table, bf16[2,3,352,1024]{3,2,1,0:T(8,128)(2,1)} %bitcast.57.mine, bf16[2,3,352,1024]{3,2,1,0:T(8,128)(2,1)} %collective-permute-done.34.peer, f32[8,2,352,1024]{3,2,1,0:T(8,128)} %place.4.refs_0_), custom_call_target="tpu_custom_call", output_to_operand_aliasing={{}: (3, {})} | custom-call | flops 1 | bytes 1 | tf_op jit(solution)/shard_map/place/pallas_call | solution.py:795
  (268 shorter events, 80.8 us)
Async XLA Ops:
  7.2 70.9 %all-gather.3.cloned.1.call-start = ((), (), s32[]{:S(2)}) async-start(), calls=%async_computation.1 | async-start | bytes 3276800 | tf_op jit(solution)/shard_map/all_gather | solution.py:898
  10.2 11.4 %collective-permute-start = (bf16[1,12032]{1,0:T(2,128)(2,1)S(1)}, bf16[1,12032]{1,0:T(2,128)(2,1)S(1)}, u32[]{:S(2)}, u32[]{:S(2)}) collective-permute-start(bf16[1,12032]{1,0:T(2,128)(2,1)S(1)} %broadcast_in_dim.48), channel_id=1, source_target_pairs={{0,4},{4,0},{1,5},{5,1},{2,6},{6,2},{3,7},{7,3},{8,12},{12,8},{9,1... | collective-permute-start | bytes 72200 | tf_op jit(solution)/shard_map/ppermute | solution.py:34
  14.2 29.3 %collective-permute-start.5 = (bf16[128,1024]{1,0:T(8,128)(2,1)S(1)}, bf16[128,1024]{1,0:T(8,128)(2,1)S(1)}, u32[]{:S(2)}, u32[]{:S(2)}) collective-permute-start(bf16[128,1024]{1,0:T(8,128)(2,1)S(1)} %constant_dynamic-slice_fusion.4), channel_id=1, source_target_pairs={{0,4},{4,0},{1,5},{5,1},{2,6},{6,2},{3,7},{7,3},{8,12},{12,8},{9,1... | collective-permute-start | bytes 786440 | tf_op jit(solution)/shard_map/ppermute | solution.py:34
  15.5 26.0 %collective-permute-start.2 = (bf16[3,1024,128]{2,1,0:T(8,128)(2,1)S(1)}, bf16[3,1024,128]{2,1,0:T(8,128)(2,1)S(1)}, u32[]{:S(2)}, u32[]{:S(2)}) collective-permute-start(bf16[3,1024,128]{2,1,0:T(8,128)(2,1)S(1)} %constant_dynamic-slice_fusion.5), channel_id=1, source_target_pairs={{0,4},{4,0},{1,5},{5,1},{2,6},{6,2},{3,7},{7,3},{8,12},{12,8},{9,1... | collective-permute-start | bytes 2359304 | tf_op jit(solution)/shard_map/ppermute | solution.py:34
  19.3 18.6 %copy-start.21 = (bf16[160,2048]{1,0:T(8,128)(2,1)}, bf16[160,2048]{1,0:T(8,128)(2,1)S(1)}, u32[]{:S(2)}) copy-start(bf16[160,2048]{1,0:T(8,128)(2,1)S(1)} %get-tuple-element.190.refs_1_) | copy-start | bytes 1966084
  22.8 181.6 %all-gather.5.cloned.1.call-start = ((), (), s32[]{:S(2)}) async-start(), calls=%async_computation.2 | async-start | bytes 3276800 | tf_op jit(solution)/shard_map/all_gather | solution.py:949
  22.8 46.0 %collective-permute-start.1 = (s32[640,4]{0,1:T(4,128)}, s32[640,4]{0,1:T(4,128)}, u32[]{:S(2)}, u32[]{:S(2)}) collective-permute-start(s32[640,4]{0,1:T(4,128)} %param.19), channel_id=1, source_target_pairs={{0,8},{8,0},{16,24},{24,16},{1,9},{9,1},{17,25},{25,17},{2,10},{10... | collective-permute-start | bytes 30728 | tf_op jit(solution)/shard_map/ppermute | solution.py:44
  41.5 25.8 %collective-permute-start.3 = (bf16[3,1024,128]{2,1,0:T(8,128)(2,1)S(1)}, bf16[3,1024,128]{2,1,0:T(8,128)(2,1)S(1)}, u32[]{:S(2)}, u32[]{:S(2)}) collective-permute-start(bf16[3,1024,128]{2,1,0:T(8,128)(2,1)S(1)} %collective-permute-done.2), channel_id=1, source_target_pairs={{0,16},{8,24},{16,0},{24,8},{1,17},{9,25},{17,1},{25,9},{2,18},{10... | collective-permute-start | bytes 2359304 | tf_op jit(solution)/shard_map/ppermute | solution.py:39
  43.6 23.6 %collective-permute-start.6 = (bf16[128,1024]{1,0:T(8,128)(2,1)S(1)}, bf16[128,1024]{1,0:T(8,128)(2,1)S(1)}, u32[]{:S(2)}, u32[]{:S(2)}) collective-permute-start(bf16[128,1024]{1,0:T(8,128)(2,1)S(1)} %collective-permute-done.5), channel_id=1, source_target_pairs={{0,16},{8,24},{16,0},{24,8},{1,17},{9,25},{17,1},{25,9},{2,18},{10... | collective-permute-start | bytes 786440 | tf_op jit(solution)/shard_map/ppermute | solution.py:39
  67.2 3.1 collective-permute-start.7
  67.4 4.5 collective-permute-start.4
  78.1 643.6 %reduce-scatter.2.cloned.1.call-start = ((), (), s32[]{:S(2)}) async-start(), calls=%async_computation.3 | async-start | bytes 3276800 | tf_op jit(solution)/shard_map/reduce_scatter | solution.py:1089
  84.4 126.0 %collective-permute-start.9 = (bf16[2,3,352,1024]{3,2,1,0:T(8,128)(2,1)}, bf16[2,3,352,1024]{3,2,1,0:T(8,128)(2,1)}, u32[]{:S(2)}, u32[]{:S(2)}) collective-permute-start(bf16[2,3,352,1024]{3,2,1,0:T(8,128)(2,1)} %pad_maximum_fusion.1.refs_5_), channel_id=1, source_target_pairs={{0,4},{4,0},{1,5},{5,1},{2,6},{6,2},{3,7},{7,3},{8,12},{12,8},{9,1... | collective-permute-start | bytes 12976136 | tf_op jit(solution)/shard_map/ppermute | solution.py:34
  86.5 187.2 %collective-permute-start.11 = (bf16[2,3,352,1024]{3,2,1,0:T(8,128)(2,1)}, bf16[2,3,352,1024]{3,2,1,0:T(8,128)(2,1)}, u32[]{:S(2)}, u32[]{:S(2)}) collective-permute-start(bf16[2,3,352,1024]{3,2,1,0:T(8,128)(2,1)} %pad_maximum_fusion.refs_5_), channel_id=1, source_target_pairs={{0,4},{4,0},{1,5},{5,1},{2,6},{6,2},{3,7},{7,3},{8,12},{12,8},{9,1... | collective-permute-start | bytes 12976136 | tf_op jit(solution)/shard_map/ppermute | solution.py:34
  103.9 101.2 %copy-start.34 = (s32[1280,4]{0,1:T(4,128)S(1)}, s32[1280,4]{0,1:T(4,128)}, u32[]{:S(2)}) copy-start(s32[1280,4]{0,1:T(4,128)} %constant_dynamic-update-slice_fusion) | copy-start | bytes 61444
  204.4 8.4 %collective-permute-start.8 = (bf16[640,2048]{1,0:T(8,128)(2,1)}, bf16[640,2048]{1,0:T(8,128)(2,1)S(1)}, u32[]{:S(2)}, u32[]{:S(2)}) collective-permute-start(bf16[640,2048]{1,0:T(8,128)(2,1)} %all-gather.5.cloned.1.call-done.refs_2_.refs_3_), channel_id=1, source_target_pairs={{0,8},{8,0},{16,24},{24,16},{1,9},{9,1},{17,25},{25,17},{2,10},{10... | collective-permute-start | bytes 7864328 | tf_op jit(solution)/shard_map/ppermute | solution.py:44
  210.3 115.1 %collective-permute-start.12 = (bf16[2,3,352,1024]{3,2,1,0:T(8,128)(2,1)}, bf16[2,3,352,1024]{3,2,1,0:T(8,128)(2,1)}, u32[]{:S(2)}, u32[]{:S(2)}) collective-permute-start(bf16[2,3,352,1024]{3,2,1,0:T(8,128)(2,1)} %collective-permute-done.9.refs_6_), channel_id=1, source_target_pairs={{0,16},{8,24},{16,0},{24,8},{1,17},{9,25},{17,1},{25,9},{2,18},{10... | collective-permute-start | bytes 12976136 | tf_op jit(solution)/shard_map/ppermute | solution.py:39
  262.8 114.2 %collective-permute-start.10 = (bf16[2,3,352,1024]{3,2,1,0:T(8,128)(2,1)}, bf16[2,3,352,1024]{3,2,1,0:T(8,128)(2,1)}, u32[]{:S(2)}, u32[]{:S(2)}) collective-permute-start(bf16[2,3,352,1024]{3,2,1,0:T(8,128)(2,1)} %get-tuple-element.116), channel_id=1, source_target_pairs={{0,4},{4,0},{1,5},{5,1},{2,6},{6,2},{3,7},{7,3},{8,12},{12,8},{9,1... | collective-permute-start | bytes 12976136 | tf_op jit(solution)/shard_map/ppermute | solution.py:34
  322.4 147.4 %collective-permute-start.13 = (bf16[2,3,352,1024]{3,2,1,0:T(8,128)(2,1)}, bf16[2,3,352,1024]{3,2,1,0:T(8,128)(2,1)}, u32[]{:S(2)}, u32[]{:S(2)}) collective-permute-start(bf16[2,3,352,1024]{3,2,1,0:T(8,128)(2,1)} %get-tuple-element.133), channel_id=1, source_target_pairs={{0,4},{4,0},{1,5},{5,1},{2,6},{6,2},{3,7},{7,3},{8,12},{12,8},{9,1... | collective-permute-start | bytes 12976136 | tf_op jit(solution)/shard_map/ppermute | solution.py:34
  325.5 51.6 %slice-start.4 = ((s8[4325376]{0:T(1024)(128)(4,1)}), s8[4194304]{0:T(1024)(128)(4,1)S(1)}, s32[]{:S(2)}) async-start(s8[4325376]{0:T(1024)(128)(4,1)} %bitcast.124), calls=%async_computation.8 | async-start | bytes 8388608
  325.5 51.6 %slice-start.5 = ((s8[4325376]{0:T(1024)(128)(4,1)}), s8[131072]{0:T(1024)(128)(4,1)S(1)}, s32[]{:S(2)}) async-start(s8[4325376]{0:T(1024)(128)(4,1)} %bitcast.124), calls=%async_computation.9 | async-start | bytes 262144
  374.8 175.8 %collective-permute-start.15 = (bf16[2,3,352,1024]{3,2,1,0:T(8,128)(2,1)}, bf16[2,3,352,1024]{3,2,1,0:T(8,128)(2,1)}, u32[]{:S(2)}, u32[]{:S(2)}) collective-permute-start(bf16[2,3,352,1024]{3,2,1,0:T(8,128)(2,1)} %get-tuple-element.145), channel_id=1, source_target_pairs={{0,4},{4,0},{1,5},{5,1},{2,6},{6,2},{3,7},{7,3},{8,12},{12,8},{9,1... | collective-permute-start | bytes 12976136 | tf_op jit(solution)/shard_map/ppermute | solution.py:34
  382.2 112.7 %collective-permute-start.14 = (bf16[2,3,352,1024]{3,2,1,0:T(8,128)(2,1)}, bf16[2,3,352,1024]{3,2,1,0:T(8,128)(2,1)}, u32[]{:S(2)}, u32[]{:S(2)}) collective-permute-start(bf16[2,3,352,1024]{3,2,1,0:T(8,128)(2,1)} %bitcast.38), channel_id=1, source_target_pairs={{0,16},{8,24},{16,0},{24,8},{1,17},{9,25},{17,1},{25,9},{2,18},{10... | collective-permute-start | bytes 12976136 | tf_op jit(solution)/shard_map/ppermute | solution.py:39
  385.7 84.2 %slice-start.2 = ((s8[4325376]{0:T(1024)(128)(4,1)}), s8[4194304]{0:T(1024)(128)(4,1)S(1)}, s32[]{:S(2)}) async-start(s8[4325376]{0:T(1024)(128)(4,1)} %bitcast.121), calls=%async_computation.6 | async-start | bytes 8388608
  385.7 84.2 %slice-start.3 = ((s8[4325376]{0:T(1024)(128)(4,1)}), s8[131072]{0:T(1024)(128)(4,1)S(1)}, s32[]{:S(2)}) async-start(s8[4325376]{0:T(1024)(128)(4,1)} %bitcast.121), calls=%async_computation.7 | async-start | bytes 262144
  475.0 105.9 %collective-permute-start.18 = (bf16[2,3,352,1024]{3,2,1,0:T(8,128)(2,1)}, bf16[2,3,352,1024]{3,2,1,0:T(8,128)(2,1)}, u32[]{:S(2)}, u32[]{:S(2)}) collective-permute-start(bf16[2,3,352,1024]{3,2,1,0:T(8,128)(2,1)} %bitcast.43), channel_id=1, source_target_pairs={{0,16},{8,24},{16,0},{24,8},{1,17},{9,25},{17,1},{25,9},{2,18},{10... | collective-permute-start | bytes 12976136 | tf_op jit(solution)/shard_map/ppermute | solution.py:39
  475.5 75.0 %slice-start = ((s8[4325376]{0:T(1024)(128)(4,1)}), s8[4194304]{0:T(1024)(128)(4,1)S(1)}, s32[]{:S(2)}) async-start(s8[4325376]{0:T(1024)(128)(4,1)} %bitcast.118), calls=%async_computation.4 | async-start | bytes 8388608
  475.6 75.0 %slice-start.1 = ((s8[4325376]{0:T(1024)(128)(4,1)}), s8[131072]{0:T(1024)(128)(4,1)S(1)}, s32[]{:S(2)}) async-start(s8[4325376]{0:T(1024)(128)(4,1)} %bitcast.118), calls=%async_computation.5 | async-start | bytes 262144
  569.2 22.4 %collective-permute-start.17 = (bf16[3,2048,256]{2,1,0:T(8,128)(2,1)}, bf16[3,2048,256]{2,1,0:T(8,128)(2,1)}, u32[]{:S(2)}, u32[]{:S(2)}) collective-permute-start(bf16[3,2048,256]{2,1,0:T(8,128)(2,1)} %get-tuple-element.149), channel_id=1, source_target_pairs={{0,8},{8,0},{16,24},{24,16},{1,9},{9,1},{17,25},{25,17},{2,10},{10... | collective-permute-start | bytes 9437192 | tf_op jit(solution)/shard_map/ppermute | solution.py:44
  569.2 18.4 %collective-permute-start.21 = (bf16[256,2048]{1,0:T(8,128)(2,1)}, bf16[256,2048]{1,0:T(8,128)(2,1)}, u32[]{:S(2)}, u32[]{:S(2)}) collective-permute-start(bf16[256,2048]{1,0:T(8,128)(2,1)} %get-tuple-element.168), channel_id=1, source_target_pairs={{0,8},{8,0},{16,24},{24,16},{1,9},{9,1},{17,25},{25,17},{2,10},{10... | collective-permute-start | bytes 3145736 | tf_op jit(solution)/shard_map/ppermute | solution.py:44
  570.0 109.3 %collective-permute-start.29 = (bf16[2,3,352,1024]{3,2,1,0:T(8,128)(2,1)}, bf16[2,3,352,1024]{3,2,1,0:T(8,128)(2,1)}, u32[]{:S(2)}, u32[]{:S(2)}) collective-permute-start(bf16[2,3,352,1024]{3,2,1,0:T(8,128)(2,1)} %bitcast.117), channel_id=1, source_target_pairs={{0,16},{8,24},{16,0},{24,8},{1,17},{9,25},{17,1},{25,9},{2,18},{10... | collective-permute-start | bytes 12976136 | tf_op jit(solution)/shard_map/ppermute | solution.py:39
  579.8 72.6 %collective-permute-start.24 = (bf16[2,3,352,1024]{3,2,1,0:T(8,128)(2,1)}, bf16[2,3,352,1024]{3,2,1,0:T(8,128)(2,1)}, u32[]{:S(2)}, u32[]{:S(2)}) collective-permute-start(bf16[2,3,352,1024]{3,2,1,0:T(8,128)(2,1)} %bitcast.48.mine), channel_id=1, source_target_pairs={{0,8},{8,0},{16,24},{24,16},{1,9},{9,1},{17,25},{25,17},{2,10},{10... | collective-permute-start | bytes 12976136 | tf_op jit(solution)/shard_map/ppermute | solution.py:44
  580.9 22.2 %collective-permute-start.16 = (bf16[640,2048]{1,0:T(8,128)(2,1)S(1)}, bf16[640,2048]{1,0:T(8,128)(2,1)}, u32[]{:S(2)}, u32[]{:S(2)}) collective-permute-start(bf16[640,2048]{1,0:T(8,128)(2,1)S(1)} %sums.11), channel_id=1, source_target_pairs={{0,8},{8,0},{16,24},{24,16},{1,9},{9,1},{17,25},{25,17},{2,10},{10... | collective-permute-start | bytes 7864328 | tf_op jit(solution)/shard_map/ppermute | solution.py:44
  587.7 70.5 %collective-permute-start.23 = (bf16[2,3,352,1024]{3,2,1,0:T(8,128)(2,1)}, bf16[2,3,352,1024]{3,2,1,0:T(8,128)(2,1)}, u32[]{:S(2)}, u32[]{:S(2)}) collective-permute-start(bf16[2,3,352,1024]{3,2,1,0:T(8,128)(2,1)} %bitcast.51.mine), channel_id=1, source_target_pairs={{0,8},{8,0},{16,24},{24,16},{1,9},{9,1},{17,25},{25,17},{2,10},{10... | collective-permute-start | bytes 12976136 | tf_op jit(solution)/shard_map/ppermute | solution.py:44
  595.8 5.6 collective-permute-start.25
  601.3 37.6 %collective-permute-start.19 = (bf16[3,1024,256]{2,1,0:T(8,128)(2,1)}, bf16[3,1024,256]{2,1,0:T(8,128)(2,1)}, u32[]{:S(2)}, u32[]{:S(2)}) collective-permute-start(bf16[3,1024,256]{2,1,0:T(8,128)(2,1)} %add_convert_fusion.2), channel_id=1, source_target_pairs={{0,4},{4,0},{1,5},{5,1},{2,6},{6,2},{3,7},{7,3},{8,12},{12,8},{9,1... | collective-permute-start | bytes 4718600 | tf_op jit(solution)/shard_map/ppermute | solution.py:34
  603.1 12.1 %collective-permute-start.26 = (f32[11,2048]{1,0:T(8,128)S(1)}, f32[11,2048]{1,0:T(8,128)S(1)}, u32[]{:S(2)}, u32[]{:S(2)}) collective-permute-start(f32[11,2048]{1,0:T(8,128)S(1)} %fusion.53), channel_id=1, source_target_pairs={{0,2},{1,3},{2,0},{3,1},{4,6},{5,7},{6,4},{7,5},{8,10},{9,11},{10,... | collective-permute-start | bytes 270344 | tf_op jit(solution)/shard_map/ppermute | solution.py:418
  615.1 25.4 %copy-start.9 = (bf16[3,1024,256]{2,1,0:T(8,128)(2,1)S(1)}, bf16[3,1024,256]{2,1,0:T(8,128)(2,1)}, u32[]{:S(2)}) copy-start(bf16[3,1024,256]{2,1,0:T(8,128)(2,1)} %copy-done.8) | copy-start | bytes 4718596
  615.2 1.4 collective-permute-start.27
  616.6 32.5 %collective-permute-start.22 = (bf16[256,1024]{1,0:T(8,128)(2,1)}, bf16[256,1024]{1,0:T(8,128)(2,1)S(1)}, u32[]{:S(2)}, u32[]{:S(2)}) collective-permute-start(bf16[256,1024]{1,0:T(8,128)(2,1)} %add_convert_fusion.7), channel_id=1, source_target_pairs={{0,4},{4,0},{1,5},{5,1},{2,6},{6,2},{3,7},{7,3},{8,12},{12,8},{9,1... | collective-permute-start | bytes 1572872 | tf_op jit(solution)/shard_map/ppermute | solution.py:34
  617.6 32.1 %copy-start.14 = (bf16[256,1024]{1,0:T(8,128)(2,1)S(1)}, bf16[256,1024]{1,0:T(8,128)(2,1)}, u32[]{:S(2)}) copy-start(bf16[256,1024]{1,0:T(8,128)(2,1)} %copy-done.13) | copy-start | bytes 1572868
  639.0 12.8 %collective-permute-start.28 = (f32[12,1024]{1,0:T(8,128)S(1)}, f32[12,1024]{1,0:T(8,128)S(1)}, u32[]{:S(2)}, u32[]{:S(2)}) collective-permute-start(f32[12,1024]{1,0:T(8,128)S(1)} %slice.166), channel_id=1, source_target_pairs={{0,4},{4,0},{1,5},{5,1},{2,6},{6,2},{3,7},{7,3},{8,12},{12,8},{9,1... | collective-permute-start | bytes 147464 | tf_op jit(solution)/shard_map/ppermute | solution.py:34
  649.2 51.2 %collective-permute-start.20 = (bf16[3,1024,256]{2,1,0:T(8,128)(2,1)S(1)}, bf16[3,1024,256]{2,1,0:T(8,128)(2,1)}, u32[]{:S(2)}, u32[]{:S(2)}) collective-permute-start(bf16[3,1024,256]{2,1,0:T(8,128)(2,1)S(1)} %add_convert_fusion.1), channel_id=1, source_target_pairs={{0,16},{8,24},{16,0},{24,8},{1,17},{9,25},{17,1},{25,9},{2,18},{10... | collective-permute-start | bytes 4718600 | tf_op jit(solution)/shard_map/ppermute | solution.py:39
  685.5 38.7 %collective-permute-start.34 = (bf16[2,3,352,1024]{3,2,1,0:T(8,128)(2,1)}, bf16[2,3,352,1024]{3,2,1,0:T(8,128)(2,1)}, u32[]{:S(2)}, u32[]{:S(2)}) collective-permute-start(bf16[2,3,352,1024]{3,2,1,0:T(8,128)(2,1)} %bitcast.57.mine), channel_id=1, source_target_pairs={{0,8},{8,0},{16,24},{24,16},{1,9},{9,1},{17,25},{25,17},{2,10},{10... | collective-permute-start | bytes 12976136 | tf_op jit(solution)/shard_map/ppermute | solution.py:44
  685.5 25.7 %collective-permute-start.32 = (bf16[256,1024]{1,0:T(8,128)(2,1)}, bf16[256,1024]{1,0:T(8,128)(2,1)S(1)}, u32[]{:S(2)}, u32[]{:S(2)}) collective-permute-start(bf16[256,1024]{1,0:T(8,128)(2,1)} %add_convert_fusion.6), channel_id=1, source_target_pairs={{0,16},{8,24},{16,0},{24,8},{1,17},{9,25},{17,1},{25,9},{2,18},{10... | collective-permute-start | bytes 1572872 | tf_op jit(solution)/shard_map/ppermute | solution.py:39
  702.6 14.4 %collective-permute-start.30 = (bf16[3,1024,256]{2,1,0:T(8,128)(2,1)S(1)}, bf16[3,1024,256]{2,1,0:T(8,128)(2,1)}, u32[]{:S(2)}, u32[]{:S(2)}) collective-permute-start(bf16[3,1024,256]{2,1,0:T(8,128)(2,1)S(1)} %add_convert_fusion), channel_id=1, source_target_pairs={{0,8},{8,0},{16,24},{24,16},{1,9},{9,1},{17,25},{25,17},{2,10},{10... | collective-permute-start | bytes 4718600 | tf_op jit(solution)/shard_map/ppermute | solution.py:44
  703.4 9.3 %collective-permute-start.31 = (f32[12,1024]{1,0:T(8,128)S(1)}, f32[12,1024]{1,0:T(8,128)S(1)}, u32[]{:S(2)}, u32[]{:S(2)}) collective-permute-start(f32[12,1024]{1,0:T(8,128)S(1)} %copy-done.33), channel_id=1, source_target_pairs={{0,16},{8,24},{16,0},{24,8},{1,17},{9,25},{17,1},{25,9},{2,18},{10... | collective-permute-start | bytes 147464 | tf_op jit(solution)/shard_map/ppermute | solution.py:39
  711.4 3.9 collective-permute-start.33
  (34 other events, 199.1 us)
Sparse Core Ops, SparseCore 0:
  22.9 55.0 all-gather.2
  80.2 72.1 all-gather.4
  615.3 49.8 reduce-scatter.1

commit v4 on v3

--- a/solution.py
+++ b/solution.py
@@ -529,9 +529,9 @@
 
 def experts_kernel(rows, width, own_width, hidden, direct, *refs):
     if direct:
-        first, x0, x1, c0, c1, gate, gate_up, down, w_oth, *refs = refs
+        first, x0, x1, c0, c10, c11, gate, gate_up, down, w_oth, *refs = refs
     else:
-        x0, x1, c0, c1, gate, w_own, w_oth, *refs = refs
+        x0, x1, c0, c10, c11, gate, w_own, w_oth, *refs = refs
     dw_own, dw_oth, mix0, mix1, ng0, ng1, gate_grad, *refs = refs
     xv, cv, wgu, wd, ga, pre, ga_t, pre_t, st_mix, st_ng, st_dw, w_sem, x_sem, c_sem, out_sem, dw_sem = refs
     seq = rows // 2
@@ -557,18 +557,23 @@
             pltpu.make_async_copy(sources[s], to.at[pl.ds(s * seq, seq)], sem.at[s]) for s in range(2)
         ]
 
-    x_copies, c_copies = row_copies((x0, x1), xv, x_sem), row_copies((c0, c1), cv, c_sem)
-    order = [x_copies[0], *w_copies(0), *w_copies(1), c_copies[0], *w_copies(2), x_copies[1], c_copies[1]]
+    x_copies = row_copies((x0, x1), xv, x_sem)
+    c_copies = [pltpu.make_async_copy(c0, cv.at[pl.ds(0, seq)], c_sem.at[0])]
+    for i, part in enumerate((c10, c11)):
+        here = pl.ds(seq + i * part.shape[0], part.shape[0])
+        c_copies.append(pltpu.make_async_copy(part, cv.at[here], c_sem.at[1 + i]))
+    order = [x_copies[0], *w_copies(0), *w_copies(1), c_copies[0], *w_copies(2)]
+    later = [x_copies[1], *c_copies[1:]]
+    for copy in order + later:
+        copy.start()
     for copy in order:
-        copy.start()
-    for copy in order[:-2]:
         copy.wait()
 
     def token_tile(t, carry):
         @pl.when(t == seq // COLS)
         def _():
-            x_copies[1].wait()
-            c_copies[1].wait()
+            for copy in later:
+                copy.wait()
 
         here = pl.ds(pl.multiple_of(t * COLS, COLS), COLS)
         gu = dot_nt(wgu[...], xv[here, :])
@@ -667,7 +672,7 @@
             out_rows, out_rows, out_rows, out_rows,
             jax.ShapeDtypeStruct((8, rows), F32),
         ],
-        in_specs=[smem_spec] * direct + [any_spec] * 4 + [vmem_spec] + [any_spec] * (len(own_operands) + 1),
+        in_specs=[smem_spec] * direct + [any_spec] * 5 + [vmem_spec] + [any_spec] * (len(own_operands) + 1),
         out_specs=[any_spec] * 6 + [vmem_spec],
         scratch_shapes=[
             pltpu.VMEM((rows, width), BF16),
@@ -683,14 +688,14 @@
             pltpu.VMEM((2, 6 * hidden, COLS), BF16),
             pltpu.SemaphoreType.DMA((3, 2, 2)),
             pltpu.SemaphoreType.DMA((2,)),
-            pltpu.SemaphoreType.DMA((2,)),
+            pltpu.SemaphoreType.DMA((3,)),
             pltpu.SemaphoreType.DMA((2, 2, 2)),
             pltpu.SemaphoreType.DMA((2, 3, 2)),
         ],
         cost_estimate=CHEAP,
         compiler_params=pltpu.CompilerParams(vmem_limit_bytes=58 * 2**20),
         name="experts",
-    )(*([w_own[0]] if direct else []), x0, x1, c0, c1, gate, *own_operands, w_oth)
+    )(*([w_own[0]] if direct else []), x0, x1, c0, *c1, gate, *own_operands, w_oth)
 
 
 def sum_kernel(*refs):
@@ -764,48 +769,28 @@
     )(core, rows, project_grad, attended, branch_grad)
 
 
-def place_kernel(table, mine, peer, *refs):
-    out = refs[-1]
-    which = table[1, pl.program_id(0)]
-
-    @pl.when(which == 0)
-    def _():
-        out[...] = mine[...].astype(F32)
-
-    @pl.when(which == 1)
-    def _():
-        out[...] = peer[...].astype(F32)
-
-
-def place_call(mine, peer, c, first, parts, base=None):
+def place_kernel(table, source, *refs):
+    refs[-1][...] = source[...].astype(F32)
+
+
+def place_call(source, first, parts, base=None):
     at, length = parts
-    hidden, width = mine.shape[2:]
-    half = EXPERTS // 2
-    step = jnp.arange(4, dtype=jnp.int32)
-    which = (step // 2 != c).astype(jnp.int32)
-
-    def blocks(own_half):
-        return jnp.clip(step - 2 * own_half, 0, 1)
-
-    table = jnp.stack([step // 2 * half + first + step % 2, which, blocks(c), blocks(1 - c)]).astype(jnp.int32)
-
-    def source(row):
-        return pl.BlockSpec((1, length, hidden, width), lambda e, tab: (tab[row, e], at // length, 0, 0))
-
+    count, _, hidden, width = source.shape
     return pl.pallas_call(
         place_kernel,
         out_shape=jax.ShapeDtypeStruct((EXPERTS, length, hidden, width), F32),
         grid_spec=pltpu.PrefetchScalarGridSpec(
             num_scalar_prefetch=1,
-            grid=(4,),
-            in_specs=[source(2), source(3)] + [pl.BlockSpec(memory_space=pl.ANY)] * (base is not None),
-            out_specs=pl.BlockSpec((1, length, hidden, width), lambda e, tab: (tab[0, e], 0, 0, 0)),
+            grid=(count, length),
+            in_specs=[pl.BlockSpec((1, 1, hidden, width), lambda e, part, tab: (e, at + part, 0, 0))]
+            + [pl.BlockSpec(memory_space=pl.ANY)] * (base is not None),
+            out_specs=pl.BlockSpec((1, 1, hidden, width), lambda e, part, tab: (tab[0] + e, part, 0, 0)),
         ),
-        input_output_aliases={} if base is None else {3: 0},
+        input_output_aliases={} if base is None else {2: 0},
         cost_estimate=CHEAP,
         compiler_params=pltpu.CompilerParams(vmem_limit_bytes=40 * 2**20),
         name="place",
-    )(table, mine, peer, *([] if base is None else [base]))
+    )(jnp.reshape(first, (1,)).astype(jnp.int32), source, *([] if base is None else [base]))
 
 
 def shared_kernel(table, mine, peer, up, down):
@@ -878,17 +863,7 @@
     def turn_back(rows):
         return jnp.roll(rows, f * shard, axis=1)
 
-    small = jnp.concatenate(
-        [norm_gains.reshape(-1), router_weight.T.reshape(-1), shared_gate, qkv_bias.reshape(-1)]
-    )
-    small_all = jnp.concatenate([small[None], others_of(small[None], f, 0)], axis=0)
-    gains = jnp.swapaxes(small_all[:, : 2 * shard].reshape(owners, 2, shard), 0, 1).reshape(2, width)
-    gains = gains.astype(F32)
-    router = jnp.swapaxes(
-        small_all[:, 2 * shard : 11 * shard].reshape(owners, 9, shard), 0, 1
-    ).reshape(9, width)
-    bias = jnp.roll(small_all[:, 11 * shard :], f, axis=0).reshape(owners, 3, local_heads, -1)
-    bias = jnp.moveaxis(bias, 0, 2).reshape(3, local_width).astype(F32)
+    gains = jnp.concatenate([norm_gains, others_of(norm_gains, f, 1)], axis=1).astype(F32)
     cos_table, sin_table = rope_tables(LENGTH, HEAD_DIM)
     inputs = turn(block_input)
     inputs_f = inputs.astype(F32)
@@ -897,6 +872,11 @@
     normed_local = (inputs_f * inverse_one * gains[0]).astype(BF16)
     normed = lax.all_gather(normed_local, "tensor", axis=0, tiled=True)
     gate_up_t = jnp.transpose(after(expert_gate_up, normed_local), (0, 2, 3, 1))
+    small = jnp.concatenate([after(router_weight, normed_local).T.reshape(-1), shared_gate, qkv_bias.reshape(-1)])
+    small_all = jnp.concatenate([small[None], others_of(small[None], f, 0)], axis=0)
+    router = jnp.swapaxes(small_all[:, : 9 * shard].reshape(owners, 9, shard), 0, 1).reshape(9, width)
+    bias = jnp.roll(small_all[:, 9 * shard :], f, axis=0).reshape(owners, 3, local_heads, -1)
+    bias = jnp.moveaxis(bias, 0, 2).reshape(3, local_width).astype(F32)
 
     quarter = local_width // 4
 
@@ -965,7 +945,7 @@
         1, [heads_part], extras=(inputs, gains[1:2]), core_out=True, middle=norm_middle, out_types=[block_f32]
     )
     cot_rows = after(cot_rows, mixed)
-    cot_peer = swap_core(cot_rows)
+    cot_peer = [swap_core(piece) for piece in jnp.split(cot_rows, 2)]
     oth_b = swap_x(after(oth_a, mixed))
     mixed_pair = jnp.concatenate([mixed, mixed_peer], axis=0)
 
@@ -1097,13 +1077,19 @@
     bias_out = small_sums[11, : 3 * local_heads * per_shard].reshape(3, local_heads, per_shard)
 
     shared_up_out, shared_down_out = shared_call(after(total_s, qkv_part, out_part), peer_s, c, x)
-    gate_up_out = place_call(after(total_b, shared_up_out), peer_b, c, 2 * (1 - x), (0, 2))
-    down_out = place_call(total_b, peer_b, c, 2 * (1 - x), (2, 1))
+    own_first, peer_first = EXPERTS // 2 * c, EXPERTS // 2 * (1 - c)
+    gate_up_out = place_call(after(total_b, shared_up_out), own_first + 2 * (1 - x), (0, 2))
+    gate_up_out = place_call(peer_b, peer_first + 2 * (1 - x), (0, 2), gate_up_out)
+    down_out = place_call(total_b, own_first + 2 * (1 - x), (2, 1))
+    down_out = place_call(peer_b, peer_first + 2 * (1 - x), (2, 1), down_out)
     total_a = add_experts(after(sum_a, qkv_part, out_part, gate_up_out, down_out, small_here), from_b)
     peer_a = swap_core(total_a)
 
+    gate_up_out = place_call(total_a, own_first + 2 * x, (0, 2), gate_up_out)
+    down_out = place_call(total_a, own_first + 2 * x, (2, 1), down_out)
+
     def core_join(part, hidden_axis):
-        part = add(part, after(swap_x(part), total_a))
+        part = add(part, after(swap_x(part), gate_up_out, down_out))
         peer = swap_core(part)
         return jnp.where(
             c == 0,
@@ -1113,9 +1099,9 @@
 
     qkv_out, out_out = core_join(qkv_part, 2), core_join(out_part, 0)
     result = turn_back((hidden_rows + after(mixer_local, qkv_out).astype(F32)).astype(BF16))
-    gate_up_out = place_call(total_a, peer_a, c, 2 * x, (0, 2), gate_up_out)
+    gate_up_out = place_call(peer_a, peer_first + 2 * x, (0, 2), gate_up_out)
     gate_up_out = jnp.transpose(gate_up_out, (0, 3, 1, 2))
-    down_out = place_call(total_a, peer_a, c, 2 * x, (2, 1), down_out).reshape(EXPERTS, hidden, shard)
+    down_out = place_call(peer_a, peer_first + 2 * x, (2, 1), down_out).reshape(EXPERTS, hidden, shard)
 
     return (
         result,

time: 754 us -> 746 us (0.989)
  waiting for transfers between devices: 87 us -> 75.3 us
    ppermute x11 -> x12, waiting for transfers between devices: 42.3 us -> 32.1 us  [swap_y(): return lax.ppermute(a, 'fsdp', [(0, 1), (1, 0)])]
    pallas_call x4 -> x8, Pallas kernels: 28 us -> 30.9 us  [place_call(): pl.pallas_call(place_kernel, out_shape=jax.ShapeDtypeStruct((EXPERTS, len...]
    unnamed x99 -> x101, local copies, waits for them, and re-layouts: 22 us -> 19.4 us
  transfers between devices with their start and end apart: 38 -> 40, of which waited for: 10 -> 11; matrix products, arithmetic and copies ran while one was open for 11% -> 12% of each run, Pallas kernels for 66% -> 68%
where the time goes in v4:
time: 746 us; the launch traced here: 737 us
  Pallas kernels  511 us (68%)
  waiting for transfers between devices  75.3 us (10%)
  local copies, waits for them, and re-layouts  56.4 us (8%)
  other arithmetic  43.1 us (6%)
  starting transfers between devices  32.1 us (4%)
  between operations  15 us (2%)
    pallas_call x3, Pallas kernels, rows_call(): pl.pallas_call(functools.partial(rows_kernel, n, rows, len(parts), bool(p...  234 us
    pallas_call x3, Pallas kernels, experts_call(): pl.pallas_call(functools.partial(experts_kernel, rows, width, own_width,...  148 us
    pallas_call x8, Pallas kernels, sum_call(): pl.pallas_call(sum_kernel, out_shape=jax.ShapeDtypeStruct((rows, columns)...  38.5 us
    ppermute x9, waiting for transfers between devices, swap_x(): return lax.ppermute(a, 'rep', [(i, i ^ 2) for i in range(n)])  36.5 us
    pallas_call x2, Pallas kernels, attention_call(): pl.pallas_call(functools.partial(kernel, heads, own_width), out_shape=out...  36.3 us
    ppermute x12, waiting for transfers between devices, swap_y(): return lax.ppermute(a, 'fsdp', [(0, 1), (1, 0)])  32.1 us
    pallas_call x8, Pallas kernels, place_call(): pl.pallas_call(place_kernel, out_shape=jax.ShapeDtypeStruct((EXPERTS, len...  30.9 us
    unnamed x101, local copies, waits for them, and re-layouts  19.4 us
  transfers between devices with their start and end apart: 40, of which 11 were waited for; matrix products, arithmetic and copies ran while one was open for 12% of the time, Pallas kernels for 68%

profile of v4, /device:TPU:0, one launch (start us, length us, event | category | flops | bytes accessed | tf_op | source)
XLA Modules:
  0.0 737.2 jit_solution(2477967709119193433)
XLA Ops:
  7.2 3.0 collective-permute-start
  14.6 2.2 fusion.21.refs_10_
  21.8 14.9 %copy.71 = bf16[1024,2,1408]{0,2,1:T(8,128)(2,1)} copy(bf16[1024,2,1408]{2,1,0:T(2,128)(2,1)} %param.28) | data formatting | bytes 11534336 | tf_op jit(solution)/shard_map/optimization_barrier | solution.py:916
  36.7 3.5 slice_bitcast_fusion
  43.2 2.4 pad_maximum_fusion.refs_6_
  45.7 20.4 %collective-permute-done.7 = bf16[128,1024]{1,0:T(8,128)(2,1)S(1)} collective-permute-done((bf16[128,1024]{1,0:T(8,128)(2,1)S(1)}, bf16[128,1024]{1,0:T(8,128)(2,1)S(1)}, u32[]{:S(2)}, u32[]{:S(2)}) %collective-permute-start.7) | collective-permute-done | bytes 262176 | tf_op jit(solution)/shard_map/ppermute | solution.py:39
  70.4 2.3 fusion.2
  78.5 2.1 constant_dynamic-slice_fusion.2
  80.6 2.4 pad_maximum_fusion.1.refs_6_
  85.4 16.8 %attend.1 = (bf16[640,512]{1,0:T(8,128)(2,1)}, bf16[640,512]{1,0:T(8,128)(2,1)}, bf16[640,512]{1,0:T(8,128)(2,1)}, bf16[640,512]{1,0:T(8,128)(2,1)}, f32[8,640]{1,0:T(8,128)}, /*index=5*/bf16[640,2048]{1,0:T(8,128)(2,1)}) custom-call(s32[1,2]{1,0:T(1,128)} %starts.3, bf16[640,2048]{1,0:T(8,128)(2,1)} %all-gather.3.cloned.1.call-done.rows, ...), custom_call_target="tpu_custom_call" | custom-call | flops 1 | bytes 1 | tf_op jit(solution)/shard_map/attend/pallas_call | solution.py:518
  102.2 100.5 %rows.3 = (f32[160,2048]{1,0:T(8,128)}, bf16[640,2048]{1,0:T(8,128)(2,1)}, bf16[640,2048]{1,0:T(8,128)(2,1)}) custom-call(bf16[640,2048]{1,0:T(8,128)(2,1)} %get-tuple-element.105.refs_0_, bf16[160,2048]{1,0:T(8,128)(2,1)} %copy-done.19, f32[1,2048]{1,0:T(1,128)} %get-tuple-element.213.refs_2_.refs_11_), custom_call_target="tpu_custom_call" | custom-call | flops 1 | bytes 1 | tf_op jit(solution)/shard_map/rows/pallas_call | solution.py:343
  202.7 3.6 constant_dynamic-update-slice_fusion.3
  210.6 3.9 fusion.48
  219.1 48.9 %experts.3 = (bf16[2,3,352,1024]{3,2,1,0:T(8,128)(2,1)}, bf16[2,3,352,1024]{3,2,1,0:T(8,128)(2,1)}, bf16[640,2048]{1,0:T(8,128)(2,1)}, bf16[640,2048]{1,0:T(8,12...) custom-call(bf16[640,2048]{1,0:T(8,128)(2,1)} %get-tuple-element.107.refs_0_.refs_1_, ...), custom_call_target="tpu_custom_call" | custom-call | flops 1 | bytes 1 | tf_op jit(solution)/shard_map/experts/pallas_call | solution.py:667
  271.1 49.1 %experts.4 = (bf16[2,3,352,1024]{3,2,1,0:T(8,128)(2,1)}, bf16[2,3,352,1024]{3,2,1,0:T(8,128)(2,1)}, bf16[640,2048]{1,0:T(8,128)(2,1)}, bf16[640,2048]{1,0:T(8,12...) custom-call(bf16[640,2048]{1,0:T(8,128)(2,1)} %get-tuple-element.107.refs_0_.refs_1_, ...), custom_call_target="tpu_custom_call" | custom-call | flops 1 | bytes 1 | tf_op jit(solution)/shard_map/experts/pallas_call | solution.py:667
  325.0 49.9 %experts.5 = (bf16[2,3,352,1024]{3,2,1,0:T(8,128)(2,1)}, bf16[2,3,352,1024]{3,2,1,0:T(8,128)(2,1)}, bf16[640,2048]{1,0:T(8,128)(2,1)}, bf16[640,2048]{1,0:T(8,12...) custom-call(s32[1]{0:T(128)} %bitcast.37.refs_0_.table, ...), custom_call_target="tpu_custom_call" | custom-call | flops 1 | bytes 1 | tf_op jit(solution)/shard_map/experts/pallas_call | solution.py:667
  375.6 5.2 sums.8
  380.7 2.5 collective-permute-start.16
  385.2 84.0 %rows.4 = (f32[160,2048]{1,0:T(8,128)}, f32[160,2048]{1,0:T(8,128)}, bf16[640,2048]{1,0:T(8,128)(2,1)}) custom-call(bf16[640,2048]{1,0:T(8,128)(2,1)} %get-tuple-element.119.refs_0_, bf16[640,2048]{1,0:T(8,128)(2,1)} %get-tuple-element.123.refs_1_, bf16[640,2048]{1,0:T(8,128)(2,1)} %get-tuple-element.127.refs_2_, ...), custom_call_target="tpu_custom_call" | custom-call | flops 1 | bytes 1 | tf_op jit(solution)/shard_map/rows/pallas_call | solution.py:343
  469.3 5.1 sums.9
  474.5 19.5 %attend_back.1 = (bf16[3,640,512]{2,1,0:T(8,128)(2,1)}, f32[3,512]{1,0:T(4,128)}, bf16[640,2048]{1,0:T(8,128)(2,1)}) custom-call(s32[1,2]{1,0:T(1,128)} %starts.3, bf16[640,2048]{1,0:T(8,128)(2,1)} %get-tuple-element.150.grad.branch_grad, bf16[3,1024,512]{2,1,0:T(8,128)(2,1)} %w_own.3, bf16[3,1024,512]{2,1,0:T(8,128)(2,1)} %pad_maximum_fusion.2.w_oth, ...), custom_call_target="tpu_custom_call" | custom-call | flops 1 | bytes 1 | tf_op jit(solution)/shard_map/attend_back/pallas_call | solution.py:518
  494.0 49.5 %rows.5 = f32[160,2048]{1,0:T(8,128)} custom-call(bf16[640,2048]{1,0:T(8,128)(2,1)} %get-tuple-element.142.refs_0_), custom_call_target="tpu_custom_call" | custom-call | flops 1 | bytes 1 | tf_op jit(solution)/shard_map/rows/pallas_call | solution.py:343
  543.5 5.7 collective-permute-done.17
  549.2 3.5 sums.10.refs_0_
  552.7 2.0 copy-done
  554.7 10.0 %dense_grads.1 = (bf16[3,1024,256]{2,1,0:T(8,128)(2,1)S(1)}, bf16[3,1024,256]{2,1,0:T(8,128)(2,1)S(1)}, bf16[3,2048,256]{2,1,0:T(8,128)(2,1)}, bf16[256,1024]{1,...) custom-call(s32[1]{0:T(128)} %bitcast.33.core, ...), custom_call_target="tpu_custom_call" | custom-call | flops 1 | bytes 1 | tf_op jit(solution)/shard_map/dense_grads/pallas_call | solution.py:760
  570.2 2.3 copy-done.1
  572.4 6.1 sums.13
  580.2 6.2 sums.14
  590.4 3.1 add_convert_fusion.2
  594.9 4.6 collective-permute-done.27
  608.5 5.3 sums.12
  614.0 3.2 place.10.refs_0_
  617.8 19.4 %collective-permute-done.21 = bf16[3,1024,256]{2,1,0:T(8,128)(2,1)} collective-permute-done((bf16[3,1024,256]{2,1,0:T(8,128)(2,1)}, bf16[3,1024,256]{2,1,0:T(8,128)(2,1)}, u32[]{:S(2)}, u32[]{:S(2)}) %collective-permute-start.21) | collective-permute-done | bytes 1572896 | tf_op jit(solution)/shard_map/ppermute | solution.py:34
  638.6 2.6 add_convert_fusion.1
  641.2 6.1 collective-permute-done.24
  649.3 12.9 %shared.1 = (f32[1024,2,1408]{2,1,0:T(2,128)}, f32[1408,1024]{1,0:T(8,128)}) custom-call(s32[8]{0:T(128)S(1)} %pad_add_fusion.table, bf16[2,3,352,1024]{3,2,1,0:T(8,128)(2,1)} %bitcast.49.mine, bf16[2,3,352,1024]{3,2,1,0:T(8,128)(2,1)} %collective-permute-done.26.peer), custom_call_target="tpu_custom_call" | custom-call | flops 1 | bytes 1 | tf_op jit(solution)/shard_map/shared/pallas_call | solution.py:811
  662.1 4.8 place.8.refs_0_
  667.0 2.8 place.11.refs_0_
  669.7 4.8 place.9.refs_0_
  674.5 6.1 sums.15
  682.2 2.8 place.13.refs_0_
  684.9 4.9 place.12.refs_0_
  689.9 9.1 %collective-permute-done.22 = bf16[3,1024,256]{2,1,0:T(8,128)(2,1)} collective-permute-done((bf16[3,1024,256]{2,1,0:T(8,128)(2,1)S(1)}, bf16[3,1024,256]{2,1,0:T(8,128)(2,1)}, u32[]{:S(2)}, u32[]{:S(2)}) %collective-permute-start.22) | collective-permute-done | bytes 1572896 | tf_op jit(solution)/shard_map/ppermute | solution.py:39
  702.9 7.0 collective-permute-done.34
  715.7 4.7 fusion
  722.8 2.8 place.15
  725.6 4.8 place.14
  (274 shorter events, 82.9 us)
Async XLA Ops:
  7.2 69.5 %all-gather.3.cloned.1.call-start = ((), (), s32[]{:S(2)}) async-start(), calls=%async_computation.1 | async-start | bytes 3276800 | tf_op jit(solution)/shard_map/all_gather | solution.py:873
  7.2 12.5 %collective-permute-start = (bf16[2,1024]{1,0:T(2,128)(2,1)}, bf16[2,1024]{1,0:T(2,128)(2,1)S(1)}, u32[]{:S(2)}, u32[]{:S(2)}) collective-permute-start(bf16[2,1024]{1,0:T(2,128)(2,1)} %param.20), channel_id=1, source_target_pairs={{0,4},{4,0},{1,5},{5,1},{2,6},{6,2},{3,7},{7,3},{8,12},{12,8},{9,1... | collective-permute-start | bytes 12296 | tf_op jit(solution)/shard_map/ppermute | solution.py:34
  11.2 31.5 %collective-permute-start.6 = (bf16[128,1024]{1,0:T(8,128)(2,1)S(1)}, bf16[128,1024]{1,0:T(8,128)(2,1)S(1)}, u32[]{:S(2)}, u32[]{:S(2)}) collective-permute-start(bf16[128,1024]{1,0:T(8,128)(2,1)S(1)} %constant_dynamic-slice_fusion.4), channel_id=1, source_target_pairs={{0,4},{4,0},{1,5},{5,1},{2,6},{6,2},{3,7},{7,3},{8,12},{12,8},{9,1... | collective-permute-start | bytes 786440 | tf_op jit(solution)/shard_map/ppermute | solution.py:34
  12.6 27.8 %collective-permute-start.3 = (bf16[3,1024,128]{2,1,0:T(8,128)(2,1)S(1)}, bf16[3,1024,128]{2,1,0:T(8,128)(2,1)S(1)}, u32[]{:S(2)}, u32[]{:S(2)}) collective-permute-start(bf16[3,1024,128]{2,1,0:T(8,128)(2,1)S(1)} %constant_dynamic-slice_fusion.5), channel_id=1, source_target_pairs={{0,4},{4,0},{1,5},{5,1},{2,6},{6,2},{3,7},{7,3},{8,12},{12,8},{9,1... | collective-permute-start | bytes 2359304 | tf_op jit(solution)/shard_map/ppermute | solution.py:34
  21.5 184.8 %all-gather.5.cloned.1.call-start = ((), (), s32[]{:S(2)}) async-start(), calls=%async_computation.2 | async-start | bytes 3276800 | tf_op jit(solution)/shard_map/all_gather | solution.py:929
  21.6 45.3 %collective-permute-start.1 = (s32[640,4]{0,1:T(4,128)S(1)}, s32[640,4]{0,1:T(4,128)S(1)}, u32[]{:S(2)}, u32[]{:S(2)}) collective-permute-start(s32[640,4]{0,1:T(4,128)S(1)} %copy-done.34), channel_id=1, source_target_pairs={{0,8},{8,0},{16,24},{24,16},{1,9},{9,1},{17,25},{25,17},{2,10},{10... | collective-permute-start | bytes 30728 | tf_op jit(solution)/shard_map/ppermute | solution.py:44
  21.7 45.2 %collective-permute-start.2 = (bf16[1,9984]{1,0:T(2,128)(2,1)S(1)}, bf16[1,9984]{1,0:T(2,128)(2,1)S(1)}, u32[]{:S(2)}, u32[]{:S(2)}) collective-permute-start(bf16[1,9984]{1,0:T(2,128)(2,1)S(1)} %broadcast_in_dim.52), channel_id=1, source_target_pairs={{0,4},{4,0},{1,5},{5,1},{2,6},{6,2},{3,7},{7,3},{8,12},{12,8},{9,1... | collective-permute-start | bytes 59912 | tf_op jit(solution)/shard_map/ppermute | solution.py:34
  40.4 25.7 %collective-permute-start.4 = (bf16[3,1024,128]{2,1,0:T(8,128)(2,1)S(1)}, bf16[3,1024,128]{2,1,0:T(8,128)(2,1)S(1)}, u32[]{:S(2)}, u32[]{:S(2)}) collective-permute-start(bf16[3,1024,128]{2,1,0:T(8,128)(2,1)S(1)} %collective-permute-done.3), channel_id=1, source_target_pairs={{0,16},{8,24},{16,0},{24,8},{1,17},{9,25},{17,1},{25,9},{2,18},{10... | collective-permute-start | bytes 2359304 | tf_op jit(solution)/shard_map/ppermute | solution.py:39
  42.7 23.3 %collective-permute-start.7 = (bf16[128,1024]{1,0:T(8,128)(2,1)S(1)}, bf16[128,1024]{1,0:T(8,128)(2,1)S(1)}, u32[]{:S(2)}, u32[]{:S(2)}) collective-permute-start(bf16[128,1024]{1,0:T(8,128)(2,1)S(1)} %collective-permute-done.6), channel_id=1, source_target_pairs={{0,16},{8,24},{16,0},{24,8},{1,17},{9,25},{17,1},{25,9},{2,18},{10... | collective-permute-start | bytes 786440 | tf_op jit(solution)/shard_map/ppermute | solution.py:39
  66.1 2.0 collective-permute-start.8
  66.3 4.1 collective-permute-start.5
  76.8 643.6 %reduce-scatter.2.cloned.1.call-start = ((), (), s32[]{:S(2)}) async-start(), calls=%async_computation.3 | async-start | bytes 3276800 | tf_op jit(solution)/shard_map/reduce_scatter | solution.py:1069
  83.0 131.6 %collective-permute-start.11 = (bf16[2,3,352,1024]{3,2,1,0:T(8,128)(2,1)}, bf16[2,3,352,1024]{3,2,1,0:T(8,128)(2,1)}, u32[]{:S(2)}, u32[]{:S(2)}) collective-permute-start(bf16[2,3,352,1024]{3,2,1,0:T(8,128)(2,1)} %pad_maximum_fusion.1.refs_6_), channel_id=1, source_target_pairs={{0,4},{4,0},{1,5},{5,1},{2,6},{6,2},{3,7},{7,3},{8,12},{12,8},{9,1... | collective-permute-start | bytes 12976136 | tf_op jit(solution)/shard_map/ppermute | solution.py:34
  84.8 186.4 %collective-permute-start.13 = (bf16[2,3,352,1024]{3,2,1,0:T(8,128)(2,1)}, bf16[2,3,352,1024]{3,2,1,0:T(8,128)(2,1)}, u32[]{:S(2)}, u32[]{:S(2)}) collective-permute-start(bf16[2,3,352,1024]{3,2,1,0:T(8,128)(2,1)} %pad_maximum_fusion.refs_6_), channel_id=1, source_target_pairs={{0,4},{4,0},{1,5},{5,1},{2,6},{6,2},{3,7},{7,3},{8,12},{12,8},{9,1... | collective-permute-start | bytes 12976136 | tf_op jit(solution)/shard_map/ppermute | solution.py:34
  208.3 8.7 %collective-permute-start.10 = (bf16[320,2048]{1,0:T(8,128)(2,1)S(1)}, bf16[320,2048]{1,0:T(8,128)(2,1)S(1)}, u32[]{:S(2)}, u32[]{:S(2)}) collective-permute-start(bf16[320,2048]{1,0:T(8,128)(2,1)S(1)} %get-tuple-element.203), channel_id=1, source_target_pairs={{0,8},{8,0},{16,24},{24,16},{1,9},{9,1},{17,25},{25,17},{2,10},{10... | collective-permute-start | bytes 3932168 | tf_op jit(solution)/shard_map/ppermute | solution.py:44
  208.7 8.3 %collective-permute-start.9 = (bf16[320,2048]{1,0:T(8,128)(2,1)S(1)}, bf16[320,2048]{1,0:T(8,128)(2,1)S(1)}, u32[]{:S(2)}, u32[]{:S(2)}) collective-permute-start(bf16[320,2048]{1,0:T(8,128)(2,1)S(1)} %get-tuple-element.204), channel_id=1, source_target_pairs={{0,8},{8,0},{16,24},{24,16},{1,9},{9,1},{17,25},{25,17},{2,10},{10... | collective-permute-start | bytes 3932168 | tf_op jit(solution)/shard_map/ppermute | solution.py:44
  214.6 110.3 %collective-permute-start.14 = (bf16[2,3,352,1024]{3,2,1,0:T(8,128)(2,1)}, bf16[2,3,352,1024]{3,2,1,0:T(8,128)(2,1)}, u32[]{:S(2)}, u32[]{:S(2)}) collective-permute-start(bf16[2,3,352,1024]{3,2,1,0:T(8,128)(2,1)} %collective-permute-done.11.refs_7_), channel_id=1, source_target_pairs={{0,16},{8,24},{16,0},{24,8},{1,17},{9,25},{17,1},{25,9},{2,18},{10... | collective-permute-start | bytes 12976136 | tf_op jit(solution)/shard_map/ppermute | solution.py:39
  268.1 107.5 %collective-permute-start.12 = (bf16[2,3,352,1024]{3,2,1,0:T(8,128)(2,1)}, bf16[2,3,352,1024]{3,2,1,0:T(8,128)(2,1)}, u32[]{:S(2)}, u32[]{:S(2)}) collective-permute-start(bf16[2,3,352,1024]{3,2,1,0:T(8,128)(2,1)} %get-tuple-element.118), channel_id=1, source_target_pairs={{0,4},{4,0},{1,5},{5,1},{2,6},{6,2},{3,7},{7,3},{8,12},{12,8},{9,1... | collective-permute-start | bytes 12976136 | tf_op jit(solution)/shard_map/ppermute | solution.py:34
  320.3 149.0 %collective-permute-start.15 = (bf16[2,3,352,1024]{3,2,1,0:T(8,128)(2,1)}, bf16[2,3,352,1024]{3,2,1,0:T(8,128)(2,1)}, u32[]{:S(2)}, u32[]{:S(2)}) collective-permute-start(bf16[2,3,352,1024]{3,2,1,0:T(8,128)(2,1)} %get-tuple-element.135), channel_id=1, source_target_pairs={{0,4},{4,0},{1,5},{5,1},{2,6},{6,2},{3,7},{7,3},{8,12},{12,8},{9,1... | collective-permute-start | bytes 12976136 | tf_op jit(solution)/shard_map/ppermute | solution.py:34
  325.0 50.6 %slice-start.4 = ((s8[4325376]{0:T(1024)(128)(4,1)}), s8[4194304]{0:T(1024)(128)(4,1)S(1)}, s32[]{:S(2)}) async-start(s8[4325376]{0:T(1024)(128)(4,1)} %bitcast.112), calls=%async_computation.8 | async-start | bytes 8388608
  325.0 50.6 %slice-start.5 = ((s8[4325376]{0:T(1024)(128)(4,1)}), s8[131072]{0:T(1024)(128)(4,1)S(1)}, s32[]{:S(2)}) async-start(s8[4325376]{0:T(1024)(128)(4,1)} %bitcast.112), calls=%async_computation.9 | async-start | bytes 262144
  374.9 174.3 %collective-permute-start.17 = (bf16[2,3,352,1024]{3,2,1,0:T(8,128)(2,1)}, bf16[2,3,352,1024]{3,2,1,0:T(8,128)(2,1)}, u32[]{:S(2)}, u32[]{:S(2)}) collective-permute-start(bf16[2,3,352,1024]{3,2,1,0:T(8,128)(2,1)} %get-tuple-element.147), channel_id=1, source_target_pairs={{0,4},{4,0},{1,5},{5,1},{2,6},{6,2},{3,7},{7,3},{8,12},{12,8},{9,1... | collective-permute-start | bytes 12976136 | tf_op jit(solution)/shard_map/ppermute | solution.py:34
  380.7 113.2 %collective-permute-start.16 = (bf16[2,3,352,1024]{3,2,1,0:T(8,128)(2,1)}, bf16[2,3,352,1024]{3,2,1,0:T(8,128)(2,1)}, u32[]{:S(2)}, u32[]{:S(2)}) collective-permute-start(bf16[2,3,352,1024]{3,2,1,0:T(8,128)(2,1)} %bitcast.36), channel_id=1, source_target_pairs={{0,16},{8,24},{16,0},{24,8},{1,17},{9,25},{17,1},{25,9},{2,18},{10... | collective-permute-start | bytes 12976136 | tf_op jit(solution)/shard_map/ppermute | solution.py:39
  385.2 84.0 %slice-start = ((s8[4325376]{0:T(1024)(128)(4,1)}), s8[4194304]{0:T(1024)(128)(4,1)S(1)}, s32[]{:S(2)}) async-start(s8[4325376]{0:T(1024)(128)(4,1)} %bitcast.106), calls=%async_computation.4 | async-start | bytes 8388608
  385.2 84.0 %slice-start.1 = ((s8[4325376]{0:T(1024)(128)(4,1)}), s8[131072]{0:T(1024)(128)(4,1)S(1)}, s32[]{:S(2)}) async-start(s8[4325376]{0:T(1024)(128)(4,1)} %bitcast.106), calls=%async_computation.5 | async-start | bytes 262144
  474.4 105.2 %collective-permute-start.20 = (bf16[2,3,352,1024]{3,2,1,0:T(8,128)(2,1)}, bf16[2,3,352,1024]{3,2,1,0:T(8,128)(2,1)}, u32[]{:S(2)}, u32[]{:S(2)}) collective-permute-start(bf16[2,3,352,1024]{3,2,1,0:T(8,128)(2,1)} %bitcast.41), channel_id=1, source_target_pairs={{0,16},{8,24},{16,0},{24,8},{1,17},{9,25},{17,1},{25,9},{2,18},{10... | collective-permute-start | bytes 12976136 | tf_op jit(solution)/shard_map/ppermute | solution.py:39
  474.5 74.7 %slice-start.2 = ((s8[4325376]{0:T(1024)(128)(4,1)}), s8[4194304]{0:T(1024)(128)(4,1)S(1)}, s32[]{:S(2)}) async-start(s8[4325376]{0:T(1024)(128)(4,1)} %bitcast.109), calls=%async_computation.6 | async-start | bytes 8388608
  474.5 74.7 %slice-start.3 = ((s8[4325376]{0:T(1024)(128)(4,1)}), s8[131072]{0:T(1024)(128)(4,1)S(1)}, s32[]{:S(2)}) async-start(s8[4325376]{0:T(1024)(128)(4,1)} %bitcast.109), calls=%async_computation.7 | async-start | bytes 262144
  567.9 22.4 %collective-permute-start.19 = (bf16[3,2048,256]{2,1,0:T(8,128)(2,1)}, bf16[3,2048,256]{2,1,0:T(8,128)(2,1)}, u32[]{:S(2)}, u32[]{:S(2)}) collective-permute-start(bf16[3,2048,256]{2,1,0:T(8,128)(2,1)} %get-tuple-element.151), channel_id=1, source_target_pairs={{0,8},{8,0},{16,24},{24,16},{1,9},{9,1},{17,25},{25,17},{2,10},{10... | collective-permute-start | bytes 9437192 | tf_op jit(solution)/shard_map/ppermute | solution.py:44
  567.9 18.4 %collective-permute-start.23 = (bf16[256,2048]{1,0:T(8,128)(2,1)}, bf16[256,2048]{1,0:T(8,128)(2,1)}, u32[]{:S(2)}, u32[]{:S(2)}) collective-permute-start(bf16[256,2048]{1,0:T(8,128)(2,1)} %get-tuple-element.170), channel_id=1, source_target_pairs={{0,8},{8,0},{16,24},{24,16},{1,9},{9,1},{17,25},{25,17},{2,10},{10... | collective-permute-start | bytes 3145736 | tf_op jit(solution)/shard_map/ppermute | solution.py:44
  568.6 105.9 %collective-permute-start.31 = (bf16[2,3,352,1024]{3,2,1,0:T(8,128)(2,1)}, bf16[2,3,352,1024]{3,2,1,0:T(8,128)(2,1)}, u32[]{:S(2)}, u32[]{:S(2)}) collective-permute-start(bf16[2,3,352,1024]{3,2,1,0:T(8,128)(2,1)} %bitcast.105), channel_id=1, source_target_pairs={{0,16},{8,24},{16,0},{24,8},{1,17},{9,25},{17,1},{25,9},{2,18},{10... | collective-permute-start | bytes 12976136 | tf_op jit(solution)/shard_map/ppermute | solution.py:39
  578.5 88.4 %collective-permute-start.25 = (bf16[2,3,352,1024]{3,2,1,0:T(8,128)(2,1)}, bf16[2,3,352,1024]{3,2,1,0:T(8,128)(2,1)}, u32[]{:S(2)}, u32[]{:S(2)}) collective-permute-start(bf16[2,3,352,1024]{3,2,1,0:T(8,128)(2,1)} %bitcast.46.source), channel_id=1, source_target_pairs={{0,8},{8,0},{16,24},{24,16},{1,9},{9,1},{17,25},{25,17},{2,10},{10... | collective-permute-start | bytes 12976136 | tf_op jit(solution)/shard_map/ppermute | solution.py:44
  579.6 21.7 %collective-permute-start.18 = (bf16[640,2048]{1,0:T(8,128)(2,1)S(1)}, bf16[640,2048]{1,0:T(8,128)(2,1)}, u32[]{:S(2)}, u32[]{:S(2)}) collective-permute-start(bf16[640,2048]{1,0:T(8,128)(2,1)S(1)} %sums.11), channel_id=1, source_target_pairs={{0,8},{8,0},{16,24},{24,16},{1,9},{9,1},{17,25},{25,17},{2,10},{10... | collective-permute-start | bytes 7864328 | tf_op jit(solution)/shard_map/ppermute | solution.py:44
  586.4 62.9 %collective-permute-start.26 = (bf16[2,3,352,1024]{3,2,1,0:T(8,128)(2,1)}, bf16[2,3,352,1024]{3,2,1,0:T(8,128)(2,1)}, u32[]{:S(2)}, u32[]{:S(2)}) collective-permute-start(bf16[2,3,352,1024]{3,2,1,0:T(8,128)(2,1)} %bitcast.49.mine), channel_id=1, source_target_pairs={{0,8},{8,0},{16,24},{24,16},{1,9},{9,1},{17,25},{25,17},{2,10},{10... | collective-permute-start | bytes 12976136 | tf_op jit(solution)/shard_map/ppermute | solution.py:44
  593.9 5.6 collective-permute-start.27
  599.5 37.6 %collective-permute-start.21 = (bf16[3,1024,256]{2,1,0:T(8,128)(2,1)}, bf16[3,1024,256]{2,1,0:T(8,128)(2,1)}, u32[]{:S(2)}, u32[]{:S(2)}) collective-permute-start(bf16[3,1024,256]{2,1,0:T(8,128)(2,1)} %add_convert_fusion.2), channel_id=1, source_target_pairs={{0,4},{4,0},{1,5},{5,1},{2,6},{6,2},{3,7},{7,3},{8,12},{12,8},{9,1... | collective-permute-start | bytes 4718600 | tf_op jit(solution)/shard_map/ppermute | solution.py:34
  601.3 12.5 %collective-permute-start.28 = (f32[11,2048]{1,0:T(8,128)S(1)}, f32[11,2048]{1,0:T(8,128)S(1)}, u32[]{:S(2)}, u32[]{:S(2)}) collective-permute-start(f32[11,2048]{1,0:T(8,128)S(1)} %fusion.55), channel_id=1, source_target_pairs={{0,2},{1,3},{2,0},{3,1},{4,6},{5,7},{6,4},{7,5},{8,10},{9,11},{10,... | collective-permute-start | bytes 270344 | tf_op jit(solution)/shard_map/ppermute | solution.py:418
  613.8 3.3 collective-permute-start.29
  614.0 24.7 %copy-start.9 = (bf16[3,1024,256]{2,1,0:T(8,128)(2,1)S(1)}, bf16[3,1024,256]{2,1,0:T(8,128)(2,1)}, u32[]{:S(2)}) copy-start(bf16[3,1024,256]{2,1,0:T(8,128)(2,1)} %copy-done.8) | copy-start | bytes 4718596
  617.2 30.2 %collective-permute-start.24 = (bf16[256,1024]{1,0:T(8,128)(2,1)S(1)}, bf16[256,1024]{1,0:T(8,128)(2,1)S(1)}, u32[]{:S(2)}, u32[]{:S(2)}) collective-permute-start(bf16[256,1024]{1,0:T(8,128)(2,1)S(1)} %copy-done.32), channel_id=1, source_target_pairs={{0,4},{4,0},{1,5},{5,1},{2,6},{6,2},{3,7},{7,3},{8,12},{12,8},{9,1... | collective-permute-start | bytes 1572872 | tf_op jit(solution)/shard_map/ppermute | solution.py:34
  617.8 30.2 %copy-start.14 = (bf16[256,1024]{1,0:T(8,128)(2,1)S(1)}, bf16[256,1024]{1,0:T(8,128)(2,1)}, u32[]{:S(2)}) copy-start(bf16[256,1024]{1,0:T(8,128)(2,1)} %copy-done.13) | copy-start | bytes 1572868
  637.2 12.1 %collective-permute-start.30 = (f32[12,1024]{1,0:T(8,128)S(1)}, f32[12,1024]{1,0:T(8,128)S(1)}, u32[]{:S(2)}, u32[]{:S(2)}) collective-permute-start(f32[12,1024]{1,0:T(8,128)S(1)} %slice.157), channel_id=1, source_target_pairs={{0,4},{4,0},{1,5},{5,1},{2,6},{6,2},{3,7},{7,3},{8,12},{12,8},{9,1... | collective-permute-start | bytes 147464 | tf_op jit(solution)/shard_map/ppermute | solution.py:34
  647.3 51.6 %collective-permute-start.22 = (bf16[3,1024,256]{2,1,0:T(8,128)(2,1)S(1)}, bf16[3,1024,256]{2,1,0:T(8,128)(2,1)}, u32[]{:S(2)}, u32[]{:S(2)}) collective-permute-start(bf16[3,1024,256]{2,1,0:T(8,128)(2,1)S(1)} %add_convert_fusion.1), channel_id=1, source_target_pairs={{0,16},{8,24},{16,0},{24,8},{1,17},{9,25},{17,1},{25,9},{2,18},{10... | collective-permute-start | bytes 4718600 | tf_op jit(solution)/shard_map/ppermute | solution.py:39
  680.7 42.1 %collective-permute-start.36 = (bf16[2,3,352,1024]{3,2,1,0:T(8,128)(2,1)}, bf16[2,3,352,1024]{3,2,1,0:T(8,128)(2,1)}, u32[]{:S(2)}, u32[]{:S(2)}) collective-permute-start(bf16[2,3,352,1024]{3,2,1,0:T(8,128)(2,1)} %bitcast.57.source), channel_id=1, source_target_pairs={{0,8},{8,0},{16,24},{24,16},{1,9},{9,1},{17,25},{25,17},{2,10},{10... | collective-permute-start | bytes 12976136 | tf_op jit(solution)/shard_map/ppermute | solution.py:44
  680.7 29.2 %collective-permute-start.34 = (bf16[256,1024]{1,0:T(8,128)(2,1)S(1)}, bf16[256,1024]{1,0:T(8,128)(2,1)S(1)}, u32[]{:S(2)}, u32[]{:S(2)}) collective-permute-start(bf16[256,1024]{1,0:T(8,128)(2,1)S(1)} %add_convert_fusion.6), channel_id=1, source_target_pairs={{0,16},{8,24},{16,0},{24,8},{1,17},{9,25},{17,1},{25,9},{2,18},{10... | collective-permute-start | bytes 1572872 | tf_op jit(solution)/shard_map/ppermute | solution.py:39
  700.8 14.9 %collective-permute-start.32 = (bf16[3,1024,256]{2,1,0:T(8,128)(2,1)S(1)}, bf16[3,1024,256]{2,1,0:T(8,128)(2,1)}, u32[]{:S(2)}, u32[]{:S(2)}) collective-permute-start(bf16[3,1024,256]{2,1,0:T(8,128)(2,1)S(1)} %add_convert_fusion), channel_id=1, source_target_pairs={{0,8},{8,0},{16,24},{24,16},{1,9},{9,1},{17,25},{25,17},{2,10},{10... | collective-permute-start | bytes 4718600 | tf_op jit(solution)/shard_map/ppermute | solution.py:44
  701.3 10.0 %collective-permute-start.33 = (f32[12,1024]{1,0:T(8,128)S(1)}, f32[12,1024]{1,0:T(8,128)S(1)}, u32[]{:S(2)}, u32[]{:S(2)}) collective-permute-start(f32[12,1024]{1,0:T(8,128)S(1)} %slice_add_fusion.1), channel_id=1, source_target_pairs={{0,16},{8,24},{16,0},{24,8},{1,17},{9,25},{17,1},{25,9},{2,18},{10... | collective-permute-start | bytes 147464 | tf_op jit(solution)/shard_map/ppermute | solution.py:39
  710.0 3.9 collective-permute-start.35
  (39 other events, 223.9 us)
Sparse Core Ops, SparseCore 0:
  21.6 55.0 all-gather.2
  78.3 72.0 all-gather.4
  613.9 49.8 reduce-scatter.1

commit v5 on v4

--- a/solution.py
+++ b/solution.py
@@ -533,7 +533,7 @@
     else:
         x0, x1, c0, c10, c11, gate, w_own, w_oth, *refs = refs
     dw_own, dw_oth, mix0, mix1, ng0, ng1, gate_grad, *refs = refs
-    xv, cv, wgu, wd, ga, pre, ga_t, pre_t, st_mix, st_ng, st_dw, w_sem, x_sem, c_sem, out_sem, dw_sem = refs
+    xv, cv, wgu, wd, ga, pre, ga_t, pre_t, gu_all, st_mix, st_ng, st_dw, w_sem, x_sem, c_sem, out_sem, dw_sem = refs
     seq = rows // 2
     both = 2 * hidden
     oth_width = width - own_width
@@ -562,22 +562,20 @@
     for i, part in enumerate((c10, c11)):
         here = pl.ds(seq + i * part.shape[0], part.shape[0])
         c_copies.append(pltpu.make_async_copy(part, cv.at[here], c_sem.at[1 + i]))
-    order = [x_copies[0], *w_copies(0), *w_copies(1), c_copies[0], *w_copies(2)]
-    later = [x_copies[1], *c_copies[1:]]
-    for copy in order + later:
+    for_gate_up = [x_copies[0], *w_copies(0), *w_copies(1)]
+    for_down = [*w_copies(2), *c_copies]
+    for copy in [*for_gate_up, x_copies[1], *for_down]:
         copy.start()
-    for copy in order:
-        copy.wait()
+
+    def gate_up_tile(t, carry):
+        here = pl.ds(pl.multiple_of(t * COLS, COLS), COLS)
+        gu_all[:, here] = dot_nt(wgu[...], xv[here, :])
+        return carry
 
     def token_tile(t, carry):
-        @pl.when(t == seq // COLS)
-        def _():
-            for copy in later:
-                copy.wait()
-
         here = pl.ds(pl.multiple_of(t * COLS, COLS), COLS)
-        gu = dot_nt(wgu[...], xv[here, :])
         h = dot_nt(wd[...], cv[here, :])
+        gu = gu_all[:, here]
         g, u = gu[:both], gu[both:]
         sig = jax.nn.sigmoid(g)
         act = g * sig * u
@@ -600,6 +598,13 @@
         pre_t[here, both:] = pu_here.T
         return carry
 
+    for copy in for_gate_up:
+        copy.wait()
+    lax.fori_loop(0, seq // COLS, gate_up_tile, 0)
+    x_copies[1].wait()
+    lax.fori_loop(seq // COLS, rows // COLS, gate_up_tile, 0)
+    for copy in for_down:
+        copy.wait()
     lax.fori_loop(0, rows // COLS, token_tile, 0)
 
     def row_outs(slot, cols):
@@ -683,6 +688,7 @@
             pltpu.VMEM((4 * hidden, rows), BF16),
             pltpu.VMEM((rows, 2 * hidden), BF16),
             pltpu.VMEM((rows, 4 * hidden), BF16),
+            pltpu.VMEM((4 * hidden, rows), F32),
             pltpu.VMEM((2, rows, COLS), BF16),
             pltpu.VMEM((2, rows, COLS), BF16),
             pltpu.VMEM((2, 6 * hidden, COLS), BF16),

time: 746 us -> 746 us (level)
  no operation moved by 1% of the time
where the time goes in v5:
time: 746 us; the launch traced here: 738 us
  Pallas kernels  510 us (68%)
  waiting for transfers between devices  76.1 us (10%)
  local copies, waits for them, and re-layouts  56.4 us (8%)
  other arithmetic  43.1 us (6%)
  starting transfers between devices  32.5 us (4%)
  between operations  15.1 us (2%)
    pallas_call x3, Pallas kernels, rows_call(): pl.pallas_call(functools.partial(rows_kernel, n, rows, len(parts), bool(p...  233 us
    pallas_call x3, Pallas kernels, experts_call(): pl.pallas_call(functools.partial(experts_kernel, rows, width, own_width,...  148 us
    pallas_call x8, Pallas kernels, sum_call(): pl.pallas_call(sum_kernel, out_shape=jax.ShapeDtypeStruct((rows, columns)...  38.5 us
    ppermute x9, waiting for transfers between devices, swap_x(): return lax.ppermute(a, 'rep', [(i, i ^ 2) for i in range(n)])  36.4 us
    pallas_call x2, Pallas kernels, attention_call(): pl.pallas_call(functools.partial(kernel, heads, own_width), out_shape=out...  36.3 us
    ppermute x12, waiting for transfers between devices, swap_y(): return lax.ppermute(a, 'fsdp', [(0, 1), (1, 0)])  32.8 us
    pallas_call x8, Pallas kernels, place_call(): pl.pallas_call(place_kernel, out_shape=jax.ShapeDtypeStruct((EXPERTS, len...  30.9 us
    unnamed x101, local copies, waits for them, and re-layouts  19.4 us
  transfers between devices with their start and end apart: 40, of which 11 were waited for; matrix products, arithmetic and copies ran while one was open for 12% of the time, Pallas kernels for 68%

profile of v5, /device:TPU:0, one launch (start us, length us, event | category | flops | bytes accessed | tf_op | source)
XLA Modules:
  0.0 737.7 jit_solution(4681325249399768862)
XLA Ops:
  7.2 3.0 collective-permute-start
  14.6 2.2 fusion.21.refs_10_
  21.8 14.9 %copy.71 = bf16[1024,2,1408]{0,2,1:T(8,128)(2,1)} copy(bf16[1024,2,1408]{2,1,0:T(2,128)(2,1)} %param.28) | data formatting | bytes 11534336 | tf_op jit(solution)/shard_map/optimization_barrier | solution.py:922
  36.7 3.5 slice_bitcast_fusion
  43.2 2.4 pad_maximum_fusion.refs_6_
  45.7 20.4 %collective-permute-done.7 = bf16[128,1024]{1,0:T(8,128)(2,1)S(1)} collective-permute-done((bf16[128,1024]{1,0:T(8,128)(2,1)S(1)}, bf16[128,1024]{1,0:T(8,128)(2,1)S(1)}, u32[]{:S(2)}, u32[]{:S(2)}) %collective-permute-start.7) | collective-permute-done | bytes 262176 | tf_op jit(solution)/shard_map/ppermute | solution.py:39
  70.4 2.3 fusion.2
  78.8 2.1 constant_dynamic-slice_fusion.2
  80.9 2.4 pad_maximum_fusion.1.refs_6_
  85.7 16.8 %attend.1 = (bf16[640,512]{1,0:T(8,128)(2,1)}, bf16[640,512]{1,0:T(8,128)(2,1)}, bf16[640,512]{1,0:T(8,128)(2,1)}, bf16[640,512]{1,0:T(8,128)(2,1)}, f32[8,640]{1,0:T(8,128)}, /*index=5*/bf16[640,2048]{1,0:T(8,128)(2,1)}) custom-call(s32[1,2]{1,0:T(1,128)} %starts.3, bf16[640,2048]{1,0:T(8,128)(2,1)} %all-gather.3.cloned.1.call-done.rows, ...), custom_call_target="tpu_custom_call" | custom-call | flops 1 | bytes 1 | tf_op jit(solution)/shard_map/attend/pallas_call | solution.py:518
  102.5 100.1 %rows.3 = (f32[160,2048]{1,0:T(8,128)}, bf16[640,2048]{1,0:T(8,128)(2,1)}, bf16[640,2048]{1,0:T(8,128)(2,1)}) custom-call(bf16[640,2048]{1,0:T(8,128)(2,1)} %get-tuple-element.105.refs_0_, bf16[160,2048]{1,0:T(8,128)(2,1)} %copy-done.19, f32[1,2048]{1,0:T(1,128)} %get-tuple-element.213.refs_2_.refs_11_), custom_call_target="tpu_custom_call" | custom-call | flops 1 | bytes 1 | tf_op jit(solution)/shard_map/rows/pallas_call | solution.py:343
  202.7 3.6 constant_dynamic-update-slice_fusion.3
  210.6 3.9 fusion.48
  219.1 49.1 %experts.3 = (bf16[2,3,352,1024]{3,2,1,0:T(8,128)(2,1)}, bf16[2,3,352,1024]{3,2,1,0:T(8,128)(2,1)}, bf16[640,2048]{1,0:T(8,128)(2,1)}, bf16[640,2048]{1,0:T(8,12...) custom-call(bf16[640,2048]{1,0:T(8,128)(2,1)} %get-tuple-element.107.refs_0_.refs_1_, ...), custom_call_target="tpu_custom_call" | custom-call | flops 1 | bytes 1 | tf_op jit(solution)/shard_map/experts/pallas_call | solution.py:672
  271.6 49.2 %experts.4 = (bf16[2,3,352,1024]{3,2,1,0:T(8,128)(2,1)}, bf16[2,3,352,1024]{3,2,1,0:T(8,128)(2,1)}, bf16[640,2048]{1,0:T(8,128)(2,1)}, bf16[640,2048]{1,0:T(8,12...) custom-call(bf16[640,2048]{1,0:T(8,128)(2,1)} %get-tuple-element.107.refs_0_.refs_1_, ...), custom_call_target="tpu_custom_call" | custom-call | flops 1 | bytes 1 | tf_op jit(solution)/shard_map/experts/pallas_call | solution.py:672
  325.5 49.5 %experts.5 = (bf16[2,3,352,1024]{3,2,1,0:T(8,128)(2,1)}, bf16[2,3,352,1024]{3,2,1,0:T(8,128)(2,1)}, bf16[640,2048]{1,0:T(8,128)(2,1)}, bf16[640,2048]{1,0:T(8,12...) custom-call(s32[1]{0:T(128)} %bitcast.37.refs_0_.table, ...), custom_call_target="tpu_custom_call" | custom-call | flops 1 | bytes 1 | tf_op jit(solution)/shard_map/experts/pallas_call | solution.py:672
  375.7 5.2 sums.8
  380.9 2.5 collective-permute-start.16
  385.4 83.8 %rows.4 = (f32[160,2048]{1,0:T(8,128)}, f32[160,2048]{1,0:T(8,128)}, bf16[640,2048]{1,0:T(8,128)(2,1)}) custom-call(bf16[640,2048]{1,0:T(8,128)(2,1)} %get-tuple-element.119.refs_0_, bf16[640,2048]{1,0:T(8,128)(2,1)} %get-tuple-element.123.refs_1_, bf16[640,2048]{1,0:T(8,128)(2,1)} %get-tuple-element.127.refs_2_, ...), custom_call_target="tpu_custom_call" | custom-call | flops 1 | bytes 1 | tf_op jit(solution)/shard_map/rows/pallas_call | solution.py:343
  469.3 5.1 sums.9
  474.4 19.5 %attend_back.1 = (bf16[3,640,512]{2,1,0:T(8,128)(2,1)}, f32[3,512]{1,0:T(4,128)}, bf16[640,2048]{1,0:T(8,128)(2,1)}) custom-call(s32[1,2]{1,0:T(1,128)} %starts.3, bf16[640,2048]{1,0:T(8,128)(2,1)} %get-tuple-element.150.grad.branch_grad, bf16[3,1024,512]{2,1,0:T(8,128)(2,1)} %w_own.3, bf16[3,1024,512]{2,1,0:T(8,128)(2,1)} %pad_maximum_fusion.2.w_oth, ...), custom_call_target="tpu_custom_call" | custom-call | flops 1 | bytes 1 | tf_op jit(solution)/shard_map/attend_back/pallas_call | solution.py:518
  493.9 49.5 %rows.5 = f32[160,2048]{1,0:T(8,128)} custom-call(bf16[640,2048]{1,0:T(8,128)(2,1)} %get-tuple-element.142.refs_0_), custom_call_target="tpu_custom_call" | custom-call | flops 1 | bytes 1 | tf_op jit(solution)/shard_map/rows/pallas_call | solution.py:343
  543.4 6.1 collective-permute-done.17
  549.5 3.5 sums.10.refs_0_
  553.0 2.0 copy-done
  555.1 10.0 %dense_grads.1 = (bf16[3,1024,256]{2,1,0:T(8,128)(2,1)S(1)}, bf16[3,1024,256]{2,1,0:T(8,128)(2,1)S(1)}, bf16[3,2048,256]{2,1,0:T(8,128)(2,1)}, bf16[256,1024]{1,...) custom-call(s32[1]{0:T(128)} %bitcast.33.core, ...), custom_call_target="tpu_custom_call" | custom-call | flops 1 | bytes 1 | tf_op jit(solution)/shard_map/dense_grads/pallas_call | solution.py:766
  570.5 2.3 copy-done.1
  572.8 6.1 sums.13
  580.5 6.2 sums.14
  590.7 3.1 add_convert_fusion.2
  595.2 4.6 collective-permute-done.27
  608.8 5.3 sums.12
  614.3 3.2 place.10.refs_0_
  618.1 19.4 %collective-permute-done.21 = bf16[3,1024,256]{2,1,0:T(8,128)(2,1)} collective-permute-done((bf16[3,1024,256]{2,1,0:T(8,128)(2,1)}, bf16[3,1024,256]{2,1,0:T(8,128)(2,1)}, u32[]{:S(2)}, u32[]{:S(2)}) %collective-permute-start.21) | collective-permute-done | bytes 1572896 | tf_op jit(solution)/shard_map/ppermute | solution.py:34
  639.0 2.6 add_convert_fusion.1
  641.6 6.1 collective-permute-done.24
  649.6 12.9 %shared.1 = (f32[1024,2,1408]{2,1,0:T(2,128)}, f32[1408,1024]{1,0:T(8,128)}) custom-call(s32[8]{0:T(128)S(1)} %pad_add_fusion.table, bf16[2,3,352,1024]{3,2,1,0:T(8,128)(2,1)} %bitcast.49.mine, bf16[2,3,352,1024]{3,2,1,0:T(8,128)(2,1)} %collective-permute-done.26.peer), custom_call_target="tpu_custom_call" | custom-call | flops 1 | bytes 1 | tf_op jit(solution)/shard_map/shared/pallas_call | solution.py:817
  662.5 4.8 place.8.refs_0_
  667.3 2.8 place.11.refs_0_
  670.1 4.8 place.9.refs_0_
  674.9 6.1 sums.15
  682.5 2.8 place.13.refs_0_
  685.3 4.9 place.12.refs_0_
  690.2 9.1 %collective-permute-done.22 = bf16[3,1024,256]{2,1,0:T(8,128)(2,1)} collective-permute-done((bf16[3,1024,256]{2,1,0:T(8,128)(2,1)S(1)}, bf16[3,1024,256]{2,1,0:T(8,128)(2,1)}, u32[]{:S(2)}, u32[]{:S(2)}) %collective-permute-start.22) | collective-permute-done | bytes 1572896 | tf_op jit(solution)/shard_map/ppermute | solution.py:39
  703.2 7.0 collective-permute-done.34
  716.0 4.7 fusion
  723.1 2.8 place.15
  725.9 4.8 place.14
  (274 shorter events, 83.5 us)
Async XLA Ops:
  7.2 69.5 %all-gather.3.cloned.1.call-start = ((), (), s32[]{:S(2)}) async-start(), calls=%async_computation.1 | async-start | bytes 3276800 | tf_op jit(solution)/shard_map/all_gather | solution.py:879
  7.2 12.5 %collective-permute-start = (bf16[2,1024]{1,0:T(2,128)(2,1)}, bf16[2,1024]{1,0:T(2,128)(2,1)S(1)}, u32[]{:S(2)}, u32[]{:S(2)}) collective-permute-start(bf16[2,1024]{1,0:T(2,128)(2,1)} %param.20), channel_id=1, source_target_pairs={{0,4},{4,0},{1,5},{5,1},{2,6},{6,2},{3,7},{7,3},{8,12},{12,8},{9,1... | collective-permute-start | bytes 12296 | tf_op jit(solution)/shard_map/ppermute | solution.py:34
  11.2 31.5 %collective-permute-start.6 = (bf16[128,1024]{1,0:T(8,128)(2,1)S(1)}, bf16[128,1024]{1,0:T(8,128)(2,1)S(1)}, u32[]{:S(2)}, u32[]{:S(2)}) collective-permute-start(bf16[128,1024]{1,0:T(8,128)(2,1)S(1)} %constant_dynamic-slice_fusion.4), channel_id=1, source_target_pairs={{0,4},{4,0},{1,5},{5,1},{2,6},{6,2},{3,7},{7,3},{8,12},{12,8},{9,1... | collective-permute-start | bytes 786440 | tf_op jit(solution)/shard_map/ppermute | solution.py:34
  12.6 27.8 %collective-permute-start.3 = (bf16[3,1024,128]{2,1,0:T(8,128)(2,1)S(1)}, bf16[3,1024,128]{2,1,0:T(8,128)(2,1)S(1)}, u32[]{:S(2)}, u32[]{:S(2)}) collective-permute-start(bf16[3,1024,128]{2,1,0:T(8,128)(2,1)S(1)} %constant_dynamic-slice_fusion.5), channel_id=1, source_target_pairs={{0,4},{4,0},{1,5},{5,1},{2,6},{6,2},{3,7},{7,3},{8,12},{12,8},{9,1... | collective-permute-start | bytes 2359304 | tf_op jit(solution)/shard_map/ppermute | solution.py:34
  21.5 184.8 %all-gather.5.cloned.1.call-start = ((), (), s32[]{:S(2)}) async-start(), calls=%async_computation.2 | async-start | bytes 3276800 | tf_op jit(solution)/shard_map/all_gather | solution.py:935
  21.6 45.3 %collective-permute-start.1 = (s32[640,4]{0,1:T(4,128)S(1)}, s32[640,4]{0,1:T(4,128)S(1)}, u32[]{:S(2)}, u32[]{:S(2)}) collective-permute-start(s32[640,4]{0,1:T(4,128)S(1)} %copy-done.34), channel_id=1, source_target_pairs={{0,8},{8,0},{16,24},{24,16},{1,9},{9,1},{17,25},{25,17},{2,10},{10... | collective-permute-start | bytes 30728 | tf_op jit(solution)/shard_map/ppermute | solution.py:44
  21.7 45.2 %collective-permute-start.2 = (bf16[1,9984]{1,0:T(2,128)(2,1)S(1)}, bf16[1,9984]{1,0:T(2,128)(2,1)S(1)}, u32[]{:S(2)}, u32[]{:S(2)}) collective-permute-start(bf16[1,9984]{1,0:T(2,128)(2,1)S(1)} %broadcast_in_dim.52), channel_id=1, source_target_pairs={{0,4},{4,0},{1,5},{5,1},{2,6},{6,2},{3,7},{7,3},{8,12},{12,8},{9,1... | collective-permute-start | bytes 59912 | tf_op jit(solution)/shard_map/ppermute | solution.py:34
  40.4 25.7 %collective-permute-start.4 = (bf16[3,1024,128]{2,1,0:T(8,128)(2,1)S(1)}, bf16[3,1024,128]{2,1,0:T(8,128)(2,1)S(1)}, u32[]{:S(2)}, u32[]{:S(2)}) collective-permute-start(bf16[3,1024,128]{2,1,0:T(8,128)(2,1)S(1)} %collective-permute-done.3), channel_id=1, source_target_pairs={{0,16},{8,24},{16,0},{24,8},{1,17},{9,25},{17,1},{25,9},{2,18},{10... | collective-permute-start | bytes 2359304 | tf_op jit(solution)/shard_map/ppermute | solution.py:39
  42.7 23.3 %collective-permute-start.7 = (bf16[128,1024]{1,0:T(8,128)(2,1)S(1)}, bf16[128,1024]{1,0:T(8,128)(2,1)S(1)}, u32[]{:S(2)}, u32[]{:S(2)}) collective-permute-start(bf16[128,1024]{1,0:T(8,128)(2,1)S(1)} %collective-permute-done.6), channel_id=1, source_target_pairs={{0,16},{8,24},{16,0},{24,8},{1,17},{9,25},{17,1},{25,9},{2,18},{10... | collective-permute-start | bytes 786440 | tf_op jit(solution)/shard_map/ppermute | solution.py:39
  66.1 2.0 collective-permute-start.8
  66.3 4.1 collective-permute-start.5
  76.8 643.9 %reduce-scatter.2.cloned.1.call-start = ((), (), s32[]{:S(2)}) async-start(), calls=%async_computation.3 | async-start | bytes 3276800 | tf_op jit(solution)/shard_map/reduce_scatter | solution.py:1075
  83.4 131.3 %collective-permute-start.11 = (bf16[2,3,352,1024]{3,2,1,0:T(8,128)(2,1)}, bf16[2,3,352,1024]{3,2,1,0:T(8,128)(2,1)}, u32[]{:S(2)}, u32[]{:S(2)}) collective-permute-start(bf16[2,3,352,1024]{3,2,1,0:T(8,128)(2,1)} %pad_maximum_fusion.1.refs_6_), channel_id=1, source_target_pairs={{0,4},{4,0},{1,5},{5,1},{2,6},{6,2},{3,7},{7,3},{8,12},{12,8},{9,1... | collective-permute-start | bytes 12976136 | tf_op jit(solution)/shard_map/ppermute | solution.py:34
  85.1 186.5 %collective-permute-start.13 = (bf16[2,3,352,1024]{3,2,1,0:T(8,128)(2,1)}, bf16[2,3,352,1024]{3,2,1,0:T(8,128)(2,1)}, u32[]{:S(2)}, u32[]{:S(2)}) collective-permute-start(bf16[2,3,352,1024]{3,2,1,0:T(8,128)(2,1)} %pad_maximum_fusion.refs_6_), channel_id=1, source_target_pairs={{0,4},{4,0},{1,5},{5,1},{2,6},{6,2},{3,7},{7,3},{8,12},{12,8},{9,1... | collective-permute-start | bytes 12976136 | tf_op jit(solution)/shard_map/ppermute | solution.py:34
  208.3 8.7 %collective-permute-start.10 = (bf16[320,2048]{1,0:T(8,128)(2,1)S(1)}, bf16[320,2048]{1,0:T(8,128)(2,1)S(1)}, u32[]{:S(2)}, u32[]{:S(2)}) collective-permute-start(bf16[320,2048]{1,0:T(8,128)(2,1)S(1)} %get-tuple-element.203), channel_id=1, source_target_pairs={{0,8},{8,0},{16,24},{24,16},{1,9},{9,1},{17,25},{25,17},{2,10},{10... | collective-permute-start | bytes 3932168 | tf_op jit(solution)/shard_map/ppermute | solution.py:44
  208.7 8.3 %collective-permute-start.9 = (bf16[320,2048]{1,0:T(8,128)(2,1)S(1)}, bf16[320,2048]{1,0:T(8,128)(2,1)S(1)}, u32[]{:S(2)}, u32[]{:S(2)}) collective-permute-start(bf16[320,2048]{1,0:T(8,128)(2,1)S(1)} %get-tuple-element.204), channel_id=1, source_target_pairs={{0,8},{8,0},{16,24},{24,16},{1,9},{9,1},{17,25},{25,17},{2,10},{10... | collective-permute-start | bytes 3932168 | tf_op jit(solution)/shard_map/ppermute | solution.py:44
  214.6 110.9 %collective-permute-start.14 = (bf16[2,3,352,1024]{3,2,1,0:T(8,128)(2,1)}, bf16[2,3,352,1024]{3,2,1,0:T(8,128)(2,1)}, u32[]{:S(2)}, u32[]{:S(2)}) collective-permute-start(bf16[2,3,352,1024]{3,2,1,0:T(8,128)(2,1)} %collective-permute-done.11.refs_7_), channel_id=1, source_target_pairs={{0,16},{8,24},{16,0},{24,8},{1,17},{9,25},{17,1},{25,9},{2,18},{10... | collective-permute-start | bytes 12976136 | tf_op jit(solution)/shard_map/ppermute | solution.py:39
  268.2 107.5 %collective-permute-start.12 = (bf16[2,3,352,1024]{3,2,1,0:T(8,128)(2,1)}, bf16[2,3,352,1024]{3,2,1,0:T(8,128)(2,1)}, u32[]{:S(2)}, u32[]{:S(2)}) collective-permute-start(bf16[2,3,352,1024]{3,2,1,0:T(8,128)(2,1)} %get-tuple-element.118), channel_id=1, source_target_pairs={{0,4},{4,0},{1,5},{5,1},{2,6},{6,2},{3,7},{7,3},{8,12},{12,8},{9,1... | collective-permute-start | bytes 12976136 | tf_op jit(solution)/shard_map/ppermute | solution.py:34
  320.8 148.4 %collective-permute-start.15 = (bf16[2,3,352,1024]{3,2,1,0:T(8,128)(2,1)}, bf16[2,3,352,1024]{3,2,1,0:T(8,128)(2,1)}, u32[]{:S(2)}, u32[]{:S(2)}) collective-permute-start(bf16[2,3,352,1024]{3,2,1,0:T(8,128)(2,1)} %get-tuple-element.135), channel_id=1, source_target_pairs={{0,4},{4,0},{1,5},{5,1},{2,6},{6,2},{3,7},{7,3},{8,12},{12,8},{9,1... | collective-permute-start | bytes 12976136 | tf_op jit(solution)/shard_map/ppermute | solution.py:34
  325.5 50.2 %slice-start.4 = ((s8[4325376]{0:T(1024)(128)(4,1)}), s8[4194304]{0:T(1024)(128)(4,1)S(1)}, s32[]{:S(2)}) async-start(s8[4325376]{0:T(1024)(128)(4,1)} %bitcast.112), calls=%async_computation.8 | async-start | bytes 8388608
  325.5 50.2 %slice-start.5 = ((s8[4325376]{0:T(1024)(128)(4,1)}), s8[131072]{0:T(1024)(128)(4,1)S(1)}, s32[]{:S(2)}) async-start(s8[4325376]{0:T(1024)(128)(4,1)} %bitcast.112), calls=%async_computation.9 | async-start | bytes 262144
  375.1 174.4 %collective-permute-start.17 = (bf16[2,3,352,1024]{3,2,1,0:T(8,128)(2,1)}, bf16[2,3,352,1024]{3,2,1,0:T(8,128)(2,1)}, u32[]{:S(2)}, u32[]{:S(2)}) collective-permute-start(bf16[2,3,352,1024]{3,2,1,0:T(8,128)(2,1)} %get-tuple-element.147), channel_id=1, source_target_pairs={{0,4},{4,0},{1,5},{5,1},{2,6},{6,2},{3,7},{7,3},{8,12},{12,8},{9,1... | collective-permute-start | bytes 12976136 | tf_op jit(solution)/shard_map/ppermute | solution.py:34
  380.9 113.0 %collective-permute-start.16 = (bf16[2,3,352,1024]{3,2,1,0:T(8,128)(2,1)}, bf16[2,3,352,1024]{3,2,1,0:T(8,128)(2,1)}, u32[]{:S(2)}, u32[]{:S(2)}) collective-permute-start(bf16[2,3,352,1024]{3,2,1,0:T(8,128)(2,1)} %bitcast.36), channel_id=1, source_target_pairs={{0,16},{8,24},{16,0},{24,8},{1,17},{9,25},{17,1},{25,9},{2,18},{10... | collective-permute-start | bytes 12976136 | tf_op jit(solution)/shard_map/ppermute | solution.py:39
  385.4 83.8 %slice-start = ((s8[4325376]{0:T(1024)(128)(4,1)}), s8[4194304]{0:T(1024)(128)(4,1)S(1)}, s32[]{:S(2)}) async-start(s8[4325376]{0:T(1024)(128)(4,1)} %bitcast.106), calls=%async_computation.4 | async-start | bytes 8388608
  385.4 83.8 %slice-start.1 = ((s8[4325376]{0:T(1024)(128)(4,1)}), s8[131072]{0:T(1024)(128)(4,1)S(1)}, s32[]{:S(2)}) async-start(s8[4325376]{0:T(1024)(128)(4,1)} %bitcast.106), calls=%async_computation.5 | async-start | bytes 262144
  474.4 105.6 %collective-permute-start.20 = (bf16[2,3,352,1024]{3,2,1,0:T(8,128)(2,1)}, bf16[2,3,352,1024]{3,2,1,0:T(8,128)(2,1)}, u32[]{:S(2)}, u32[]{:S(2)}) collective-permute-start(bf16[2,3,352,1024]{3,2,1,0:T(8,128)(2,1)} %bitcast.41), channel_id=1, source_target_pairs={{0,16},{8,24},{16,0},{24,8},{1,17},{9,25},{17,1},{25,9},{2,18},{10... | collective-permute-start | bytes 12976136 | tf_op jit(solution)/shard_map/ppermute | solution.py:39
  474.4 75.1 %slice-start.2 = ((s8[4325376]{0:T(1024)(128)(4,1)}), s8[4194304]{0:T(1024)(128)(4,1)S(1)}, s32[]{:S(2)}) async-start(s8[4325376]{0:T(1024)(128)(4,1)} %bitcast.109), calls=%async_computation.6 | async-start | bytes 8388608
  474.4 75.1 %slice-start.3 = ((s8[4325376]{0:T(1024)(128)(4,1)}), s8[131072]{0:T(1024)(128)(4,1)S(1)}, s32[]{:S(2)}) async-start(s8[4325376]{0:T(1024)(128)(4,1)} %bitcast.109), calls=%async_computation.7 | async-start | bytes 262144
  568.3 22.4 %collective-permute-start.19 = (bf16[3,2048,256]{2,1,0:T(8,128)(2,1)}, bf16[3,2048,256]{2,1,0:T(8,128)(2,1)}, u32[]{:S(2)}, u32[]{:S(2)}) collective-permute-start(bf16[3,2048,256]{2,1,0:T(8,128)(2,1)} %get-tuple-element.151), channel_id=1, source_target_pairs={{0,8},{8,0},{16,24},{24,16},{1,9},{9,1},{17,25},{25,17},{2,10},{10... | collective-permute-start | bytes 9437192 | tf_op jit(solution)/shard_map/ppermute | solution.py:44
  568.3 18.4 %collective-permute-start.23 = (bf16[256,2048]{1,0:T(8,128)(2,1)}, bf16[256,2048]{1,0:T(8,128)(2,1)}, u32[]{:S(2)}, u32[]{:S(2)}) collective-permute-start(bf16[256,2048]{1,0:T(8,128)(2,1)} %get-tuple-element.170), channel_id=1, source_target_pairs={{0,8},{8,0},{16,24},{24,16},{1,9},{9,1},{17,25},{25,17},{2,10},{10... | collective-permute-start | bytes 3145736 | tf_op jit(solution)/shard_map/ppermute | solution.py:44
  569.0 105.9 %collective-permute-start.31 = (bf16[2,3,352,1024]{3,2,1,0:T(8,128)(2,1)}, bf16[2,3,352,1024]{3,2,1,0:T(8,128)(2,1)}, u32[]{:S(2)}, u32[]{:S(2)}) collective-permute-start(bf16[2,3,352,1024]{3,2,1,0:T(8,128)(2,1)} %bitcast.105), channel_id=1, source_target_pairs={{0,16},{8,24},{16,0},{24,8},{1,17},{9,25},{17,1},{25,9},{2,18},{10... | collective-permute-start | bytes 12976136 | tf_op jit(solution)/shard_map/ppermute | solution.py:39
  578.9 88.5 %collective-permute-start.25 = (bf16[2,3,352,1024]{3,2,1,0:T(8,128)(2,1)}, bf16[2,3,352,1024]{3,2,1,0:T(8,128)(2,1)}, u32[]{:S(2)}, u32[]{:S(2)}) collective-permute-start(bf16[2,3,352,1024]{3,2,1,0:T(8,128)(2,1)} %bitcast.46.source), channel_id=1, source_target_pairs={{0,8},{8,0},{16,24},{24,16},{1,9},{9,1},{17,25},{25,17},{2,10},{10... | collective-permute-start | bytes 12976136 | tf_op jit(solution)/shard_map/ppermute | solution.py:44
  579.9 21.7 %collective-permute-start.18 = (bf16[640,2048]{1,0:T(8,128)(2,1)S(1)}, bf16[640,2048]{1,0:T(8,128)(2,1)}, u32[]{:S(2)}, u32[]{:S(2)}) collective-permute-start(bf16[640,2048]{1,0:T(8,128)(2,1)S(1)} %sums.11), channel_id=1, source_target_pairs={{0,8},{8,0},{16,24},{24,16},{1,9},{9,1},{17,25},{25,17},{2,10},{10... | collective-permute-start | bytes 7864328 | tf_op jit(solution)/shard_map/ppermute | solution.py:44
  586.7 62.9 %collective-permute-start.26 = (bf16[2,3,352,1024]{3,2,1,0:T(8,128)(2,1)}, bf16[2,3,352,1024]{3,2,1,0:T(8,128)(2,1)}, u32[]{:S(2)}, u32[]{:S(2)}) collective-permute-start(bf16[2,3,352,1024]{3,2,1,0:T(8,128)(2,1)} %bitcast.49.mine), channel_id=1, source_target_pairs={{0,8},{8,0},{16,24},{24,16},{1,9},{9,1},{17,25},{25,17},{2,10},{10... | collective-permute-start | bytes 12976136 | tf_op jit(solution)/shard_map/ppermute | solution.py:44
  594.3 5.6 collective-permute-start.27
  599.9 37.6 %collective-permute-start.21 = (bf16[3,1024,256]{2,1,0:T(8,128)(2,1)}, bf16[3,1024,256]{2,1,0:T(8,128)(2,1)}, u32[]{:S(2)}, u32[]{:S(2)}) collective-permute-start(bf16[3,1024,256]{2,1,0:T(8,128)(2,1)} %add_convert_fusion.2), channel_id=1, source_target_pairs={{0,4},{4,0},{1,5},{5,1},{2,6},{6,2},{3,7},{7,3},{8,12},{12,8},{9,1... | collective-permute-start | bytes 4718600 | tf_op jit(solution)/shard_map/ppermute | solution.py:34
  601.6 12.5 %collective-permute-start.28 = (f32[11,2048]{1,0:T(8,128)S(1)}, f32[11,2048]{1,0:T(8,128)S(1)}, u32[]{:S(2)}, u32[]{:S(2)}) collective-permute-start(f32[11,2048]{1,0:T(8,128)S(1)} %fusion.55), channel_id=1, source_target_pairs={{0,2},{1,3},{2,0},{3,1},{4,6},{5,7},{6,4},{7,5},{8,10},{9,11},{10,... | collective-permute-start | bytes 270344 | tf_op jit(solution)/shard_map/ppermute | solution.py:418
  614.2 3.3 collective-permute-start.29
  614.3 24.7 %copy-start.9 = (bf16[3,1024,256]{2,1,0:T(8,128)(2,1)S(1)}, bf16[3,1024,256]{2,1,0:T(8,128)(2,1)}, u32[]{:S(2)}) copy-start(bf16[3,1024,256]{2,1,0:T(8,128)(2,1)} %copy-done.8) | copy-start | bytes 4718596
  617.5 30.2 %collective-permute-start.24 = (bf16[256,1024]{1,0:T(8,128)(2,1)S(1)}, bf16[256,1024]{1,0:T(8,128)(2,1)S(1)}, u32[]{:S(2)}, u32[]{:S(2)}) collective-permute-start(bf16[256,1024]{1,0:T(8,128)(2,1)S(1)} %copy-done.32), channel_id=1, source_target_pairs={{0,4},{4,0},{1,5},{5,1},{2,6},{6,2},{3,7},{7,3},{8,12},{12,8},{9,1... | collective-permute-start | bytes 1572872 | tf_op jit(solution)/shard_map/ppermute | solution.py:34
  618.1 30.1 %copy-start.14 = (bf16[256,1024]{1,0:T(8,128)(2,1)S(1)}, bf16[256,1024]{1,0:T(8,128)(2,1)}, u32[]{:S(2)}) copy-start(bf16[256,1024]{1,0:T(8,128)(2,1)} %copy-done.13) | copy-start | bytes 1572868
  637.5 12.0 %collective-permute-start.30 = (f32[12,1024]{1,0:T(8,128)S(1)}, f32[12,1024]{1,0:T(8,128)S(1)}, u32[]{:S(2)}, u32[]{:S(2)}) collective-permute-start(f32[12,1024]{1,0:T(8,128)S(1)} %slice.157), channel_id=1, source_target_pairs={{0,4},{4,0},{1,5},{5,1},{2,6},{6,2},{3,7},{7,3},{8,12},{12,8},{9,1... | collective-permute-start | bytes 147464 | tf_op jit(solution)/shard_map/ppermute | solution.py:34
  647.7 51.6 %collective-permute-start.22 = (bf16[3,1024,256]{2,1,0:T(8,128)(2,1)S(1)}, bf16[3,1024,256]{2,1,0:T(8,128)(2,1)}, u32[]{:S(2)}, u32[]{:S(2)}) collective-permute-start(bf16[3,1024,256]{2,1,0:T(8,128)(2,1)S(1)} %add_convert_fusion.1), channel_id=1, source_target_pairs={{0,16},{8,24},{16,0},{24,8},{1,17},{9,25},{17,1},{25,9},{2,18},{10... | collective-permute-start | bytes 4718600 | tf_op jit(solution)/shard_map/ppermute | solution.py:39
  681.0 42.1 %collective-permute-start.36 = (bf16[2,3,352,1024]{3,2,1,0:T(8,128)(2,1)}, bf16[2,3,352,1024]{3,2,1,0:T(8,128)(2,1)}, u32[]{:S(2)}, u32[]{:S(2)}) collective-permute-start(bf16[2,3,352,1024]{3,2,1,0:T(8,128)(2,1)} %bitcast.57.source), channel_id=1, source_target_pairs={{0,8},{8,0},{16,24},{24,16},{1,9},{9,1},{17,25},{25,17},{2,10},{10... | collective-permute-start | bytes 12976136 | tf_op jit(solution)/shard_map/ppermute | solution.py:44
  681.1 29.1 %collective-permute-start.34 = (bf16[256,1024]{1,0:T(8,128)(2,1)S(1)}, bf16[256,1024]{1,0:T(8,128)(2,1)S(1)}, u32[]{:S(2)}, u32[]{:S(2)}) collective-permute-start(bf16[256,1024]{1,0:T(8,128)(2,1)S(1)} %add_convert_fusion.6), channel_id=1, source_target_pairs={{0,16},{8,24},{16,0},{24,8},{1,17},{9,25},{17,1},{25,9},{2,18},{10... | collective-permute-start | bytes 1572872 | tf_op jit(solution)/shard_map/ppermute | solution.py:39
  701.1 14.9 %collective-permute-start.32 = (bf16[3,1024,256]{2,1,0:T(8,128)(2,1)S(1)}, bf16[3,1024,256]{2,1,0:T(8,128)(2,1)}, u32[]{:S(2)}, u32[]{:S(2)}) collective-permute-start(bf16[3,1024,256]{2,1,0:T(8,128)(2,1)S(1)} %add_convert_fusion), channel_id=1, source_target_pairs={{0,8},{8,0},{16,24},{24,16},{1,9},{9,1},{17,25},{25,17},{2,10},{10... | collective-permute-start | bytes 4718600 | tf_op jit(solution)/shard_map/ppermute | solution.py:44
  701.7 10.0 %collective-permute-start.33 = (f32[12,1024]{1,0:T(8,128)S(1)}, f32[12,1024]{1,0:T(8,128)S(1)}, u32[]{:S(2)}, u32[]{:S(2)}) collective-permute-start(f32[12,1024]{1,0:T(8,128)S(1)} %slice_add_fusion.1), channel_id=1, source_target_pairs={{0,16},{8,24},{16,0},{24,8},{1,17},{9,25},{17,1},{25,9},{2,18},{10... | collective-permute-start | bytes 147464 | tf_op jit(solution)/shard_map/ppermute | solution.py:39
  710.4 3.9 collective-permute-start.35
  (39 other events, 223.9 us)
Sparse Core Ops, SparseCore 0:
  21.6 55.0 all-gather.2
  78.3 71.7 all-gather.4
  614.2 49.5 reduce-scatter.1
